TPU v7x, 512 devices: a whole 4x8x8 slice. The times are simulated.
512 devices in a mesh: section: 4 (over x_hi, core), tensor: 8 (over z), dp: 16 (over y, x_lo).
Axes of the slice: x: 4 (x_hi: 2, x_lo: 2; x = x_hi * 2 + x_lo), y: 8, z: 8, core: 2. Of those that a mesh axis runs over, the one named last changes fastest.
Arguments:
- residual_in: bfloat16 [1, 256, 12288], P(None, ('section', 'tensor'), 'dp'), may hold values from -36 to 36
- up_first: bfloat16 [12288, 24576], P('dp', ('section', 'tensor')), may hold values from -0.0546875 to 0.0546875
- down_first: bfloat16 [24576, 12288], P(('section', 'tensor'), 'dp'), may hold values from -0.0390625 to 0.0390625
- gain_first: bfloat16 [12288], P('dp'), may hold values from 0.099609375 to 1.8984375
- up_second: bfloat16 [12288, 24576], P(('section', 'tensor'), 'dp'), may hold values from -0.0546875 to 0.0546875
- down_second: bfloat16 [24576, 12288], P('dp', ('section', 'tensor')), may hold values from -0.0390625 to 0.0390625
- gain_second: bfloat16 [12288], P(('section', 'tensor')), may hold values from 0.099609375 to 1.8984375
- cotangent: bfloat16 [1, 256, 12288], P(None, 'dp', ('section', 'tensor')), may hold values from -6 to 6
Outputs:
- residual_out: bfloat16 [1, 256, 12288], P(None, 'dp', ('section', 'tensor'))
- residual_grad: bfloat16 [1, 256, 12288], P(None, ('section', 'tensor'), 'dp')
All inputs are finite; a program needn't handle non-finite values.
Results may differ from a plain program's by a relative error of at most 0.033.
Values may be sent and summed in bfloat16 or wider, within the bound.
No kernel may reach another device: no remote copies, remote signals or barrier semaphores. Data moves between devices by JAX's collectives and lax.ppermute only.
A program may use at most 64 MiB of HBM per device.

v0:
```python
import jax
import jax.numpy as jnp
from jax import lax
from jax.sharding import PartitionSpec as P

D = 12288


EPS = 1e-05
GELU_C0 = 0.7978845608028654
GELU_C1 = 0.044715


def broadcast(block, axis, owner):
    block = jnp.where(lax.axis_index(axis) == owner, block, jnp.zeros_like(block))
    return lax.psum(block, axis)


def gelu_value(hidden):
    inner = jnp.tanh(GELU_C0 * (hidden + GELU_C1 * hidden * hidden * hidden))
    return 0.5 * hidden * (1.0 + inner)


def gelu_slope(hidden):
    inner = jnp.tanh(GELU_C0 * (hidden + GELU_C1 * hidden * hidden * hidden))
    return 0.5 * (1.0 + inner) + 0.5 * hidden * (1.0 - inner * inner) * GELU_C0 * (
        1.0 + 3.0 * GELU_C1 * hidden * hidden
    )


def row_moments(values):
    floats = values.astype(jnp.float32)
    return (jnp.sum(floats, axis=1), jnp.sum(floats * floats, axis=1))


def finish_stats(total, square):
    mean = (total / D)[:, None]
    return (mean, lax.rsqrt((square / D)[:, None] - mean * mean + EPS))


def contract_cols(left, right):
    return lax.dot_general(
        left, right, (((1,), (1,)), ((), ())), preferred_element_type=jnp.float32
    )


def grad_terms(d_norm, gain_floats, nhat):
    scaled = d_norm * gain_floats
    return (scaled, jnp.sum(scaled, axis=1), jnp.sum(scaled * nhat, axis=1))


def per_device(
    residual_in, up_first, down_first, gain_first, up_second, down_second, gain_second, cotangent
):
    blocks = lax.axis_size(("section", "tensor"))
    groups = lax.axis_size("dp")
    factor = blocks // groups
    own_block = lax.axis_index(("section", "tensor"))
    own_group = lax.axis_index("dp")
    tokens = residual_in.shape[1] * blocks
    block_rows = tokens // blocks
    group_rows = tokens // groups
    narrow = up_second.shape[0]
    gain_a = gain_first.astype(jnp.float32)
    gain_b = gain_second.astype(jnp.float32)
    in_rows = residual_in[0]
    rows_all = lax.all_gather(in_rows, ("section", "tensor"), axis=0, tiled=True)
    row_sum, square = row_moments(rows_all)
    row_sum, square = lax.psum((row_sum, square), "dp")
    mean_a, rstd_a = finish_stats(row_sum, square)
    rows_float = rows_all.astype(jnp.float32)
    normed_a = ((rows_float - mean_a) * rstd_a * gain_a).astype(jnp.bfloat16)
    hidden_a = lax.psum_scatter(
        jnp.dot(normed_a, up_first, preferred_element_type=jnp.float32).astype(jnp.bfloat16),
        "dp",
        scatter_dimension=0,
        tiled=True,
    ).astype(jnp.float32)
    active_a = gelu_value(hidden_a).astype(jnp.bfloat16)
    partial_a = jnp.dot(
        lax.all_gather(active_a, "dp", axis=0, tiled=True),
        down_first,
        preferred_element_type=jnp.float32,
    )
    mixed_all = lax.psum(partial_a.astype(jnp.bfloat16), ("section", "tensor")).astype(jnp.float32)
    middle_all = (rows_float + mixed_all).astype(jnp.bfloat16)
    portion_b = lax.dynamic_slice_in_dim(middle_all, own_block % factor * narrow, narrow, 1)
    middle_b = broadcast(portion_b, "dp", own_block // factor)
    row_sum, square = row_moments(middle_b)
    row_sum, square = lax.psum((row_sum, square), ("section", "tensor"))
    mean_b, rstd_b = finish_stats(row_sum, square)
    middle_float = middle_b.astype(jnp.float32)
    normed_b = ((middle_float - mean_b) * rstd_b * gain_b).astype(jnp.bfloat16)
    hidden_b = lax.psum_scatter(
        jnp.dot(normed_b, up_second, preferred_element_type=jnp.float32).astype(jnp.bfloat16),
        ("section", "tensor"),
        scatter_dimension=0,
        tiled=True,
    ).astype(jnp.float32)
    active_b = gelu_value(hidden_b).astype(jnp.bfloat16)
    partial_b = jnp.dot(
        lax.all_gather(active_b, ("section", "tensor"), axis=0, tiled=True),
        down_second,
        preferred_element_type=jnp.float32,
    )
    mixed_b = lax.psum_scatter(
        partial_b.astype(jnp.bfloat16), "dp", scatter_dimension=0, tiled=True
    ).astype(jnp.float32)
    lower_b = own_group * group_rows
    own_middle = lax.dynamic_slice_in_dim(middle_float, lower_b, group_rows, 0)
    outputs = [(own_middle + mixed_b).astype(jnp.bfloat16)]
    grad_rows = cotangent[0]
    grad_all = lax.all_gather(grad_rows, "dp", axis=0, tiled=True)
    d_act_b = lax.psum_scatter(
        contract_cols(grad_all, down_second).astype(jnp.bfloat16),
        ("section", "tensor"),
        scatter_dimension=0,
        tiled=True,
    ).astype(jnp.float32)
    d_hid_b = (d_act_b * gelu_slope(hidden_b)).astype(jnp.bfloat16)
    partial_db = contract_cols(
        lax.all_gather(d_hid_b, ("section", "tensor"), axis=0, tiled=True), up_second
    )
    nhat_b = (middle_float - mean_b) * rstd_b
    d_norm_b = lax.psum(partial_db.astype(jnp.bfloat16), "dp").astype(jnp.float32)
    scaled, sum_one, sum_two = grad_terms(d_norm_b, gain_b, nhat_b)
    sum_one, sum_two = lax.psum((sum_one, sum_two), ("section", "tensor"))
    back_float = grad_all.astype(jnp.float32) + rstd_b * (
        scaled - (sum_one / D)[:, None] - nhat_b * (sum_two / D)[:, None]
    )
    back_all = back_float.astype(jnp.bfloat16)
    slices = []
    for member in range(factor):
        slices.append(broadcast(back_all, ("section", "tensor"), own_group * factor + member))
    grad_middle = jnp.concatenate(slices, axis=1)
    d_act_a = lax.psum_scatter(
        contract_cols(grad_middle, down_first).astype(jnp.bfloat16),
        "dp",
        scatter_dimension=0,
        tiled=True,
    ).astype(jnp.float32)
    d_hid_a = (d_act_a * gelu_slope(hidden_a)).astype(jnp.bfloat16)
    partial_da = contract_cols(lax.all_gather(d_hid_a, "dp", axis=0, tiled=True), up_first)
    d_norm_a = lax.psum_scatter(
        partial_da.astype(jnp.bfloat16), ("section", "tensor"), scatter_dimension=0, tiled=True
    ).astype(jnp.float32)
    lower_a = own_block * block_rows
    mean_rows = lax.dynamic_slice_in_dim(mean_a, lower_a, block_rows, 0)
    rstd_rows_a = lax.dynamic_slice_in_dim(rstd_a, lower_a, block_rows, 0)
    nhat_a = (in_rows.astype(jnp.float32) - mean_rows) * rstd_rows_a
    scaled_a, sum_one_a, sum_two_a = grad_terms(d_norm_a, gain_a, nhat_a)
    sum_one_a, sum_two_a = lax.psum((sum_one_a, sum_two_a), "dp")
    upstream_rows = lax.dynamic_slice_in_dim(grad_middle, lower_a, block_rows, 0).astype(
        jnp.float32
    )
    result = upstream_rows + rstd_rows_a * (
        scaled_a - (sum_one_a / D)[:, None] - nhat_a * (sum_two_a / D)[:, None]
    )
    gradients = [result.astype(jnp.bfloat16)]
    return (jnp.stack(outputs), jnp.stack(gradients))


def solution(mesh):
    return jax.shard_map(
        per_device,
        mesh=mesh,
        in_specs=(
            P(None, ("section", "tensor"), "dp"),
            P("dp", ("section", "tensor")),
            P(("section", "tensor"), "dp"),
            P("dp"),
            P(("section", "tensor"), "dp"),
            P("dp", ("section", "tensor")),
            P(("section", "tensor")),
            P(None, "dp", ("section", "tensor")),
        ),
        out_specs=(P(None, "dp", ("section", "tensor")), P(None, ("section", "tensor"), "dp")),
        check_vma=False,
    )
```

profile of v0, /device:TPU:4, one launch (start us, length us, event | category | flops | bytes accessed | tf_op | source)
XLA Modules:
  0.0 1725.8 jit_solution(2560249445602651751)
XLA Ops:
  7.2 0.0 reduce-scatter.7.cloned.1.call-start
  7.2 74.5 %all-gather = bf16[1,256,768]{2,1,0:T(8,128)(2,1)S(1)} all-gather(bf16[1,8,768]{2,1,0:T(8,128)(2,1)} %param.8), channel_id=2, replica_groups=mesh['section'=4,'tensor'=8,'dp'=16] {'section','tensor'}, dimensions={1}, use_global_device_ids=true | all-gather | bytes 405504 | tf_op jit(solution)/shard_map/all_gather | solution.py:67
  81.7 0.1 convert_reduce_fusion
  81.8 0.2 multiply_reduce_fusion
  82.0 35.5 %all-reduce.3 = (f32[256]{0:T(256)S(1)}, f32[256]{0:T(256)S(1)}) all-reduce(f32[256]{0:T(256)S(1)} %multiply_reduce_fusion, f32[256]{0:T(256)S(1)} %convert_reduce_fusion), channel_id=1, replica_groups=mesh['section'=4,'tensor'=8,'dp'=16] {'dp'}, use_global_device_ids=true, to_apply=%region_3.0 | all-reduce | flops 512 | bytes 4096 | tf_op jit(solution)/shard_map/psum | solution.py:69
  117.5 2.6 convolution_convert_fusion.5
  120.2 0.0 reduce-scatter.7.cloned.1.call-update
  120.2 0.0 all-reduce.10.cloned.1.call-start
  120.2 65.5 %reduce-scatter.7.cloned.1.call-done = bf16[16,768]{1,0:T(8,128)(2,1)} async-done(((bf16[256,768]{1,0:T(8,128)(2,1)}), bf16[16,768]{1,0:T(8,128)(2,1)}) %reduce-scatter.7.cloned.1.call-update) | async-done | bytes 24592 | tf_op jit(solution)/shard_map/reduce_scatter | solution.py:73
  185.7 0.8 fusion.20
  186.5 32.5 %all_gather.19 = bf16[256,768]{1,0:T(8,128)(2,1)S(1)} all-gather(bf16[16,768]{1,0:T(8,128)(2,1)S(1)} %fusion.20), channel_id=1, replica_groups=mesh['section'=4,'tensor'=8,'dp'=16] {'dp'}, dimensions={0}, use_global_device_ids=true | all-gather | bytes 417792 | tf_op jit(solution)/shard_map/all_gather | solution.py:81
  219.0 1.3 convolution_convert_fusion.4
  220.3 0.0 all-reduce.10.cloned.1.call-update
  220.3 0.0 all-reduce.12.cloned.1.call-start
  220.4 31.9 %all-gather.1 = bf16[1,256,384]{2,1,0:T(8,128)(2,1)S(1)} all-gather(bf16[1,16,384]{2,1,0:T(8,128)(2,1)S(1)} %copy-done.7), channel_id=3, replica_groups=mesh['section'=4,'tensor'=8,'dp'=16] {'dp'}, dimensions={1}, use_global_device_ids=true | all-gather | bytes 208896 | tf_op jit(solution)/shard_map/all_gather | solution.py:113
  252.3 0.9 convert_bitcast_fusion
  253.2 231.5 %all-reduce.10.cloned.1.call-done = bf16[256,768]{1,0:T(8,128)(2,1)} async-done(((bf16[256,768]{1,0:T(8,128)(2,1)}), bf16[256,768]{1,0:T(8,128)(2,1)}) %all-reduce.10.cloned.1.call-update) | async-done | bytes 393232 | tf_op jit(solution)/shard_map/psum | solution.py:85
  484.8 1.8 fusion.5
  486.5 0.0 all-reduce.12.cloned.1.call-update
  486.6 0.0 reduce-scatter.13.cloned.1.call-start
  486.6 2.8 convolution_convert_fusion
  489.4 0.0 reduce-scatter.13.cloned.1.call-update
  489.4 0.0 reduce-scatter.9.cloned.1.call-start
  489.5 135.2 %all-reduce.12.cloned.1.call-done = bf16[256,384]{1,0:T(8,128)(2,1)} async-done(((bf16[256,384]{1,0:T(8,128)(2,1)}), bf16[256,384]{1,0:T(8,128)(2,1)}) %all-reduce.12.cloned.1.call-update) | async-done | bytes 196624 | tf_op jit(solution)/shard_map/psum | solution.py:16
  624.7 1.1 convert_reduce_fusion.1
  625.7 66.7 %all-reduce.1 = (f32[256]{0:T(256)S(1)}, f32[256]{0:T(256)S(1)}) all-reduce(f32[256]{0:T(256)S(1)} %get-tuple-element.5, f32[256]{0:T(256)S(1)} %get-tuple-element.4), channel_id=1, replica_groups=mesh['section'=4,'tensor'=8,'dp'=16] {'section','tensor'}, use_global_device_ids=true, to_apply=%region_10.11 | all-reduce | flops 512 | bytes 4096 | tf_op jit(solution)/shard_map/psum | solution.py:90
  692.4 2.5 convolution_convert_fusion.1
  694.9 0.0 reduce-scatter.9.cloned.1.call-update
  694.9 0.0 all-reduce.14.cloned.1.call-start
  694.9 56.1 %reduce-scatter.13.cloned.1.call-done = bf16[8,1536]{1,0:T(8,128)(2,1)} async-done(((bf16[256,1536]{1,0:T(8,128)(2,1)}), bf16[8,1536]{1,0:T(8,128)(2,1)}) %reduce-scatter.13.cloned.1.call-update) | async-done | bytes 24592 | tf_op jit(solution)/shard_map/reduce_scatter | solution.py:114
  751.1 125.5 %reduce-scatter.9.cloned.1.call-done = bf16[8,1536]{1,0:T(8,128)(2,1)} async-done(((bf16[256,1536]{1,0:T(8,128)(2,1)}), bf16[8,1536]{1,0:T(8,128)(2,1)}) %reduce-scatter.9.cloned.1.call-update) | async-done | bytes 24592 | tf_op jit(solution)/shard_map/reduce_scatter | solution.py:94
  876.6 1.4 fusion.19
  878.0 68.7 %all_gather.22 = bf16[256,1536]{1,0:T(8,128)(2,1)S(1)} all-gather(bf16[8,1536]{1,0:T(8,128)(2,1)S(1)} %get-tuple-element.21), channel_id=1, replica_groups=mesh['section'=4,'tensor'=8,'dp'=16] {'section','tensor'}, dimensions={0}, use_global_device_ids=true | all-gather | bytes 811008 | tf_op jit(solution)/shard_map/all_gather | solution.py:122
  946.7 1.3 convolution_convert_fusion.6
  948.0 0.0 all-reduce.14.cloned.1.call-update
  948.0 0.0 all-reduce.16.cloned.1.call-start
  948.1 136.0 %all-reduce.14.cloned.1.call-done = bf16[256,384]{1,0:T(8,128)(2,1)} async-done(((bf16[256,384]{1,0:T(8,128)(2,1)}), bf16[256,384]{1,0:T(8,128)(2,1)}) %all-reduce.14.cloned.1.call-update) | async-done | bytes 196624 | tf_op jit(solution)/shard_map/psum | solution.py:125
  1084.0 1.2 fusion.1
  1085.2 66.7 %all-reduce = (f32[256]{0:T(256)S(1)}, f32[256]{0:T(256)S(1)}) all-reduce(f32[256]{0:T(256)S(1)} %get-tuple-element.3, f32[256]{0:T(256)S(1)} %get-tuple-element.2), channel_id=1, replica_groups=mesh['section'=4,'tensor'=8,'dp'=16] {'section','tensor'}, use_global_device_ids=true, to_apply=%region_18.19 | all-reduce | flops 512 | bytes 4096 | tf_op jit(solution)/shard_map/psum | solution.py:127
  1151.9 1.9 broadcast_select_fusion
  1153.8 0.7 broadcast_select_fusion.1
  1154.5 0.0 all-reduce.16.cloned.1.call-update
  1154.5 0.0 reduce-scatter.15.cloned.1.call-start
  1154.6 256.8 %all-reduce.16.cloned.1.call-done = (bf16[256,384]{1,0:T(8,128)(2,1)}, bf16[256,384]{1,0:T(8,128)(2,1)}) async-done(((bf16[256,384]{1,0:T(8,128)(2,1)}, bf16[256,384]{1,0:T(8,128)(2,1)}), (bf16[256,384]{1,0:T(8,128)(2,1)}, bf16[256,384]{1,0:T(8,128)(2,1)})) %all-reduce.16.cloned.1.call-update) | async-done | bytes 393232 | tf_op jit(solution)/shard_map/psum | solution.py:16
  1411.3 0.9 constant_dynamic-update-slice_fusion.1
  1412.3 1.0 constant_dynamic-update-slice_fusion
  1413.3 0.7 copy-done.5
  1414.0 1.3 convolution_convert_fusion.3
  1415.3 0.0 reduce-scatter.11.cloned.1.call-start
  1415.3 70.5 %all_gather.20 = bf16[256,1536]{1,0:T(8,128)(2,1)S(1)} all-gather(bf16[8,1536]{1,0:T(8,128)(2,1)} %get-tuple-element.22), channel_id=1, replica_groups=mesh['section'=4,'tensor'=8,'dp'=16] {'section','tensor'}, dimensions={0}, use_global_device_ids=true | all-gather | bytes 811008 | tf_op jit(solution)/shard_map/all_gather | solution.py:102
  1485.8 1.3 convolution_convert_fusion.7
  1487.1 0.0 reduce-scatter.17.cloned.1.call-start
  1487.2 0.0 reduce-scatter.15.cloned.1.call-done
  1487.2 0.8 fusion.25
  1488.0 36.3 %all_gather.23 = bf16[256,768]{1,0:T(8,128)(2,1)S(1)} all-gather(bf16[16,768]{1,0:T(8,128)(2,1)S(1)} %fusion.25), channel_id=1, replica_groups=mesh['section'=4,'tensor'=8,'dp'=16] {'dp'}, dimensions={0}, use_global_device_ids=true | all-gather | bytes 417792 | tf_op jit(solution)/shard_map/all_gather | solution.py:143
  1524.3 1.3 convolution_convert_fusion.2
  1525.6 0.1 dynamic-slice.6
  1525.7 0.1 dynamic-slice.7
  1525.7 33.4 %reduce-scatter.11.cloned.1.call-done = bf16[16,384]{1,0:T(8,128)(2,1)} async-done(((bf16[256,384]{1,0:T(8,128)(2,1)}), bf16[16,384]{1,0:T(8,128)(2,1)}) %reduce-scatter.11.cloned.1.call-update) | async-done | bytes 12304 | tf_op jit(solution)/shard_map/reduce_scatter | solution.py:106
  1559.1 1.4 fusion.41
  1560.5 122.0 %reduce-scatter.17.cloned.1.call-done = bf16[8,768]{1,0:T(8,128)(2,1)} async-done(((bf16[256,768]{1,0:T(8,128)(2,1)}), bf16[8,768]{1,0:T(8,128)(2,1)}) %reduce-scatter.17.cloned.1.call-update) | async-done | bytes 12304 | tf_op jit(solution)/shard_map/reduce_scatter | solution.py:144
  1682.4 0.9 fusion.40
  1683.4 34.1 %all-reduce.2 = (f32[8]{0:T(128)S(1)}, f32[8]{0:T(128)S(1)}) all-reduce(f32[8]{0:T(128)S(1)} %get-tuple-element.7, f32[8]{0:T(128)S(1)} %get-tuple-element.6), channel_id=1, replica_groups=mesh['section'=4,'tensor'=8,'dp'=16] {'dp'}, use_global_device_ids=true, to_apply=%region_26.27 | all-reduce | flops 16 | bytes 128 | tf_op jit(solution)/shard_map/psum | solution.py:152
  1717.5 1.4 fusion.42
  (29 shorter events, 0.1 us)
Async XLA Ops:
  7.2 685.2 %copy-start = (bf16[384,1536]{1,0:T(8,128)(2,1)S(1)}, bf16[384,1536]{1,0:T(8,128)(2,1)}, u32[]{:S(2)}) copy-start(bf16[384,1536]{1,0:T(8,128)(2,1)} %param.12) | copy-start | bytes 3538948
  7.2 74.8 %copy-start.8 = (bf16[768]{0:T(1024)(128)(2,1)S(1)}, bf16[768]{0:T(1024)(128)(2,1)}, u32[]{:S(2)}) copy-start(bf16[768]{0:T(1024)(128)(2,1)} %param.11) | copy-start | bytes 4612
  7.2 178.6 %reduce-scatter.7.cloned.1.call-start = ((), (), s32[]{:S(2)}) async-start(), calls=%async_computation.6 | async-start | bytes 417792 | tf_op jit(solution)/shard_map/reduce_scatter | solution.py:73
  117.5 101.5 %copy-start.1 = (bf16[768,768]{1,0:T(8,128)(2,1)S(1)}, bf16[768,768]{1,0:T(8,128)(2,1)}, u32[]{:S(2)}) copy-start(bf16[768,768]{1,0:T(8,128)(2,1)} %param.10) | copy-start | bytes 3538948
  120.2 364.6 %all-reduce.10.cloned.1.call-start = ((), (), s32[]{:S(2)}) async-start(), calls=%async_computation.7 | async-start | bytes 786432 | tf_op jit(solution)/shard_map/psum | solution.py:85
  219.0 1.4 copy-start.7
  220.3 404.4 %all-reduce.12.cloned.1.call-start = ((), (), s32[]{:S(2)}) async-start(), calls=%async_computation.8 | async-start | bytes 393216 | tf_op jit(solution)/shard_map/psum | solution.py:16
  486.6 2.9 copy-start.9
  486.6 264.5 %reduce-scatter.13.cloned.1.call-start = ((), (), s32[]{:S(2)}) async-start(), calls=%async_computation.11 | async-start | bytes 811008 | tf_op jit(solution)/shard_map/reduce_scatter | solution.py:114
  489.4 387.2 %reduce-scatter.9.cloned.1.call-start = ((), (), s32[]{:S(2)}) async-start(), calls=%async_computation.9 | async-start | bytes 811008 | tf_op jit(solution)/shard_map/reduce_scatter | solution.py:94
  694.9 389.1 %all-reduce.14.cloned.1.call-start = ((), (), s32[]{:S(2)}) async-start(), calls=%async_computation.12 | async-start | bytes 393216 | tf_op jit(solution)/shard_map/psum | solution.py:125
  946.7 137.3 %copy-start.2 = (bf16[256,384]{1,0:T(8,128)(2,1)S(1)}, bf16[256,384]{1,0:T(8,128)(2,1)}, u32[]{:S(2)}) copy-start(bf16[256,384]{1,0:T(8,128)(2,1)} %all-reduce.12.cloned.1.call-done) | copy-start | bytes 589828
  948.0 463.3 %all-reduce.16.cloned.1.call-start = ((), (), s32[]{:S(2)}) async-start(), calls=%async_computation.15 | async-start | bytes 786432 | tf_op jit(solution)/shard_map/psum | solution.py:16
  1154.5 332.7 %reduce-scatter.15.cloned.1.call-start = ((), (), s32[]{:S(2)}) async-start(), calls=%async_computation.13 | async-start | bytes 417792 | tf_op jit(solution)/shard_map/reduce_scatter | solution.py:136
  1413.3 0.7 copy-start.5
  1414.0 71.8 %copy-start.3 = (bf16[1536,384]{1,0:T(8,128)(2,1)S(1)}, bf16[1536,384]{1,0:T(8,128)(2,1)}, u32[]{:S(2)}) copy-start(bf16[1536,384]{1,0:T(8,128)(2,1)} %param.13) | copy-start | bytes 3538948
  1415.3 143.8 %reduce-scatter.11.cloned.1.call-start = ((), (), s32[]{:S(2)}) async-start(), calls=%async_computation.10 | async-start | bytes 208896 | tf_op jit(solution)/shard_map/reduce_scatter | solution.py:106
  1485.8 38.5 %copy-start.4 = (bf16[768,768]{1,0:T(8,128)(2,1)S(1)}, bf16[768,768]{1,0:T(8,128)(2,1)}, u32[]{:S(2)}) copy-start(bf16[768,768]{1,0:T(8,128)(2,1)} %param.9) | copy-start | bytes 3538948
  1487.1 195.3 %reduce-scatter.17.cloned.1.call-start = ((), (), s32[]{:S(2)}) async-start(), calls=%async_computation.14 | async-start | bytes 405504 | tf_op jit(solution)/shard_map/reduce_scatter | solution.py:144
  1524.3 158.2 %copy-start.6 = (bf16[1,8,768]{2,1,0:T(8,128)(2,1)S(1)}, bf16[1,8,768]{2,1,0:T(8,128)(2,1)}, u32[]{:S(2)}) copy-start(bf16[1,8,768]{2,1,0:T(8,128)(2,1)} %param.8) | copy-start | bytes 36868
Sparse Core Ops, SparseCore 0:
  120.3 65.3 reduce-scatter.6
  220.4 264.3 all-reduce.9
  487.7 136.9 all-reduce.11
  629.8 121.2 reduce-scatter.12
  755.5 121.0 reduce-scatter.8
  948.1 135.8 all-reduce.13
  1154.6 256.6 all-reduce.15
  1415.4 70.0 reduce-scatter.14
  1488.3 70.7 reduce-scatter.10
  1564.2 118.2 reduce-scatter.16
where the time goes:
time: 1730 us
  waiting for transfers between devices  1160 us (67%)
  blocking collectives  517 us (30%)
    psum x2, waiting for transfers between devices, broadcast(): return lax.psum(block, axis)  392 us
    psum x1, waiting for transfers between devices, per_device(): lax.psum(partial_a.astype(jnp.bfloat16), ('section', 'tensor'))  232 us
    psum x1, waiting for transfers between devices, per_device(): lax.psum(partial_db.astype(jnp.bfloat16), 'dp').astype(jnp.float32)  136 us
    reduce_scatter x1, waiting for transfers between devices, per_device(): lax.psum_scatter(jnp.dot(normed_b, up_second, preferred_element_type=jnp....  126 us
    reduce_scatter x1, waiting for transfers between devices, per_device(): lax.psum_scatter(partial_da.astype(jnp.bfloat16), ('section', 'tensor'),...  122 us
    all_gather x1, blocking collectives, per_device(): lax.all_gather(in_rows, ('section', 'tensor'), axis=0, tiled=True)  74.5 us
    all_gather x1, blocking collectives, per_device(): lax.all_gather(active_b, ('section', 'tensor'), axis=0, tiled=True)  70.5 us
    all_gather x1, blocking collectives, per_device(): lax.all_gather(d_hid_b, ('section', 'tensor'), axis=0, tiled=True)  68.7 us
  transfers between devices with their start and end apart: 10, of which 9 were waited for; matrix products, arithmetic and copies ran while one was open for 1% of the time, Pallas kernels for 0%

commit v1 on v0

v1 whole, which is shorter than its diff:
```python
import jax
import jax.numpy as jnp
from jax import lax
from jax.sharding import Mesh, PartitionSpec as P

D = 12288
EPS = 1e-05
GELU_C0 = 0.7978845608028654
GELU_C1 = 0.044715
BF = jnp.bfloat16
F32 = jnp.float32
NAMES = ("xh", "core", "z", "y", "xl")
SIZES = (2, 2, 8, 8, 2)
ROW = ("xh", "z")
DP = ("y", "xl")
LANES = 128


def gelu_value(hidden):
    inner = jnp.tanh(GELU_C0 * (hidden + GELU_C1 * hidden * hidden * hidden))
    return 0.5 * hidden * (1.0 + inner)


def gelu_slope(hidden):
    inner = jnp.tanh(GELU_C0 * (hidden + GELU_C1 * hidden * hidden * hidden))
    return 0.5 * (1.0 + inner) + 0.5 * hidden * (1.0 - inner * inner) * GELU_C0 * (
        1.0 + 3.0 * GELU_C1 * hidden * hidden
    )


def dot(left, right):
    return jnp.dot(left, right, preferred_element_type=F32)


def contract_cols(left, right):
    return lax.dot_general(left, right, (((1,), (1,)), ((), ())), preferred_element_type=F32)


def split3(value):
    high = lax.reduce_precision(value, 8, 7)
    rest = value - high
    mid = lax.reduce_precision(rest, 8, 7)
    return high.astype(BF), mid.astype(BF), (rest - mid).astype(BF)


def pack_columns(columns):
    rows = columns[0].shape[0]
    parts = [piece[:, None] for column in columns for piece in split3(column)]
    parts.append(jnp.zeros((rows, LANES - len(parts)), BF))
    return jnp.concatenate(parts, axis=1)


def read_columns(block, count):
    floats = block.astype(F32)
    return [
        floats[:, 3 * k] + floats[:, 3 * k + 1] + floats[:, 3 * k + 2] for k in range(count)
    ]


def exchange(blocks, axis):
    return lax.all_to_all(blocks, axis, 0, 0)


def send_all(rows, axis, count):
    return exchange(jnp.broadcast_to(rows[None], (count,) + rows.shape), axis)


def gather_row(rows):
    part = send_all(rows, ROW, 16).reshape(16 * rows.shape[0], rows.shape[1])
    return lax.all_gather(part, "core", axis=0, tiled=True)


def pair_sum(values, width):
    half = exchange(values.reshape(2, 128, values.shape[1]), "core").astype(F32)
    total = half[0] + half[1]
    return total


def scatter_row(values, columns):
    width = values.shape[1]
    packed = jnp.concatenate([values, pack_columns(columns)], axis=1)
    total = pair_sum(packed, width)
    sums = read_columns(total[:, width:], len(columns))
    packed = jnp.concatenate([total[:, :width].astype(BF), pack_columns(sums)], axis=1)
    got = jnp.sum(exchange(packed.reshape(16, 8, width + LANES), ROW).astype(F32), axis=0)
    return got[:, :width], read_columns(got[:, width:], len(columns))


def swap_order(rows):
    blocks = rows.reshape(2, 2, 64, rows.shape[1])
    return jnp.transpose(blocks, (1, 0, 2, 3)).reshape(256, rows.shape[1])


def crossing(which):
    pairs = []
    for st in range(32):
        for group in range(16):
            target = (2 * group + (st + which) % 2) * 16 + st // 2
            pairs.append((st * 16 + group, target))
    return pairs


def cross(first, second):
    odd = lax.axis_index("z") % 2 == 1
    sent = (jnp.where(odd, second, first), jnp.where(odd, first, second))
    got = [lax.ppermute(sent[which], NAMES, crossing(which)) for which in range(2)]
    return jnp.where(odd, got[1], got[0]), jnp.where(odd, got[0], got[1])


def per_device(
    residual_in, up_first, down_first, gain_first, up_second, down_second, gain_second, cotangent
):
    gain_a = gain_first.astype(F32)
    gain_b = gain_second.astype(F32)
    own_rows = residual_in[0].astype(F32)
    cot_rows = cotangent[0]

    gain_up_a = dot(jnp.broadcast_to(gain_first[None], (8, 768)), up_first)[0]
    down_sum = jnp.sum(down_first.astype(F32), axis=1)
    gain_up_b = dot(jnp.broadcast_to(gain_second[None], (8, 384)), up_second)[0]

    stats = pack_columns([jnp.sum(own_rows, axis=1), jnp.sum(own_rows * own_rows, axis=1)])
    stats = jnp.concatenate([stats, jnp.zeros((16, LANES), BF)], axis=0)
    high_a, low_a, _ = split3(gain_up_a)
    high_d, low_d, _ = split3(down_sum)
    weights = jnp.concatenate([high_a, low_a, high_d, low_d]).reshape(8, 384)
    message = jnp.concatenate([jnp.concatenate([cot_rows, weights], axis=0), stats], axis=1)
    got = send_all(message, DP, 16)
    cot_all = got[:, :16, :384].reshape(256, 384)
    sums = jnp.sum(got[:, :8, 384:].astype(F32), axis=0)
    row_sum, square = read_columns(sums, 2)
    mean_a = (row_sum / D)[:, None]
    rstd_a = lax.rsqrt((square / D)[:, None] - mean_a * mean_a + EPS)
    totals = jnp.sum(got[:, 16:, :384].astype(F32), axis=0).reshape(4, 768)
    gain_up_a = totals[0] + totals[1]
    down_sum = totals[2] + totals[3]
    nhat_a = (own_rows - mean_a) * rstd_a
    normed = (nhat_a * gain_a).astype(BF)

    high_b, low_b, _ = split3(gain_up_b)
    extra = jnp.concatenate([high_b, low_b]).reshape(8, 384)
    gathered = gather_row(jnp.concatenate([normed, extra], axis=1))
    totals = jnp.sum(gathered[:, 768:].reshape(32, 8, 384).astype(F32), axis=0).reshape(2, 1536)
    gain_up_b = totals[0] + totals[1]
    part = dot(gathered[:, :768], up_first).astype(BF)
    hidden_a = jnp.sum(exchange(part.reshape(16, 16, 768), DP).astype(F32), axis=0)
    active = send_all(gelu_value(hidden_a).astype(BF), DP, 16).reshape(256, 768)
    part = dot(active, down_first).astype(BF)
    shift = jnp.sum(active.astype(F32) * down_sum, axis=1)
    mixed, (shift,) = scatter_row(part, [shift])
    middle_rows = (own_rows + mixed).astype(BF)
    mean_rows = mean_a[:, 0] + shift / D

    mean_cols = pack_columns([mean_rows])
    first, second = cross(
        jnp.concatenate([middle_rows[:, :384], mean_cols], axis=1),
        jnp.concatenate([middle_rows[:, 384:], mean_cols], axis=1),
    )
    middle_own = jnp.concatenate([first, second], axis=0)
    middle_all = swap_order(send_all(middle_own, DP, 16).reshape(256, 512))
    mean_all = read_columns(middle_all[:, 384:], 1)[0][:, None]
    mean_own = read_columns(middle_own[:, 384:], 1)[0][:, None]
    middle_own = middle_own[:, :384].astype(F32)
    centred = middle_all[:, :384].astype(F32) - mean_all
    spread = jnp.sum(centred * centred, axis=1)
    part = jnp.concatenate(
        [
            dot((centred * gain_b).astype(BF), up_second).astype(BF),
            contract_cols(swap_order(cot_all), down_second).astype(BF),
        ],
        axis=1,
    )
    both, (spread,) = scatter_row(part, [spread])
    rstd_rows = lax.rsqrt(spread / D + EPS)
    hidden_b = both[:, :1536] * rstd_rows[:, None]
    active_b = gelu_value(hidden_b).astype(BF)
    d_hid_b = (both[:, 1536:] * gelu_slope(hidden_b)).astype(BF)
    d_hid_float = d_hid_b.astype(F32)
    cols = pack_columns(
        [
            jnp.sum(d_hid_float * gain_up_b, axis=1),
            jnp.sum(d_hid_float * hidden_b, axis=1),
            rstd_rows,
        ]
    )
    gathered = gather_row(jnp.concatenate([active_b, d_hid_b, cols], axis=1))
    part = jnp.concatenate(
        [
            dot(gathered[:, :1536], down_second).astype(BF),
            contract_cols(gathered[:, 1536:3072], up_second).astype(BF),
            gathered[:, 3072:],
        ],
        axis=1,
    )
    got = exchange(swap_order(part).reshape(16, 16, 896), DP)
    sums = jnp.sum(got.astype(F32), axis=0)
    residual_out = (middle_own + sums[:, :384]).astype(BF)
    sum_one, sum_two = read_columns(sums[:, 768:], 2)
    rstd_own = read_columns(got[0, :, 768:], 3)[2][:, None]
    nhat_b = (middle_own - mean_own) * rstd_own
    grad_own = cot_rows.astype(F32) + rstd_own * (
        sums[:, 384:768] * gain_b - (sum_one / D)[:, None] - nhat_b * (sum_two / D)[:, None]
    )
    grad_own = grad_own.astype(BF)

    first, second = cross(grad_own[:8], grad_own[8:])
    grad_rows = jnp.concatenate([first, second], axis=1)
    part = contract_cols(gather_row(grad_rows), down_first).astype(BF)
    d_act_a = jnp.sum(exchange(part.reshape(16, 16, 768), DP).astype(F32), axis=0)
    d_hid_a = (d_act_a * gelu_slope(hidden_a)).astype(BF)
    d_hid_float = d_hid_a.astype(F32)
    cols = pack_columns(
        [jnp.sum(d_hid_float * gain_up_a, axis=1), jnp.sum(d_hid_float * hidden_a, axis=1)]
    )
    gathered = send_all(jnp.concatenate([d_hid_a, cols], axis=1), DP, 16).reshape(256, 896)
    part = contract_cols(gathered[:, :768], up_first).astype(BF)
    sums = read_columns(gathered[:, 768:], 2)
    d_norm_a, (sum_one, sum_two) = scatter_row(part, sums)
    result = grad_rows.astype(F32) + rstd_a * (
        d_norm_a * gain_a - (sum_one / D)[:, None] - nhat_a * (sum_two / D)[:, None]
    )
    return residual_out[None], result.astype(BF)[None]


def solution(mesh):
    fine = Mesh(mesh.devices.reshape(SIZES), NAMES)
    row = ("xh", "core", "z")
    return jax.shard_map(
        per_device,
        mesh=fine,
        in_specs=(
            P(None, row, DP),
            P(DP, row),
            P(row, DP),
            P(DP),
            P(row, DP),
            P(DP, row),
            P(row),
            P(None, DP, row),
        ),
        out_specs=(P(None, DP, row), P(None, row, DP)),
        check_vma=False,
    )
```

time: 1730 us -> 393 us (0.23)
  the two profiles are of different devices: /device:TPU:4 before, /device:TPU:64 now
where the time goes in v1:
time: 393 us; the launch traced here: 392 us
  blocking collectives  156 us (40%)
  waiting for transfers between devices  116 us (30%)
  starting transfers between devices  61.5 us (16%)
  local copies, waits for them, and re-layouts  20.7 us (5%)
  between operations  14.9 us (4%)
  matrix products  12.2 us (3%)
  other arithmetic  10.2 us (3%)
    all_to_all x9, blocking collectives, exchange(): return lax.all_to_all(blocks, axis, 0, 0)  152 us
    all_to_all x7, waiting for transfers between devices, exchange(): return lax.all_to_all(blocks, axis, 0, 0)  101 us
    all_to_all x7, starting transfers between devices, exchange(): return lax.all_to_all(blocks, axis, 0, 0)  56 us
    all_gather x1, waiting for transfers between devices, gather_row(): return lax.all_gather(part, 'core', axis=0, tiled=True)  9.43 us
  transfers between devices with their start and end apart: 12, of which 10 were waited for; matrix products, arithmetic and copies ran while one was open for 1% of the time, Pallas kernels for 0%

profile of v1, /device:TPU:64, one launch (start us, length us, event | category | flops | bytes accessed | tf_op | source)
XLA Modules:
  0.0 391.6 jit_solution(9145122452427184682)
XLA Ops:
  7.2 1.0 convert_reduce_fusion.10
  8.2 0.8 fusion.54
  9.6 0.7 reshape.497
  10.3 1.6 convolution_reduce_fusion.1
  12.3 0.8 broadcast_in_dim.36
  13.1 8.1 %all-to-all-start = ((bf16[16,24,512]{2,1,0:T(8,128)(2,1)}), bf16[16,24,512]{2,1,0:T(8,128)(2,1)S(1)}, u32[]{:S(2)}, u32[]{:S(2)}) async-start(bf16[16,24,512]{2,1,0:T(8,128)(2,1)} %broadcast_in_dim.36), calls=%async_computation | async-start | bytes 786432 | tf_op jit(solution)/shard_map/all_to_all | solution.py:61
  21.6 14.1 %all-to-all-done = bf16[16,24,512]{2,1,0:T(8,128)(2,1)S(1)} async-done(((bf16[16,24,512]{2,1,0:T(8,128)(2,1)}), bf16[16,24,512]{2,1,0:T(8,128)(2,1)S(1)}, u32[]{:S(2)}, u32[]{:S(2)}) %all-to-all-start) | async-done | bytes 393248 | tf_op jit(solution)/shard_map/all_to_all | solution.py:61
  36.0 0.5 copy-done.20
  36.6 22.9 %all_to_all.80 = bf16[16,8,1152]{2,1,0:T(8,128)(2,1)S(1)} all-to-all(bf16[16,8,1152]{2,1,0:T(8,128)(2,1)S(1)} %broadcast_in_dim.38), channel_id=1, replica_groups=mesh['xh'=2,'core'=2,'z'=8,'y'=8,'xl'=2] {'xh','z'}, dimensions={0} | all-to-all | bytes 589824 | tf_op jit(solution)/shard_map/all_to_all | solution.py:61
  59.4 2.2 all_gather.9
  62.1 19.1 %all_to_all.81 = bf16[16,16,768]{2,1,0:T(8,128)(2,1)S(1)} all-to-all(bf16[16,16,768]{2,1,0:T(8,128)(2,1)S(1)} %bitcast.191), channel_id=1, replica_groups=mesh['xh'=2,'core'=2,'z'=8,'y'=8,'xl'=2] {'y','xl'}, dimensions={0} | all-to-all | bytes 786432 | tf_op jit(solution)/shard_map/all_to_all | solution.py:61
  81.4 0.8 broadcast_in_dim.39
  82.1 3.6 all-to-all-start.3
  85.7 0.6 slice_add_fusion.34
  86.3 13.3 %all-to-all-done.3 = bf16[16,16,768]{2,1,0:T(8,128)(2,1)S(1)} async-done(((bf16[16,16,768]{2,1,0:T(8,128)(2,1)}), bf16[16,16,768]{2,1,0:T(8,128)(2,1)S(1)}, u32[]{:S(2)}, u32[]{:S(2)}) %all-to-all-start.3) | async-done | bytes 393248 | tf_op jit(solution)/shard_map/all_to_all | solution.py:61
  100.3 0.5 convolution_convert_fusion.4
  101.2 4.1 %all_to_all.82 = bf16[2,128,896]{2,1,0:T(8,128)(2,1)S(1)} all-to-all(bf16[2,128,896]{2,1,0:T(8,128)(2,1)S(1)} %concatenate.132), channel_id=1, replica_groups=mesh['xh'=2,'core'=2,'z'=8,'y'=8,'xl'=2] {'core'}, dimensions={0} | all-to-all | bytes 917504 | tf_op jit(solution)/shard_map/all_to_all | solution.py:61
  105.6 0.8 concatenate.138
  106.4 4.7 %all-to-all-start.5 = ((bf16[16,8,896]{2,1,0:T(8,128)(2,1)}), bf16[16,8,896]{2,1,0:T(8,128)(2,1)S(1)}, u32[]{:S(2)}, u32[]{:S(2)}) async-start(bf16[16,8,896]{2,1,0:T(8,128)(2,1)} %concatenate.138), calls=%async_computation.5 | async-start | bytes 458752 | tf_op jit(solution)/shard_map/all_to_all | solution.py:61
  111.1 11.2 %all-to-all-done.5 = bf16[16,8,896]{2,1,0:T(8,128)(2,1)S(1)} async-done(((bf16[16,8,896]{2,1,0:T(8,128)(2,1)}), bf16[16,8,896]{2,1,0:T(8,128)(2,1)S(1)}, u32[]{:S(2)}, u32[]{:S(2)}) %all-to-all-start.5) | async-done | bytes 229408 | tf_op jit(solution)/shard_map/all_to_all | solution.py:61
  122.7 1.9 collective-permute-start
  124.6 0.7 collective-permute-start.1
  125.3 3.0 collective-permute-done
  128.3 0.7 broadcast_in_dim.41
  129.0 19.7 %all-to-all-start.6 = ((bf16[16,16,512]{2,1,0:T(8,128)(2,1)}), bf16[16,16,512]{2,1,0:T(8,128)(2,1)S(1)}, u32[]{:S(2)}, u32[]{:S(2)}) async-start(bf16[16,16,512]{2,1,0:T(8,128)(2,1)} %broadcast_in_dim.41), calls=%async_computation.6 | async-start | bytes 524288 | tf_op jit(solution)/shard_map/all_to_all | solution.py:61
  148.7 0.6 convert_element_type.557
  149.4 1.9 convolution_convert_fusion
  151.2 9.1 %all-to-all-done.6 = bf16[16,16,512]{2,1,0:T(8,128)(2,1)S(1)} async-done(((bf16[16,16,512]{2,1,0:T(8,128)(2,1)}), bf16[16,16,512]{2,1,0:T(8,128)(2,1)S(1)}, u32[]{:S(2)}, u32[]{:S(2)}) %all-to-all-start.6) | async-done | bytes 262176 | tf_op jit(solution)/shard_map/all_to_all | solution.py:61
  160.3 0.7 copy-done.8
  161.0 1.0 copy.121
  162.2 0.6 copy-done.16
  163.0 0.5 fusion.104
  163.6 1.4 copy.125
  164.9 1.3 copy.124
  166.2 1.3 copy.123
  167.6 2.2 convolution_convert_fusion.1
  169.8 3.6 concatenate.144
  173.4 6.2 %all_to_all.83 = bf16[2,128,3200]{2,1,0:T(8,128)(2,1)S(1)} all-to-all(bf16[2,128,3200]{2,1,0:T(8,128)(2,1)} %concatenate.144), channel_id=1, replica_groups=mesh['xh'=2,'core'=2,'z'=8,'y'=8,'xl'=2] {'core'}, dimensions={0} | all-to-all | bytes 3276800 | tf_op jit(solution)/shard_map/all_to_all | solution.py:61
  180.3 0.5 copy-done.11
  180.8 1.1 concatenate.149
  181.9 5.8 %all-to-all-start.8 = ((bf16[16,8,3200]{2,1,0:T(8,128)(2,1)}), bf16[16,8,3200]{2,1,0:T(8,128)(2,1)S(1)}, u32[]{:S(2)}, u32[]{:S(2)}) async-start(bf16[16,8,3200]{2,1,0:T(8,128)(2,1)} %concatenate.149), calls=%async_computation.8 | async-start | bytes 1638400 | tf_op jit(solution)/shard_map/all_to_all | solution.py:61
  187.7 1.0 convert_reduce_fusion.7
  188.7 21.8 %all-to-all-done.8 = bf16[16,8,3200]{2,1,0:T(8,128)(2,1)S(1)} async-done(((bf16[16,8,3200]{2,1,0:T(8,128)(2,1)}), bf16[16,8,3200]{2,1,0:T(8,128)(2,1)S(1)}, u32[]{:S(2)}, u32[]{:S(2)}) %all-to-all-start.8) | async-done | bytes 819232 | tf_op jit(solution)/shard_map/all_to_all | solution.py:61
  211.8 29.2 %all_to_all.84 = bf16[16,8,3200]{2,1,0:T(8,128)(2,1)} all-to-all(bf16[16,8,3200]{2,1,0:T(8,128)(2,1)S(1)} %broadcast_in_dim.43), channel_id=1, replica_groups=mesh['xh'=2,'core'=2,'z'=8,'y'=8,'xl'=2] {'xh','z'}, dimensions={0} | all-to-all | bytes 1638400 | tf_op jit(solution)/shard_map/all_to_all | solution.py:61
  241.1 9.4 %all-gather.2.cloned.1.call-done = bf16[256,3200]{1,0:T(8,128)(2,1)} async-done(((bf16[128,3200]{1,0:T(8,128)(2,1)}), bf16[256,3200]{1,0:T(8,128)(2,1)}) %all-gather.2.cloned.1.call-update) | async-done | bytes 1638416 | tf_op jit(solution)/shard_map/all_gather | solution.py:70
  250.5 1.8 convolution_convert_fusion.6
  252.3 1.7 convolution_convert_fusion.7
  254.1 0.8 copy.135
  255.0 7.7 %all-to-all-start.10 = ((bf16[16,16,896]{2,1,0:T(8,128)(2,1)}), bf16[16,16,896]{2,1,0:T(8,128)(2,1)S(1)}, u32[]{:S(2)}, u32[]{:S(2)}) async-start(bf16[16,16,896]{2,1,0:T(8,128)(2,1)} %bitcast.33), calls=%async_computation.10 | async-start | bytes 917504 | tf_op jit(solution)/shard_map/all_to_all | solution.py:61
  262.9 16.6 %all-to-all-done.10 = bf16[16,16,896]{2,1,0:T(8,128)(2,1)S(1)} async-done(((bf16[16,16,896]{2,1,0:T(8,128)(2,1)}), bf16[16,16,896]{2,1,0:T(8,128)(2,1)S(1)}, u32[]{:S(2)}, u32[]{:S(2)}) %all-to-all-start.10) | async-done | bytes 458784 | tf_op jit(solution)/shard_map/all_to_all | solution.py:61
  280.0 0.6 fusion.70
  280.6 2.3 collective-permute-start.2
  282.9 0.7 collective-permute-start.3
  283.6 2.6 collective-permute-done.2
  286.2 32.0 %all_to_all.85 = bf16[16,8,768]{2,1,0:T(8,128)(2,1)S(1)} all-to-all(bf16[16,8,768]{2,1,0:T(8,128)(2,1)S(1)} %broadcast_in_dim.45), channel_id=1, replica_groups=mesh['xh'=2,'core'=2,'z'=8,'y'=8,'xl'=2] {'xh','z'}, dimensions={0} | all-to-all | bytes 393216 | tf_op jit(solution)/shard_map/all_to_all | solution.py:61
  318.1 2.1 all_gather.11
  320.2 1.2 convolution_convert_fusion.3
  321.5 6.3 %all-to-all-start.12 = ((bf16[16,16,768]{2,1,0:T(8,128)(2,1)}), bf16[16,16,768]{2,1,0:T(8,128)(2,1)S(1)}, u32[]{:S(2)}, u32[]{:S(2)}) async-start(bf16[16,16,768]{2,1,0:T(8,128)(2,1)} %bitcast.38), calls=%async_computation.12 | async-start | bytes 786432 | tf_op jit(solution)/shard_map/all_to_all | solution.py:61
  327.8 14.9 %all-to-all-done.12 = bf16[16,16,768]{2,1,0:T(8,128)(2,1)S(1)} async-done(((bf16[16,16,768]{2,1,0:T(8,128)(2,1)}), bf16[16,16,768]{2,1,0:T(8,128)(2,1)S(1)}, u32[]{:S(2)}, u32[]{:S(2)}) %all-to-all-start.12) | async-done | bytes 393248 | tf_op jit(solution)/shard_map/all_to_all | solution.py:61
  343.7 18.7 %all_to_all.86 = bf16[16,16,896]{2,1,0:T(8,128)(2,1)S(1)} all-to-all(bf16[16,16,896]{2,1,0:T(8,128)(2,1)S(1)} %broadcast_in_dim.47), channel_id=1, replica_groups=mesh['xh'=2,'core'=2,'z'=8,'y'=8,'xl'=2] {'y','xl'}, dimensions={0} | all-to-all | bytes 917504 | tf_op jit(solution)/shard_map/all_to_all | solution.py:61
  362.4 0.5 convolution_convert_fusion.2
  363.7 4.1 %all_to_all.87 = bf16[2,128,896]{2,1,0:T(8,128)(2,1)S(1)} all-to-all(bf16[2,128,896]{2,1,0:T(8,128)(2,1)S(1)} %concatenate.161), channel_id=1, replica_groups=mesh['xh'=2,'core'=2,'z'=8,'y'=8,'xl'=2] {'core'}, dimensions={0} | all-to-all | bytes 917504 | tf_op jit(solution)/shard_map/all_to_all | solution.py:61
  368.3 15.5 %all_to_all.88 = bf16[16,8,896]{2,1,0:T(8,128)(2,1)S(1)} all-to-all(bf16[16,8,896]{2,1,0:T(8,128)(2,1)S(1)} %concatenate.169), channel_id=1, replica_groups=mesh['xh'=2,'core'=2,'z'=8,'y'=8,'xl'=2] {'xh','z'}, dimensions={0} | all-to-all | bytes 458752 | tf_op jit(solution)/shard_map/all_to_all | solution.py:61
  384.1 0.7 fusion.76
  (174 shorter events, 9.4 us)
Async XLA Ops:
  7.2 14.1 %copy-start = (bf16[384,1536]{1,0:T(8,128)(2,1)S(1)}, bf16[384,1536]{1,0:T(8,128)(2,1)}, u32[]{:S(2)}) copy-start(bf16[384,1536]{1,0:T(8,128)(2,1)} %param.12) | copy-start | bytes 3538948
  7.2 4.7 %copy-start.1 = (bf16[768,768]{1,0:T(8,128)(2,1)S(1)}, bf16[768,768]{1,0:T(8,128)(2,1)}, u32[]{:S(2)}) copy-start(bf16[768,768]{1,0:T(8,128)(2,1)} %param.10) | copy-start | bytes 3538948
  10.3 1.9 copy-start.12
  11.9 9.4 %copy-start.17 = (bf16[768]{0:T(1024)(128)(2,1)S(1)}, bf16[768]{0:T(1024)(128)(2,1)}, u32[]{:S(2)}) copy-start(bf16[768]{0:T(1024)(128)(2,1)} %param.11) | copy-start | bytes 4612
  11.9 9.4 %copy-start.22 = (bf16[384]{0:T(512)(128)(2,1)S(1)}, bf16[384]{0:T(512)(128)(2,1)}, u32[]{:S(2)}) copy-start(bf16[384]{0:T(512)(128)(2,1)} %param.14) | copy-start | bytes 2308
  12.3 23.6 %copy-start.9 = (bf16[1,8,768]{2,1,0:T(8,128)(2,1)S(1)}, bf16[1,8,768]{2,1,0:T(8,128)(2,1)}, u32[]{:S(2)}) copy-start(bf16[1,8,768]{2,1,0:T(8,128)(2,1)} %param.8) | copy-start | bytes 36868
  13.1 22.6 %all-to-all-start = ((bf16[16,24,512]{2,1,0:T(8,128)(2,1)}), bf16[16,24,512]{2,1,0:T(8,128)(2,1)S(1)}, u32[]{:S(2)}, u32[]{:S(2)}) async-start(bf16[16,24,512]{2,1,0:T(8,128)(2,1)} %broadcast_in_dim.36), calls=%async_computation | async-start | bytes 786432 | tf_op jit(solution)/shard_map/all_to_all | solution.py:61
  35.7 50.0 %copy-start.2 = (bf16[16,24,512]{2,1,0:T(8,128)(2,1)}, bf16[16,24,512]{2,1,0:T(8,128)(2,1)S(1)}, u32[]{:S(2)}) copy-start(bf16[16,24,512]{2,1,0:T(8,128)(2,1)S(1)} %all-to-all-done) | copy-start | bytes 1179652
  35.7 25.9 %copy-start.5 = (bf16[768,768]{1,0:T(8,128)(2,1)S(1)}, bf16[768,768]{1,0:T(8,128)(2,1)}, u32[]{:S(2)}) copy-start(bf16[768,768]{1,0:T(8,128)(2,1)} %param.9) | copy-start | bytes 3538948
  35.9 0.6 copy-start.20
  35.9 26.2 %copy-start.18 = (f32[8]{0:T(128)}, f32[8]{0:T(128)S(1)}, u32[]{:S(2)}) copy-start(f32[8]{0:T(128)S(1)} %get-tuple-element.10) | copy-start | bytes 100
  61.6 19.6 %copy-start.7 = (bf16[256,1152]{1,0:T(8,128)(2,1)}, bf16[256,1152]{1,0:T(8,128)(2,1)S(1)}, u32[]{:S(2)}) copy-start(bf16[256,1152]{1,0:T(8,128)(2,1)S(1)} %all_gather.9) | copy-start | bytes 1769476
  82.1 17.5 %all-to-all-start.3 = ((bf16[16,16,768]{2,1,0:T(8,128)(2,1)}), bf16[16,16,768]{2,1,0:T(8,128)(2,1)S(1)}, u32[]{:S(2)}, u32[]{:S(2)}) async-start(bf16[16,16,768]{2,1,0:T(8,128)(2,1)} %broadcast_in_dim.39), calls=%async_computation.3 | async-start | bytes 786432 | tf_op jit(solution)/shard_map/all_to_all | solution.py:61
  105.6 0.8 copy-start.10
  105.6 43.1 %copy-start.23 = (bf16[384]{0:T(512)(128)(2,1)S(1)}, bf16[384]{0:T(512)(128)(2,1)}, u32[]{:S(2)}) copy-start(bf16[384]{0:T(512)(128)(2,1)} %param.14) | copy-start | bytes 2308
  105.6 43.7 %copy-start.3 = (bf16[16,24,512]{2,1,0:T(8,128)(2,1)S(1)}, bf16[16,24,512]{2,1,0:T(8,128)(2,1)}, u32[]{:S(2)}) copy-start(bf16[16,24,512]{2,1,0:T(8,128)(2,1)} %copy-done.2) | copy-start | bytes 1179652
  106.4 15.9 %all-to-all-start.5 = ((bf16[16,8,896]{2,1,0:T(8,128)(2,1)}), bf16[16,8,896]{2,1,0:T(8,128)(2,1)S(1)}, u32[]{:S(2)}, u32[]{:S(2)}) async-start(bf16[16,8,896]{2,1,0:T(8,128)(2,1)} %concatenate.138), calls=%async_computation.5 | async-start | bytes 458752 | tf_op jit(solution)/shard_map/all_to_all | solution.py:61
  122.7 5.5 %collective-permute-start = (bf16[8,512]{1,0:T(8,128)(2,1)S(1)}, bf16[8,512]{1,0:T(8,128)(2,1)S(1)}, u32[]{:S(2)}, u32[]{:S(2)}) collective-permute-start(bf16[8,512]{1,0:T(8,128)(2,1)S(1)} %get-tuple-element.52), channel_id=1, source_target_pairs={{0,16},{1,48},{2,80},{3,112},{4,144},{5,176},{6,208},{7,240},{8,27... | collective-permute-start | bytes 24584 | tf_op jit(solution)/shard_map/ppermute | solution.py:106
  124.6 3.6 collective-permute-start.1
  129.0 31.4 %all-to-all-start.6 = ((bf16[16,16,512]{2,1,0:T(8,128)(2,1)}), bf16[16,16,512]{2,1,0:T(8,128)(2,1)S(1)}, u32[]{:S(2)}, u32[]{:S(2)}) async-start(bf16[16,16,512]{2,1,0:T(8,128)(2,1)} %broadcast_in_dim.41), calls=%async_computation.6 | async-start | bytes 524288 | tf_op jit(solution)/shard_map/all_to_all | solution.py:61
  160.3 0.7 copy-start.8
  162.2 0.6 copy-start.16
  180.0 0.8 copy-start.11
  181.9 28.6 %all-to-all-start.8 = ((bf16[16,8,3200]{2,1,0:T(8,128)(2,1)}), bf16[16,8,3200]{2,1,0:T(8,128)(2,1)S(1)}, u32[]{:S(2)}, u32[]{:S(2)}) async-start(bf16[16,8,3200]{2,1,0:T(8,128)(2,1)} %concatenate.149), calls=%async_computation.8 | async-start | bytes 1638400 | tf_op jit(solution)/shard_map/all_to_all | solution.py:61
  187.7 62.8 %all-gather.2.cloned.1.call-start = ((), (), s32[]{:S(2)}) async-start(), calls=%async_computation.16 | async-start | bytes 2457600 | tf_op jit(solution)/shard_map/all_gather | solution.py:70
  250.5 1.8 copy-start.4
  252.3 1.8 slice-start
  254.1 25.9 %copy-start.13 = (bf16[1,16,384]{2,1,0:T(8,128)(2,1)S(1)}, bf16[1,16,384]{2,1,0:T(8,128)(2,1)}, u32[]{:S(2)}) copy-start(bf16[1,16,384]{2,1,0:T(8,128)(2,1)} %param.15) | copy-start | bytes 36868
  254.1 25.9 %copy-start.14 = (f32[384]{0:T(512)S(1)}, f32[384]{0:T(512)}, u32[]{:S(2)}) copy-start(f32[384]{0:T(512)} %convert_element_type.557) | copy-start | bytes 4612
  255.0 24.6 %all-to-all-start.10 = ((bf16[16,16,896]{2,1,0:T(8,128)(2,1)}), bf16[16,16,896]{2,1,0:T(8,128)(2,1)S(1)}, u32[]{:S(2)}, u32[]{:S(2)}) async-start(bf16[16,16,896]{2,1,0:T(8,128)(2,1)} %bitcast.33), calls=%async_computation.10 | async-start | bytes 917504 | tf_op jit(solution)/shard_map/all_to_all | solution.py:61
  280.6 5.5 %collective-permute-start.2 = (bf16[8,384]{1,0:T(8,128)(2,1)S(1)}, bf16[8,384]{1,0:T(8,128)(2,1)S(1)}, u32[]{:S(2)}, u32[]{:S(2)}) collective-permute-start(bf16[8,384]{1,0:T(8,128)(2,1)S(1)} %get-tuple-element.56), channel_id=1, source_target_pairs={{0,16},{1,48},{2,80},{3,112},{4,144},{5,176},{6,208},{7,240},{8,27... | collective-permute-start | bytes 18440 | tf_op jit(solution)/shard_map/ppermute | solution.py:106
  282.9 3.2 collective-permute-start.3
  320.2 7.6 %copy-start.15 = (f32[2,384]{1,0:T(2,128)S(1)}, f32[2,384]{1,0:T(2,128)}, u32[]{:S(2)}) copy-start(f32[2,384]{1,0:T(2,128)} %get-tuple-element.58) | copy-start | bytes 9220
  321.5 21.2 %all-to-all-start.12 = ((bf16[16,16,768]{2,1,0:T(8,128)(2,1)}), bf16[16,16,768]{2,1,0:T(8,128)(2,1)S(1)}, u32[]{:S(2)}, u32[]{:S(2)}) async-start(bf16[16,16,768]{2,1,0:T(8,128)(2,1)} %bitcast.38), calls=%async_computation.12 | async-start | bytes 786432 | tf_op jit(solution)/shard_map/all_to_all | solution.py:61
  327.8 34.6 %copy-start.6 = (bf16[768,768]{1,0:T(8,128)(2,1)S(1)}, bf16[768,768]{1,0:T(8,128)(2,1)}, u32[]{:S(2)}) copy-start(bf16[768,768]{1,0:T(8,128)(2,1)} %param.9) | copy-start | bytes 3538948
  367.9 16.1 %copy-start.19 = (f32[8]{0:T(128)S(1)}, f32[8]{0:T(128)}, u32[]{:S(2)}) copy-start(f32[8]{0:T(128)} %copy-done.18) | copy-start | bytes 100
  368.0 16.1 %copy-start.21 = (f32[8]{0:T(128)S(1)}, f32[8]{0:T(128)}, u32[]{:S(2)}) copy-start(f32[8]{0:T(128)} %copy-done.20) | copy-start | bytes 100
Sparse Core Ops, SparseCore 0:
  241.2 9.2 all-gather.1

commit v2 on v1

v2 whole, which is shorter than its diff:
```python
import jax
import jax.numpy as jnp
from jax import lax
from jax.sharding import Mesh, PartitionSpec as P

D = 12288
EPS = 1e-05
GELU_C0 = 0.7978845608028654
GELU_C1 = 0.044715
BF = jnp.bfloat16
F32 = jnp.float32
NAMES = ("xh", "core", "z", "y", "xl")
SIZES = (2, 2, 8, 8, 2)
ROW = ("xh", "z")
DP = ("y", "xl")
LANES = 128


def gelu_value(hidden):
    inner = jnp.tanh(GELU_C0 * (hidden + GELU_C1 * hidden * hidden * hidden))
    return 0.5 * hidden * (1.0 + inner)


def gelu_slope(hidden):
    inner = jnp.tanh(GELU_C0 * (hidden + GELU_C1 * hidden * hidden * hidden))
    return 0.5 * (1.0 + inner) + 0.5 * hidden * (1.0 - inner * inner) * GELU_C0 * (
        1.0 + 3.0 * GELU_C1 * hidden * hidden
    )


def dot(left, right):
    return jnp.dot(left, right, preferred_element_type=F32)


def contract_cols(left, right):
    return lax.dot_general(left, right, (((1,), (1,)), ((), ())), preferred_element_type=F32)


def row_dot(values, row):
    return lax.dot_general(
        values,
        jnp.broadcast_to(row, (LANES, values.shape[1])),
        (((1,), (1,)), ((), ())),
        precision=lax.Precision.HIGHEST,
        preferred_element_type=F32,
    )


def split3(value):
    high = lax.reduce_precision(value, 8, 7)
    rest = value - high
    mid = lax.reduce_precision(rest, 8, 7)
    return high, mid, rest - mid


def pack(columns):
    rows = columns[0].shape[0]
    lane = lax.broadcasted_iota(jnp.int32, (rows, LANES), 1)
    block = jnp.zeros((rows, LANES), F32)
    for number, column in enumerate(columns):
        for part, piece in enumerate(split3(column)):
            block = jnp.where(lane == 3 * number + part, piece, block)
    return block.astype(BF)


def unpack(floats, number):
    at = 3 * number
    return floats[..., at : at + 1] + floats[..., at + 1 : at + 2] + floats[..., at + 2 : at + 3]


def exchange(blocks, axis):
    return lax.all_to_all(blocks, axis, 0, 0)


def send_all(rows, axis):
    got = exchange(jnp.broadcast_to(rows[None], (16,) + rows.shape), axis)
    return got.reshape(16 * rows.shape[0], rows.shape[1])


def both_cores(values):
    return lax.all_gather(values, "core", axis=0, tiled=False)


def tile_rows(vector, rows):
    block = vector.reshape(-1, LANES)
    return jnp.concatenate([block, jnp.zeros((rows - block.shape[0], LANES), vector.dtype)], axis=0)


def crossing():
    pairs = []
    for xh in range(2):
        for core in range(2):
            for z in range(8):
                for group in range(16):
                    source = ((xh * 2 + core) * 8 + z) * 16 + group
                    pairs.append((source, (2 * group + core) * 16 + xh * 8 + z))
    return pairs


def per_device(
    residual_in, up_first, down_first, gain_first, up_second, down_second, gain_second, cotangent
):
    core = lax.axis_index("core")
    chunk = lax.axis_index("xh") * 8 + lax.axis_index("z")
    own_row = (lax.axis_index("xh") * 16 + core * 8 + lax.axis_index("z")) * 8
    gain_a = gain_first.astype(F32)
    gain_b = gain_second.astype(F32)
    x_own = residual_in[0]
    cot_own = cotangent[0]

    u_a = dot(jnp.broadcast_to(gain_first[None], (8, 768)), up_first)[0].astype(BF)
    u_b = dot(jnp.broadcast_to(gain_second[None], (8, 384)), up_second)[0].astype(BF)
    d_high, d_mid, _ = split3(contract_cols(jnp.ones((8, 768), BF), down_first)[0])

    floats = x_own.astype(F32)
    centre = jnp.sum(floats, axis=1, keepdims=True) / 768
    spread = jnp.sum((floats - centre) * (floats - centre), axis=1, keepdims=True)
    u_b = tile_rows(u_b, 16)
    message = jnp.concatenate([x_own, pack([centre, spread]), u_b[:8], u_b[8:]], axis=1)
    got = both_cores(send_all(message, ROW))
    gain_up_b = jnp.sum(got[:, :, 896:].reshape(32, 8, 256).astype(F32), axis=0)
    gain_up_b = jnp.concatenate([gain_up_b[:, :128], gain_up_b[:4, 128:]], axis=0).reshape(2, 768)
    gain_up_b = jnp.where(core == 0, gain_up_b[:1], gain_up_b[1:])
    x_all = jnp.transpose(got.reshape(2, 2, 64, 1152), (1, 0, 2, 3)).reshape(256, 1152)
    x_cols = x_all[:, 768:896]
    x_all = x_all[:, :768]

    centred = (x_all.astype(F32) - unpack(x_cols.astype(F32), 0)) * gain_a
    part = dot(centred.astype(BF), up_first).astype(BF)
    message = jnp.concatenate(
        [
            part.reshape(16, 16, 768),
            x_cols.reshape(16, 16, LANES),
            jnp.broadcast_to(tile_rows(u_a, 16)[None], (16, 16, LANES)),
        ],
        axis=2,
    )
    got = exchange(message, DP)
    cols = got[:, :, 768:896].astype(F32)
    centres = unpack(cols, 0)
    mean_a = jnp.mean(centres, axis=0)
    off = centres - mean_a
    var_a = (jnp.sum(unpack(cols, 1), axis=0) + 768 * jnp.sum(off * off, axis=0)) / D
    rstd_a = lax.rsqrt(var_a + EPS)
    u_all = got[:, :6, 896:].reshape(16, 1, 768).astype(F32)
    gain_up_a = jnp.sum(u_all, axis=0)
    hidden_a = rstd_a * jnp.sum(got[:, :, :768].astype(F32) + off * u_all, axis=0)
    message = jnp.concatenate(
        [
            gelu_value(hidden_a).astype(BF),
            pack([mean_a, rstd_a]),
            jnp.concatenate([tile_rows(d_high, 8), tile_rows(d_mid, 8)], axis=0).astype(BF),
        ],
        axis=1,
    )
    got = send_all(message, DP)
    stats_a = got[:, 768:896]
    sums = jnp.sum(got[:, 896:].reshape(16, 2, 8, LANES).astype(F32), axis=(0, 1))
    down_sum = sums[:6].reshape(1, 768)
    active = got[:, :768]
    part = dot(active, down_first).astype(BF)
    shift = row_dot(active.astype(F32), down_sum) + unpack(stats_a.astype(F32), 0) * (D / 32)
    cols = pack([shift])
    message = jnp.stack(
        [
            jnp.concatenate([part[:, :384], cols], axis=1),
            jnp.concatenate([part[:, 384:], cols], axis=1),
        ]
    )
    got = exchange(message, "core")
    part = jnp.sum(got[:, :, :384].astype(F32), axis=0).astype(BF)
    message = jnp.concatenate([part, got[0, :, 384:], got[1, :, 384:]], axis=1)
    sums = jnp.sum(exchange(message.reshape(16, 16, 640), ROW).astype(F32), axis=0)
    mean_b = (unpack(sums[:, 384:512], 0) + unpack(sums[:, 512:], 0)) / D
    rows = lax.dynamic_slice_in_dim(x_all, chunk * 16, 16, 0)
    rows = jnp.where(core == 0, rows[:, :384], rows[:, 384:]).astype(F32)
    middle = (rows + sums[:, :384]).astype(BF)

    crossed = lax.ppermute(jnp.concatenate([middle, pack([mean_b])], axis=1), NAMES, crossing())
    middle_own = crossed[:, :384].astype(F32)
    mean_own = unpack(crossed[:, 384:].astype(F32), 0)
    got = send_all(jnp.concatenate([crossed, cot_own], axis=1), DP)
    cot_all = got[:, 512:]
    centred = got[:, :384].astype(F32) - unpack(got[:, 384:512].astype(F32), 0)
    cols = pack([row_dot(centred * centred, jnp.ones((1, 384), F32))])
    centred = (centred * gain_b).astype(BF)
    message = jnp.stack(
        [
            jnp.concatenate(
                [
                    dot(centred, up_second[:, at : at + 768]).astype(BF),
                    contract_cols(cot_all, down_second[at : at + 768]).astype(BF),
                    cols,
                ],
                axis=1,
            )
            for at in (0, 768)
        ]
    )
    got = exchange(message, "core")
    part = jnp.sum(got[:, :, :1536].astype(F32), axis=0).astype(BF)
    message = jnp.concatenate([part, got[0, :, 1536:], got[1, :, 1536:]], axis=1)
    sums = jnp.sum(exchange(message.reshape(16, 16, 1792), ROW).astype(F32), axis=0)
    spread = unpack(sums[:, 1536:1664], 0) + unpack(sums[:, 1664:], 0)
    rstd_b = lax.rsqrt(spread / D + EPS)
    hidden_b = sums[:, :768] * rstd_b
    active_b = gelu_value(hidden_b).astype(BF)
    d_hid_b = (sums[:, 768:1536] * gelu_slope(hidden_b)).astype(BF)
    floats = d_hid_b.astype(F32)
    cols = pack(
        [
            jnp.sum(floats * gain_up_b, axis=1, keepdims=True),
            jnp.sum(floats * hidden_b, axis=1, keepdims=True),
            rstd_b,
        ]
    )
    got = both_cores(send_all(jnp.concatenate([d_hid_b, cols], axis=1), ROW))
    part = contract_cols(got[0, :, :768], up_second[:, :768])
    part = part + contract_cols(got[1, :, :768], up_second[:, 768:])
    message = jnp.concatenate([part.astype(BF), got[0, :, 768:], got[1, :, 768:]], axis=1)
    got = exchange(message.reshape(16, 16, 640), DP)
    sums = jnp.sum(got.astype(F32), axis=0)
    sum_one = unpack(sums[:, 384:512], 0) + unpack(sums[:, 512:], 0)
    sum_two = unpack(sums[:, 384:512], 1) + unpack(sums[:, 512:], 1)
    rstd_own = unpack(got[0, :, 384:512].astype(F32), 2)
    nhat_b = (middle_own - mean_own) * rstd_own
    grad_own = cot_own.astype(F32) + rstd_own * (
        sums[:, :384] * gain_b - sum_one / D - nhat_b * (sum_two / D)
    )

    crossed = lax.ppermute(
        grad_own.astype(BF), NAMES, [(target, source) for source, target in crossing()]
    )
    got = send_all(jnp.concatenate([crossed, active_b], axis=1), ROW)
    grad_all = both_cores(got[:, :384])
    active_all = both_cores(got[:, 384:])
    part = contract_cols(grad_all[0], down_first[:, :384])
    part = part + contract_cols(grad_all[1], down_first[:, 384:])
    part_b = dot(active_all[0], down_second[:768]) + dot(active_all[1], down_second[768:])
    message = jnp.concatenate([part.astype(BF), part_b.astype(BF)], axis=1)
    sums = jnp.sum(exchange(message.reshape(16, 16, 1152), DP).astype(F32), axis=0)
    residual_out = (middle_own + sums[:, 768:]).astype(BF)
    d_hid_a = (sums[:, :768] * gelu_slope(hidden_a)).astype(BF)
    floats = d_hid_a.astype(F32)
    cols = pack(
        [
            jnp.sum(floats * gain_up_a, axis=1, keepdims=True),
            jnp.sum(floats * hidden_a, axis=1, keepdims=True),
        ]
    )
    got = send_all(jnp.concatenate([d_hid_a, cols], axis=1), DP)
    part = contract_cols(got[:, :768], up_first).astype(BF)
    message = jnp.concatenate([part, got[:, 768:]], axis=1).reshape(2, 2, 64, 896)
    got = exchange(jnp.transpose(message, (1, 0, 2, 3)).reshape(2, 128, 896), "core")
    part = jnp.sum(got[:, :, :768].astype(F32), axis=0).astype(BF)
    message = jnp.concatenate([part, got[0, :, 768:], got[1, :, 768:]], axis=1)
    sums = jnp.sum(exchange(message.reshape(16, 8, 1024), ROW).astype(F32), axis=0)
    sum_one = unpack(sums[:, 768:896], 0) + unpack(sums[:, 896:], 0)
    sum_two = unpack(sums[:, 768:896], 1) + unpack(sums[:, 896:], 1)
    stats = lax.dynamic_slice_in_dim(stats_a, own_row, 8, 0).astype(F32)
    rstd = unpack(stats, 1)
    nhat_a = (x_own.astype(F32) - unpack(stats, 0)) * rstd
    upstream = lax.dynamic_slice_in_dim(grad_all, own_row, 8, 1).astype(F32)
    upstream = jnp.concatenate([upstream[0], upstream[1]], axis=1)
    result = upstream + rstd * (sums[:, :768] * gain_a - sum_one / D - nhat_a * (sum_two / D))
    return residual_out[None], result.astype(BF)[None]


def solution(mesh):
    fine = Mesh(mesh.devices.reshape(SIZES), NAMES)
    row = ("xh", "core", "z")
    return jax.shard_map(
        per_device,
        mesh=fine,
        in_specs=(
            P(None, row, DP),
            P(DP, row),
            P(row, DP),
            P(DP),
            P(row, DP),
            P(DP, row),
            P(row),
            P(None, DP, row),
        ),
        out_specs=(P(None, DP, row), P(None, row, DP)),
        check_vma=False,
    )
```

time: 393 us -> 342 us (0.87)
  blocking collectives: 156 us -> 93.1 us
  waiting for transfers between devices: 116 us -> 146 us
  local copies, waits for them, and re-layouts: 20.7 us -> 6.77 us
  between operations: 14.9 us -> 1.67 us
  other arithmetic: 10.2 us -> 16.3 us
    all_to_all x9 -> x6, blocking collectives: 152 us -> 83.6 us  [exchange(): return lax.all_to_all(blocks, axis, 0, 0)]
    all_to_all x7 -> x9, waiting for transfers between devices: 101 us -> 139 us  [exchange(): return lax.all_to_all(blocks, axis, 0, 0)]
    all_gather x1 -> x0, waiting for transfers between devices: 9.43 us -> none  [gather_row(): return lax.all_gather(part, 'core', axis=0, tiled=True)]
    concatenate x17 -> x2, local copies, waits for them, and re-layouts: 7.06 us -> 0.01 us  [the longest x1 0.01 us: tile_rows(): jnp.concatenate([block, jnp.zeros((rows - block.shape[0], LANES), vector....]
    convert_element_type x24 -> x0, local copies, waits for them, and re-layouts: 6.15 us -> none  [split3(): return (high.astype(BF), mid.astype(BF), (rest - mid).astype(BF))]
    all_gather x2 -> x4, blocking collectives: 4.29 us -> 9.42 us  [both_cores(): return lax.all_gather(values, 'core', axis=0, tiled=False)]
    concatenate x12 -> x14, other arithmetic: 0.5 us -> 5.03 us  [the longest x1 1 us: per_device(): jnp.concatenate([part, got[0, :, 1536:], got[1, :, 1536:]], axis=1)]
    all_to_all x7 -> x9, starting transfers between devices: 56 us -> 59.2 us  [exchange(): return lax.all_to_all(blocks, axis, 0, 0)]
  transfers between devices with their start and end apart: 12 -> 11, of which waited for: 10 -> 11; matrix products, arithmetic and copies ran while one was open for 1% -> 2% of each run, Pallas kernels for 0% -> 0%
where the time goes in v2:
time: 342 us; the launch traced here: 341 us
  waiting for transfers between devices  146 us (43%)
  blocking collectives  93.1 us (27%)
  starting transfers between devices  63 us (18%)
  other arithmetic  16.3 us (5%)
  matrix products  13.5 us (4%)
  local copies, waits for them, and re-layouts  6.77 us (2%)
    all_to_all x9, waiting for transfers between devices, exchange(): return lax.all_to_all(blocks, axis, 0, 0)  139 us
    all_to_all x6, blocking collectives, exchange(): return lax.all_to_all(blocks, axis, 0, 0)  83.6 us
    all_to_all x9, starting transfers between devices, exchange(): return lax.all_to_all(blocks, axis, 0, 0)  59.2 us
    all_gather x4, blocking collectives, both_cores(): return lax.all_gather(values, 'core', axis=0, tiled=False)  9.42 us
  transfers between devices with their start and end apart: 11, of which 11 were waited for; matrix products, arithmetic and copies ran while one was open for 2% of the time, Pallas kernels for 0%

profile of v2, /device:TPU:64, one launch (start us, length us, event | category | flops | bytes accessed | tf_op | source)
XLA Modules:
  0.0 340.7 jit_solution(16572251296800709633)
XLA Ops:
  0.8 1.6 convolution_convert_fusion
  2.9 0.7 broadcast_in_dim.262
  3.6 12.4 %all-to-all-start = ((bf16[16,8,1152]{2,1,0:T(8,128)(2,1)}), bf16[16,8,1152]{2,1,0:T(8,128)(2,1)S(1)}, u32[]{:S(2)}, u32[]{:S(2)}) async-start(bf16[16,8,1152]{2,1,0:T(8,128)(2,1)} %broadcast_in_dim.262), calls=%async_computation | async-start | bytes 589824 | tf_op jit(solution)/shard_map/all_to_all | solution.py:72
  16.4 11.7 %all-to-all-done = bf16[16,8,1152]{2,1,0:T(8,128)(2,1)S(1)} async-done(((bf16[16,8,1152]{2,1,0:T(8,128)(2,1)}), bf16[16,8,1152]{2,1,0:T(8,128)(2,1)S(1)}, u32[]{:S(2)}, u32[]{:S(2)}) %all-to-all-start) | async-done | bytes 294944 | tf_op jit(solution)/shard_map/all_to_all | solution.py:72
  28.1 2.2 all_gather.18
  30.6 0.5 copy-done.2
  31.2 0.5 convolution_convert_fusion.3
  31.7 0.9 pad_maximum_fusion.5
  32.6 7.2 %all-to-all-start.1 = ((bf16[16,16,1024]{2,1,0:T(8,128)(2,1)}), bf16[16,16,1024]{2,1,0:T(8,128)(2,1)S(1)}, u32[]{:S(2)}, u32[]{:S(2)}) async-start(bf16[16,16,1024]{2,1,0:T(8,128)(2,1)} %pad_maximum_fusion.5), calls=%async_computation.1 | async-start | bytes 1048576 | tf_op jit(solution)/shard_map/all_to_all | solution.py:72
  39.8 0.4 convolution_reduce_fusion
  40.3 17.4 %all-to-all-done.1 = bf16[16,16,1024]{2,1,0:T(8,128)(2,1)S(1)} async-done(((bf16[16,16,1024]{2,1,0:T(8,128)(2,1)}), bf16[16,16,1024]{2,1,0:T(8,128)(2,1)S(1)}, u32[]{:S(2)}, u32[]{:S(2)}) %all-to-all-start.1) | async-done | bytes 524320 | tf_op jit(solution)/shard_map/all_to_all | solution.py:72
  59.4 19.8 %all_to_all.75 = bf16[16,16,1024]{2,1,0:T(8,128)(2,1)S(1)} all-to-all(bf16[16,16,1024]{2,1,0:T(8,128)(2,1)S(1)} %broadcast_in_dim.272), channel_id=1, replica_groups=mesh['xh'=2,'core'=2,'z'=8,'y'=8,'xl'=2] {'y','xl'}, dimensions={0} | all-to-all | bytes 1048576 | tf_op jit(solution)/shard_map/all_to_all | solution.py:72
  79.2 0.6 fusion.133
  79.9 0.5 convolution_convert_fusion.2
  80.7 0.5 fusion.37
  81.3 4.2 %all_to_all.76 = bf16[2,256,512]{2,1,0:T(8,128)(2,1)S(1)} all-to-all(bf16[2,256,512]{2,1,0:T(8,128)(2,1)S(1)} %pad_maximum_fusion.6), channel_id=1, replica_groups=mesh['xh'=2,'core'=2,'z'=8,'y'=8,'xl'=2] {'core'}, dimensions={0} | all-to-all | bytes 1048576 | tf_op jit(solution)/shard_map/all_to_all | solution.py:72
  85.6 0.8 pad_maximum_fusion.10
  86.3 5.4 %all-to-all-start.4 = ((bf16[16,16,640]{2,1,0:T(8,128)(2,1)}), bf16[16,16,640]{2,1,0:T(8,128)(2,1)S(1)}, u32[]{:S(2)}, u32[]{:S(2)}) async-start(bf16[16,16,640]{2,1,0:T(8,128)(2,1)} %pad_maximum_fusion.10), calls=%async_computation.4 | async-start | bytes 655360 | tf_op jit(solution)/shard_map/all_to_all | solution.py:72
  91.8 0.8 slice.585
  92.5 12.3 %all-to-all-done.4 = bf16[16,16,640]{2,1,0:T(8,128)(2,1)S(1)} async-done(((bf16[16,16,640]{2,1,0:T(8,128)(2,1)}), bf16[16,16,640]{2,1,0:T(8,128)(2,1)S(1)}, u32[]{:S(2)}, u32[]{:S(2)}) %all-to-all-start.4) | async-done | bytes 327712 | tf_op jit(solution)/shard_map/all_to_all | solution.py:72
  105.3 0.7 fusion.86
  106.0 1.9 collective-permute-start
  107.9 3.1 collective-permute-done
  111.1 0.6 copy-done.11
  111.7 0.8 broadcast_in_dim.281
  112.5 11.3 %all-to-all-start.5 = ((bf16[16,16,896]{2,1,0:T(8,128)(2,1)}), bf16[16,16,896]{2,1,0:T(8,128)(2,1)}, u32[]{:S(2)}, u32[]{:S(2)}) async-start(bf16[16,16,896]{2,1,0:T(8,128)(2,1)} %broadcast_in_dim.281), calls=%async_computation.5 | async-start | bytes 917504 | tf_op jit(solution)/shard_map/all_to_all | solution.py:72
  123.8 1.3 convert_element_type.230
  125.1 14.5 %all-to-all-done.5 = bf16[16,16,896]{2,1,0:T(8,128)(2,1)} async-done(((bf16[16,16,896]{2,1,0:T(8,128)(2,1)}), bf16[16,16,896]{2,1,0:T(8,128)(2,1)}, u32[]{:S(2)}, u32[]{:S(2)}) %all-to-all-start.5) | async-done | bytes 458784 | tf_op jit(solution)/shard_map/all_to_all | solution.py:72
  139.6 0.9 slice_convert_fusion
  140.6 1.5 fusion.43
  142.2 1.4 convolution_convert_fusion.5
  143.6 1.3 convolution_convert_fusion.7
  145.0 1.3 convolution_convert_fusion.4
  146.3 1.3 convolution_convert_fusion.6
  147.9 5.1 %all_to_all.77 = bf16[2,256,1664]{2,1,0:T(8,128)(2,1)S(1)} all-to-all(bf16[2,256,1664]{2,1,0:T(8,128)(2,1)S(1)} %pad_maximum_fusion), channel_id=1, replica_groups=mesh['xh'=2,'core'=2,'z'=8,'y'=8,'xl'=2] {'core'}, dimensions={0} | all-to-all | bytes 3407872 | tf_op jit(solution)/shard_map/all_to_all | solution.py:72
  153.3 1.0 pad_maximum_fusion.3
  154.3 6.6 %all-to-all-start.7 = ((bf16[16,16,1792]{2,1,0:T(8,128)(2,1)}), bf16[16,16,1792]{2,1,0:T(8,128)(2,1)S(1)}, u32[]{:S(2)}, u32[]{:S(2)}) async-start(bf16[16,16,1792]{2,1,0:T(8,128)(2,1)} %pad_maximum_fusion.3), calls=%async_computation.7 | async-start | bytes 1835008 | tf_op jit(solution)/shard_map/all_to_all | solution.py:72
  160.9 0.9 slice.636
  161.9 24.1 %all-to-all-done.7 = bf16[16,16,1792]{2,1,0:T(8,128)(2,1)S(1)} async-done(((bf16[16,16,1792]{2,1,0:T(8,128)(2,1)}), bf16[16,16,1792]{2,1,0:T(8,128)(2,1)S(1)}, u32[]{:S(2)}, u32[]{:S(2)}) %all-to-all-start.7) | async-done | bytes 917536 | tf_op jit(solution)/shard_map/all_to_all | solution.py:72
  186.9 20.5 %all_to_all.78 = bf16[16,16,896]{2,1,0:T(8,128)(2,1)S(1)} all-to-all(bf16[16,16,896]{2,1,0:T(8,128)(2,1)S(1)} %broadcast_in_dim.294), channel_id=1, replica_groups=mesh['xh'=2,'core'=2,'z'=8,'y'=8,'xl'=2] {'xh','z'}, dimensions={0} | all-to-all | bytes 917504 | tf_op jit(solution)/shard_map/all_to_all | solution.py:72
  207.4 2.5 all_gather.19
  210.7 0.7 pad_maximum_fusion.11
  211.4 3.5 %all-to-all-start.9 = ((bf16[16,16,640]{2,1,0:T(8,128)(2,1)}), bf16[16,16,640]{2,1,0:T(8,128)(2,1)S(1)}, u32[]{:S(2)}, u32[]{:S(2)}) async-start(bf16[16,16,640]{2,1,0:T(8,128)(2,1)} %pad_maximum_fusion.11), calls=%async_computation.9 | async-start | bytes 655360 | tf_op jit(solution)/shard_map/all_to_all | solution.py:72
  215.2 14.2 %all-to-all-done.9 = bf16[16,16,640]{2,1,0:T(8,128)(2,1)S(1)} async-done(((bf16[16,16,640]{2,1,0:T(8,128)(2,1)}), bf16[16,16,640]{2,1,0:T(8,128)(2,1)S(1)}, u32[]{:S(2)}, u32[]{:S(2)}) %all-to-all-start.9) | async-done | bytes 327712 | tf_op jit(solution)/shard_map/all_to_all | solution.py:72
  229.9 1.9 collective-permute-start.1
  231.8 4.6 %collective-permute-done.1 = bf16[16,384]{1,0:T(8,128)(2,1)S(1)} collective-permute-done((bf16[16,384]{1,0:T(8,128)(2,1)S(1)}, bf16[16,384]{1,0:T(8,128)(2,1)S(1)}, u32[]{:S(2)}, u32[]{:S(2)}) %collective-permute-start.1) | collective-permute-done | bytes 12320 | tf_op jit(solution)/shard_map/ppermute | solution.py:231
  236.5 29.9 %all_to_all.79 = bf16[16,16,1152]{2,1,0:T(8,128)(2,1)S(1)} all-to-all(bf16[16,16,1152]{2,1,0:T(8,128)(2,1)S(1)} %broadcast_in_dim.295), channel_id=1, replica_groups=mesh['xh'=2,'core'=2,'z'=8,'y'=8,'xl'=2] {'xh','z'}, dimensions={0} | all-to-all | bytes 1179648 | tf_op jit(solution)/shard_map/all_to_all | solution.py:72
  266.4 2.2 all-gather
  268.7 2.5 all-gather.1
  272.7 0.9 pad_maximum_fusion.4
  273.6 4.6 %all-to-all-start.11 = ((bf16[16,16,1152]{2,1,0:T(8,128)(2,1)}), bf16[16,16,1152]{2,1,0:T(8,128)(2,1)S(1)}, u32[]{:S(2)}, u32[]{:S(2)}) async-start(bf16[16,16,1152]{2,1,0:T(8,128)(2,1)} %bitcast.34), calls=%async_computation.11 | async-start | bytes 1179648 | tf_op jit(solution)/shard_map/all_to_all | solution.py:72
  278.2 0.8 fusion.87
  279.0 18.5 %all-to-all-done.11 = bf16[16,16,1152]{2,1,0:T(8,128)(2,1)S(1)} async-done(((bf16[16,16,1152]{2,1,0:T(8,128)(2,1)}), bf16[16,16,1152]{2,1,0:T(8,128)(2,1)S(1)}, u32[]{:S(2)}, u32[]{:S(2)}) %all-to-all-start.11) | async-done | bytes 589856 | tf_op jit(solution)/shard_map/all_to_all | solution.py:72
  298.0 0.8 broadcast_in_dim.303
  298.8 3.6 %all-to-all-start.12 = ((bf16[16,16,896]{2,1,0:T(8,128)(2,1)}), bf16[16,16,896]{2,1,0:T(8,128)(2,1)S(1)}, u32[]{:S(2)}, u32[]{:S(2)}) async-start(bf16[16,16,896]{2,1,0:T(8,128)(2,1)} %broadcast_in_dim.303), calls=%async_computation.12 | async-start | bytes 917504 | tf_op jit(solution)/shard_map/all_to_all | solution.py:72
  302.3 0.7 dynamic-slice_convert_fusion.1
  303.2 14.3 %all-to-all-done.12 = bf16[16,16,896]{2,1,0:T(8,128)(2,1)S(1)} async-done(((bf16[16,16,896]{2,1,0:T(8,128)(2,1)}), bf16[16,16,896]{2,1,0:T(8,128)(2,1)S(1)}, u32[]{:S(2)}, u32[]{:S(2)}) %all-to-all-start.12) | async-done | bytes 458784 | tf_op jit(solution)/shard_map/all_to_all | solution.py:72
  317.5 0.5 convolution_convert_fusion.1
  318.2 4.1 %all_to_all.80 = bf16[2,128,896]{2,1,0:T(8,128)(2,1)S(1)} all-to-all(bf16[2,128,896]{2,1,0:T(8,128)(2,1)S(1)} %bitcast.100), channel_id=1, replica_groups=mesh['xh'=2,'core'=2,'z'=8,'y'=8,'xl'=2] {'core'}, dimensions={0} | all-to-all | bytes 917504 | tf_op jit(solution)/shard_map/all_to_all | solution.py:72
  322.3 0.7 pad_maximum_fusion.12
  323.0 4.5 %all-to-all-start.14 = ((bf16[16,8,1024]{2,1,0:T(8,128)(2,1)}), bf16[16,8,1024]{2,1,0:T(8,128)(2,1)S(1)}, u32[]{:S(2)}, u32[]{:S(2)}) async-start(bf16[16,8,1024]{2,1,0:T(8,128)(2,1)} %pad_maximum_fusion.12), calls=%async_computation.14 | async-start | bytes 524288 | tf_op jit(solution)/shard_map/all_to_all | solution.py:72
  327.5 0.6 fusion.88
  328.1 11.6 %all-to-all-done.14 = bf16[16,8,1024]{2,1,0:T(8,128)(2,1)S(1)} async-done(((bf16[16,8,1024]{2,1,0:T(8,128)(2,1)}), bf16[16,8,1024]{2,1,0:T(8,128)(2,1)S(1)}, u32[]{:S(2)}, u32[]{:S(2)}) %all-to-all-start.14) | async-done | bytes 262176 | tf_op jit(solution)/shard_map/all_to_all | solution.py:72
  340.0 0.7 fusion.89
  (170 shorter events, 9.2 us)
Async XLA Ops:
  0.6 15.5 %copy-start = (bf16[768,768]{1,0:T(8,128)(2,1)S(1)}, bf16[768,768]{1,0:T(8,128)(2,1)}, u32[]{:S(2)}) copy-start(bf16[768,768]{1,0:T(8,128)(2,1)} %param.9) | copy-start | bytes 3538948
  0.6 1.8 copy-start.10
  0.7 15.4 %copy-start.21 = (bf16[768]{0:T(1024)(128)(2,1)S(1)}, bf16[768]{0:T(1024)(128)(2,1)}, u32[]{:S(2)}) copy-start(bf16[768]{0:T(1024)(128)(2,1)} %param.11) | copy-start | bytes 4612
  0.7 58.2 %copy-start.24 = (pred[128]{0:T(512)(128)(4,1)}, pred[128]{0:T(512)(128)(4,1)S(1)}, u32[]{:S(2)}) copy-start(pred[128]{0:T(512)(128)(4,1)S(1)} %get-tuple-element.87) | copy-start | bytes 388
  0.7 58.2 %copy-start.26 = (pred[128]{0:T(512)(128)(4,1)}, pred[128]{0:T(512)(128)(4,1)S(1)}, u32[]{:S(2)}) copy-start(pred[128]{0:T(512)(128)(4,1)S(1)} %get-tuple-element.88) | copy-start | bytes 388
  0.7 58.1 %copy-start.28 = (pred[128]{0:T(512)(128)(4,1)}, pred[128]{0:T(512)(128)(4,1)S(1)}, u32[]{:S(2)}) copy-start(pred[128]{0:T(512)(128)(4,1)S(1)} %get-tuple-element.86) | copy-start | bytes 388
  0.7 104.4 %copy-start.15 = (pred[128]{0:T(512)(128)(4,1)}, pred[128]{0:T(512)(128)(4,1)S(1)}, u32[]{:S(2)}) copy-start(pred[128]{0:T(512)(128)(4,1)S(1)} %get-tuple-element.85) | copy-start | bytes 388
  0.7 104.4 %copy-start.17 = (pred[128]{0:T(512)(128)(4,1)}, pred[128]{0:T(512)(128)(4,1)S(1)}, u32[]{:S(2)}) copy-start(pred[128]{0:T(512)(128)(4,1)S(1)} %get-tuple-element.83) | copy-start | bytes 388
  0.8 104.4 %copy-start.19 = (pred[128]{0:T(512)(128)(4,1)}, pred[128]{0:T(512)(128)(4,1)S(1)}, u32[]{:S(2)}) copy-start(pred[128]{0:T(512)(128)(4,1)S(1)} %get-tuple-element.84) | copy-start | bytes 388
  3.6 24.5 %all-to-all-start = ((bf16[16,8,1152]{2,1,0:T(8,128)(2,1)}), bf16[16,8,1152]{2,1,0:T(8,128)(2,1)S(1)}, u32[]{:S(2)}, u32[]{:S(2)}) async-start(bf16[16,8,1152]{2,1,0:T(8,128)(2,1)} %broadcast_in_dim.262), calls=%async_computation | async-start | bytes 589824 | tf_op jit(solution)/shard_map/all_to_all | solution.py:72
  30.3 0.8 copy-start.2
  30.4 1.3 copy-start.4
  31.7 8.1 %copy-start.1 = (bf16[768,768]{1,0:T(8,128)(2,1)S(1)}, bf16[768,768]{1,0:T(8,128)(2,1)}, u32[]{:S(2)}) copy-start(bf16[768,768]{1,0:T(8,128)(2,1)} %param.10) | copy-start | bytes 3538948
  32.6 25.2 %all-to-all-start.1 = ((bf16[16,16,1024]{2,1,0:T(8,128)(2,1)}), bf16[16,16,1024]{2,1,0:T(8,128)(2,1)S(1)}, u32[]{:S(2)}, u32[]{:S(2)}) async-start(bf16[16,16,1024]{2,1,0:T(8,128)(2,1)} %pad_maximum_fusion.5), calls=%async_computation.1 | async-start | bytes 1048576 | tf_op jit(solution)/shard_map/all_to_all | solution.py:72
  57.8 0.8 copy-start.3
  58.4 21.5 %copy-start.30 = (f32[16]{0:T(128)}, f32[16]{0:T(128)S(1)}, u32[]{:S(2)}) copy-start(f32[16]{0:T(128)S(1)} %get-tuple-element.30) | copy-start | bytes 196
  58.7 0.6 copy-start.8
  85.5 6.3 %copy-start.5 = (bf16[2,2,64,1152]{3,2,1,0:T(8,128)(2,1)S(1)}, bf16[2,2,64,1152]{3,2,1,0:T(8,128)(2,1)}, u32[]{:S(2)}) copy-start(bf16[2,2,64,1152]{3,2,1,0:T(8,128)(2,1)} %copy-done.4) | copy-start | bytes 1769476
  85.5 26.1 %copy-start.13 = (bf16[1,16,384]{2,1,0:T(8,128)(2,1)S(1)}, bf16[1,16,384]{2,1,0:T(8,128)(2,1)}, u32[]{:S(2)}) copy-start(bf16[1,16,384]{2,1,0:T(8,128)(2,1)} %param.15) | copy-start | bytes 36868
  86.3 18.5 %all-to-all-start.4 = ((bf16[16,16,640]{2,1,0:T(8,128)(2,1)}), bf16[16,16,640]{2,1,0:T(8,128)(2,1)S(1)}, u32[]{:S(2)}, u32[]{:S(2)}) async-start(bf16[16,16,640]{2,1,0:T(8,128)(2,1)} %pad_maximum_fusion.10), calls=%async_computation.4 | async-start | bytes 655360 | tf_op jit(solution)/shard_map/all_to_all | solution.py:72
  106.0 5.1 %collective-permute-start = (bf16[16,512]{1,0:T(8,128)(2,1)S(1)}, bf16[16,512]{1,0:T(8,128)(2,1)S(1)}, u32[]{:S(2)}, u32[]{:S(2)}) collective-permute-start(bf16[16,512]{1,0:T(8,128)(2,1)S(1)} %pad_maximum_fusion.18), channel_id=1, source_target_pairs={{0,0},{1,32},{2,64},{3,96},{4,128},{5,160},{6,192},{7,224},{8,256}... | collective-permute-start | bytes 49160 | tf_op jit(solution)/shard_map/ppermute | solution.py:179
  111.1 0.6 copy-start.11
  112.5 29.7 %copy-start.6 = (bf16[384,1536]{1,0:T(8,128)(2,1)S(1)}, bf16[384,1536]{1,0:T(8,128)(2,1)}, u32[]{:S(2)}) copy-start(bf16[384,1536]{1,0:T(8,128)(2,1)} %param.12) | copy-start | bytes 3538948
  112.5 27.1 %all-to-all-start.5 = ((bf16[16,16,896]{2,1,0:T(8,128)(2,1)}), bf16[16,16,896]{2,1,0:T(8,128)(2,1)}, u32[]{:S(2)}, u32[]{:S(2)}) async-start(bf16[16,16,896]{2,1,0:T(8,128)(2,1)} %broadcast_in_dim.281), calls=%async_computation.5 | async-start | bytes 917504 | tf_op jit(solution)/shard_map/all_to_all | solution.py:72
  139.6 2.6 copy-start.22
  142.2 2.8 copy-start.32
  154.3 31.8 %all-to-all-start.7 = ((bf16[16,16,1792]{2,1,0:T(8,128)(2,1)}), bf16[16,16,1792]{2,1,0:T(8,128)(2,1)S(1)}, u32[]{:S(2)}, u32[]{:S(2)}) async-start(bf16[16,16,1792]{2,1,0:T(8,128)(2,1)} %pad_maximum_fusion.3), calls=%async_computation.7 | async-start | bytes 1835008 | tf_op jit(solution)/shard_map/all_to_all | solution.py:72
  160.8 25.8 %copy-start.16 = (pred[128]{0:T(512)(128)(4,1)S(1)}, pred[128]{0:T(512)(128)(4,1)}, u32[]{:S(2)}) copy-start(pred[128]{0:T(512)(128)(4,1)} %copy-done.15) | copy-start | bytes 388
  160.8 25.8 %copy-start.18 = (pred[128]{0:T(512)(128)(4,1)S(1)}, pred[128]{0:T(512)(128)(4,1)}, u32[]{:S(2)}) copy-start(pred[128]{0:T(512)(128)(4,1)} %copy-done.17) | copy-start | bytes 388
  160.9 25.8 %copy-start.20 = (pred[128]{0:T(512)(128)(4,1)S(1)}, pred[128]{0:T(512)(128)(4,1)}, u32[]{:S(2)}) copy-start(pred[128]{0:T(512)(128)(4,1)} %copy-done.19) | copy-start | bytes 388
  160.9 25.8 %copy-start.25 = (pred[128]{0:T(512)(128)(4,1)S(1)}, pred[128]{0:T(512)(128)(4,1)}, u32[]{:S(2)}) copy-start(pred[128]{0:T(512)(128)(4,1)} %copy-done.24) | copy-start | bytes 388
  160.9 25.8 %copy-start.27 = (pred[128]{0:T(512)(128)(4,1)S(1)}, pred[128]{0:T(512)(128)(4,1)}, u32[]{:S(2)}) copy-start(pred[128]{0:T(512)(128)(4,1)} %copy-done.26) | copy-start | bytes 388
  160.9 25.8 %copy-start.29 = (pred[128]{0:T(512)(128)(4,1)S(1)}, pred[128]{0:T(512)(128)(4,1)}, u32[]{:S(2)}) copy-start(pred[128]{0:T(512)(128)(4,1)} %copy-done.28) | copy-start | bytes 388
  186.9 23.0 %copy-start.7 = (bf16[384,1536]{1,0:T(8,128)(2,1)S(1)}, bf16[384,1536]{1,0:T(8,128)(2,1)}, u32[]{:S(2)}) copy-start(bf16[384,1536]{1,0:T(8,128)(2,1)} %param.12) | copy-start | bytes 3538948
  210.3 4.7 %copy-start.12 = (bf16[16,512]{1,0:T(8,128)(2,1)S(1)}, bf16[16,512]{1,0:T(8,128)(2,1)}, u32[]{:S(2)}) copy-start(bf16[16,512]{1,0:T(8,128)(2,1)} %copy-done.11) | copy-start | bytes 49156
  210.7 19.1 %copy-start.14 = (bf16[1,16,384]{2,1,0:T(8,128)(2,1)S(1)}, bf16[1,16,384]{2,1,0:T(8,128)(2,1)}, u32[]{:S(2)}) copy-start(bf16[1,16,384]{2,1,0:T(8,128)(2,1)} %param.15) | copy-start | bytes 36868
  210.7 19.1 %copy-start.23 = (f32[384]{0:T(512)S(1)}, f32[384]{0:T(512)}, u32[]{:S(2)}) copy-start(f32[384]{0:T(512)} %convert_element_type.230) | copy-start | bytes 4612
  211.4 17.9 %all-to-all-start.9 = ((bf16[16,16,640]{2,1,0:T(8,128)(2,1)}), bf16[16,16,640]{2,1,0:T(8,128)(2,1)S(1)}, u32[]{:S(2)}, u32[]{:S(2)}) async-start(bf16[16,16,640]{2,1,0:T(8,128)(2,1)} %pad_maximum_fusion.11), calls=%async_computation.9 | async-start | bytes 655360 | tf_op jit(solution)/shard_map/all_to_all | solution.py:72
  229.9 6.5 %collective-permute-start.1 = (bf16[16,384]{1,0:T(8,128)(2,1)S(1)}, bf16[16,384]{1,0:T(8,128)(2,1)S(1)}, u32[]{:S(2)}, u32[]{:S(2)}) collective-permute-start(bf16[16,384]{1,0:T(8,128)(2,1)S(1)} %fusion.74), channel_id=1, source_target_pairs={{0,0},{32,1},{64,2},{96,3},{128,4},{160,5},{192,6},{224,7},{256,8}... | collective-permute-start | bytes 36872 | tf_op jit(solution)/shard_map/ppermute | solution.py:231
  266.4 4.8 %copy-start.33 = (bf16[1536,384]{1,0:T(8,128)(2,1)S(1)}, bf16[1536,384]{1,0:T(8,128)(2,1)}, u32[]{:S(2)}) copy-start(bf16[1536,384]{1,0:T(8,128)(2,1)} %param.13) | copy-start | bytes 3538948
  273.6 24.0 %copy-start.9 = (f32[16,768]{1,0:T(8,128)S(1)}, f32[16,768]{1,0:T(8,128)}, u32[]{:S(2)}) copy-start(f32[16,768]{1,0:T(8,128)} %copy-done.8) | copy-start | bytes 147460
  273.6 24.0 %copy-start.31 = (f32[16]{0:T(128)S(1)}, f32[16]{0:T(128)}, u32[]{:S(2)}) copy-start(f32[16]{0:T(128)} %copy-done.30) | copy-start | bytes 196
  273.6 23.9 %all-to-all-start.11 = ((bf16[16,16,1152]{2,1,0:T(8,128)(2,1)}), bf16[16,16,1152]{2,1,0:T(8,128)(2,1)S(1)}, u32[]{:S(2)}, u32[]{:S(2)}) async-start(bf16[16,16,1152]{2,1,0:T(8,128)(2,1)} %bitcast.34), calls=%async_computation.11 | async-start | bytes 1179648 | tf_op jit(solution)/shard_map/all_to_all | solution.py:72
  298.8 18.8 %all-to-all-start.12 = ((bf16[16,16,896]{2,1,0:T(8,128)(2,1)}), bf16[16,16,896]{2,1,0:T(8,128)(2,1)S(1)}, u32[]{:S(2)}, u32[]{:S(2)}) async-start(bf16[16,16,896]{2,1,0:T(8,128)(2,1)} %broadcast_in_dim.303), calls=%async_computation.12 | async-start | bytes 917504 | tf_op jit(solution)/shard_map/all_to_all | solution.py:72
  323.0 16.7 %all-to-all-start.14 = ((bf16[16,8,1024]{2,1,0:T(8,128)(2,1)}), bf16[16,8,1024]{2,1,0:T(8,128)(2,1)S(1)}, u32[]{:S(2)}, u32[]{:S(2)}) async-start(bf16[16,8,1024]{2,1,0:T(8,128)(2,1)} %pad_maximum_fusion.12), calls=%async_computation.14 | async-start | bytes 524288 | tf_op jit(solution)/shard_map/all_to_all | solution.py:72

commit v3 on v2

--- a/solution.py
+++ b/solution.py
@@ -53,9 +53,9 @@
     return high, mid, rest - mid
 
 
-def pack(columns):
+def pack(columns, first=0):
     rows = columns[0].shape[0]
-    lane = lax.broadcasted_iota(jnp.int32, (rows, LANES), 1)
+    lane = lax.broadcasted_iota(jnp.int32, (rows, LANES), 1) - first
     block = jnp.zeros((rows, LANES), F32)
     for number, column in enumerate(columns):
         for part, piece in enumerate(split3(column)):
@@ -66,6 +66,10 @@
 def unpack(floats, number):
     at = 3 * number
     return floats[..., at : at + 1] + floats[..., at + 1 : at + 2] + floats[..., at + 2 : at + 3]
+
+
+def unpack_pair(floats, number):
+    return unpack(floats, number) + unpack(floats[..., 64:], number)
 
 
 def exchange(blocks, axis):
@@ -110,19 +114,16 @@
 
     u_a = dot(jnp.broadcast_to(gain_first[None], (8, 768)), up_first)[0].astype(BF)
     u_b = dot(jnp.broadcast_to(gain_second[None], (8, 384)), up_second)[0].astype(BF)
-    d_high, d_mid, _ = split3(contract_cols(jnp.ones((8, 768), BF), down_first)[0])
+    down_sum = contract_cols(jnp.ones((8, 768), BF), down_first)[0].astype(BF)
+    sums_a = jnp.concatenate([tile_rows(u_a, 8), tile_rows(down_sum, 8)], axis=0)
 
     floats = x_own.astype(F32)
     centre = jnp.sum(floats, axis=1, keepdims=True) / 768
     spread = jnp.sum((floats - centre) * (floats - centre), axis=1, keepdims=True)
-    u_b = tile_rows(u_b, 16)
-    message = jnp.concatenate([x_own, pack([centre, spread]), u_b[:8], u_b[8:]], axis=1)
+    message = jnp.concatenate([x_own, pack([centre, spread])], axis=1)
     got = both_cores(send_all(message, ROW))
-    gain_up_b = jnp.sum(got[:, :, 896:].reshape(32, 8, 256).astype(F32), axis=0)
-    gain_up_b = jnp.concatenate([gain_up_b[:, :128], gain_up_b[:4, 128:]], axis=0).reshape(2, 768)
-    gain_up_b = jnp.where(core == 0, gain_up_b[:1], gain_up_b[1:])
-    x_all = jnp.transpose(got.reshape(2, 2, 64, 1152), (1, 0, 2, 3)).reshape(256, 1152)
-    x_cols = x_all[:, 768:896]
+    x_all = jnp.transpose(got.reshape(2, 2, 64, 896), (1, 0, 2, 3)).reshape(256, 896)
+    x_cols = x_all[:, 768:]
     x_all = x_all[:, :768]
 
     centred = (x_all.astype(F32) - unpack(x_cols.astype(F32), 0)) * gain_a
@@ -131,7 +132,7 @@
         [
             part.reshape(16, 16, 768),
             x_cols.reshape(16, 16, LANES),
-            jnp.broadcast_to(tile_rows(u_a, 16)[None], (16, 16, LANES)),
+            jnp.broadcast_to(sums_a[None], (16, 16, LANES)),
         ],
         axis=2,
     )
@@ -144,23 +145,15 @@
     rstd_a = lax.rsqrt(var_a + EPS)
     u_all = got[:, :6, 896:].reshape(16, 1, 768).astype(F32)
     gain_up_a = jnp.sum(u_all, axis=0)
+    down_sum = jnp.sum(got[:, 8:14, 896:].astype(F32), axis=0).reshape(1, 768)
     hidden_a = rstd_a * jnp.sum(got[:, :, :768].astype(F32) + off * u_all, axis=0)
-    message = jnp.concatenate(
-        [
-            gelu_value(hidden_a).astype(BF),
-            pack([mean_a, rstd_a]),
-            jnp.concatenate([tile_rows(d_high, 8), tile_rows(d_mid, 8)], axis=0).astype(BF),
-        ],
-        axis=1,
-    )
-    got = send_all(message, DP)
-    stats_a = got[:, 768:896]
-    sums = jnp.sum(got[:, 896:].reshape(16, 2, 8, LANES).astype(F32), axis=(0, 1))
-    down_sum = sums[:6].reshape(1, 768)
+    active = gelu_value(hidden_a).astype(BF)
+    got = send_all(jnp.concatenate([active, pack([mean_a, rstd_a])], axis=1), DP)
+    stats_a = got[:, 768:]
     active = got[:, :768]
     part = dot(active, down_first).astype(BF)
     shift = row_dot(active.astype(F32), down_sum) + unpack(stats_a.astype(F32), 0) * (D / 32)
-    cols = pack([shift])
+    cols = pack([shift], 64 * core)
     message = jnp.stack(
         [
             jnp.concatenate([part[:, :384], cols], axis=1),
@@ -168,21 +161,20 @@
         ]
     )
     got = exchange(message, "core")
-    part = jnp.sum(got[:, :, :384].astype(F32), axis=0).astype(BF)
-    message = jnp.concatenate([part, got[0, :, 384:], got[1, :, 384:]], axis=1)
-    sums = jnp.sum(exchange(message.reshape(16, 16, 640), ROW).astype(F32), axis=0)
-    mean_b = (unpack(sums[:, 384:512], 0) + unpack(sums[:, 512:], 0)) / D
+    part = jnp.sum(got.astype(F32), axis=0).astype(BF)
+    sums = jnp.sum(exchange(part.reshape(16, 16, 512), ROW).astype(F32), axis=0)
+    centre = unpack_pair(sums[:, 384:], 0) / D
     rows = lax.dynamic_slice_in_dim(x_all, chunk * 16, 16, 0)
     rows = jnp.where(core == 0, rows[:, :384], rows[:, 384:]).astype(F32)
     middle = (rows + sums[:, :384]).astype(BF)
 
-    crossed = lax.ppermute(jnp.concatenate([middle, pack([mean_b])], axis=1), NAMES, crossing())
+    crossed = lax.ppermute(jnp.concatenate([middle, pack([centre])], axis=1), NAMES, crossing())
     middle_own = crossed[:, :384].astype(F32)
-    mean_own = unpack(crossed[:, 384:].astype(F32), 0)
     got = send_all(jnp.concatenate([crossed, cot_own], axis=1), DP)
     cot_all = got[:, 512:]
     centred = got[:, :384].astype(F32) - unpack(got[:, 384:512].astype(F32), 0)
-    cols = pack([row_dot(centred * centred, jnp.ones((1, 384), F32))])
+    ones = jnp.ones((1, 384), F32)
+    cols = pack([row_dot(centred * centred, ones), row_dot(centred, ones)], 64 * core)
     centred = (centred * gain_b).astype(BF)
     message = jnp.stack(
         [
@@ -191,6 +183,7 @@
                     dot(centred, up_second[:, at : at + 768]).astype(BF),
                     contract_cols(cot_all, down_second[at : at + 768]).astype(BF),
                     cols,
+                    jnp.tile(tile_rows(u_b[at : at + 768], 16), (16, 1)),
                 ],
                 axis=1,
             )
@@ -198,12 +191,12 @@
         ]
     )
     got = exchange(message, "core")
-    part = jnp.sum(got[:, :, :1536].astype(F32), axis=0).astype(BF)
-    message = jnp.concatenate([part, got[0, :, 1536:], got[1, :, 1536:]], axis=1)
-    sums = jnp.sum(exchange(message.reshape(16, 16, 1792), ROW).astype(F32), axis=0)
-    spread = unpack(sums[:, 1536:1664], 0) + unpack(sums[:, 1664:], 0)
-    rstd_b = lax.rsqrt(spread / D + EPS)
-    hidden_b = sums[:, :768] * rstd_b
+    part = jnp.sum(got.astype(F32), axis=0).astype(BF)
+    sums = jnp.sum(exchange(part.reshape(16, 16, 1792), ROW).astype(F32), axis=0)
+    gain_up_b = sums[:6, 1664:].reshape(1, 768)
+    off = unpack_pair(sums[:, 1536:1664], 1) / D
+    rstd_b = lax.rsqrt(unpack_pair(sums[:, 1536:1664], 0) / D - off * off + EPS)
+    hidden_b = (sums[:, :768] - off * gain_up_b) * rstd_b
     active_b = gelu_value(hidden_b).astype(BF)
     d_hid_b = (sums[:, 768:1536] * gelu_slope(hidden_b)).astype(BF)
     floats = d_hid_b.astype(F32)
@@ -212,17 +205,26 @@
             jnp.sum(floats * gain_up_b, axis=1, keepdims=True),
             jnp.sum(floats * hidden_b, axis=1, keepdims=True),
             rstd_b,
-        ]
-    )
-    got = both_cores(send_all(jnp.concatenate([d_hid_b, cols], axis=1), ROW))
+            off,
+        ],
+        64 * core,
+    )
+    got = send_all(jnp.concatenate([d_hid_b, cols, active_b], axis=1), ROW)
+    active = both_cores(got[:, 896:])
+    got = both_cores(got[:, :896])
     part = contract_cols(got[0, :, :768], up_second[:, :768])
     part = part + contract_cols(got[1, :, :768], up_second[:, 768:])
-    message = jnp.concatenate([part.astype(BF), got[0, :, 768:], got[1, :, 768:]], axis=1)
-    got = exchange(message.reshape(16, 16, 640), DP)
+    cols = got[0, :, 768:] + got[1, :, 768:]
+    part_b = dot(active[0], down_second[:768]) + dot(active[1], down_second[768:])
+    message = jnp.concatenate([part.astype(BF), cols, part_b.astype(BF)], axis=1)
+    got = exchange(message.reshape(16, 16, 896), DP)
     sums = jnp.sum(got.astype(F32), axis=0)
-    sum_one = unpack(sums[:, 384:512], 0) + unpack(sums[:, 512:], 0)
-    sum_two = unpack(sums[:, 384:512], 1) + unpack(sums[:, 512:], 1)
-    rstd_own = unpack(got[0, :, 384:512].astype(F32), 2)
+    residual_out = (middle_own + sums[:, 512:]).astype(BF)
+    sum_one = unpack_pair(sums[:, 384:512], 0)
+    sum_two = unpack_pair(sums[:, 384:512], 1)
+    cols = got[0, :, 384:512].astype(F32)
+    rstd_own = unpack(cols, 2)
+    mean_own = unpack(crossed[:, 384:].astype(F32), 0) + unpack(cols, 3)
     nhat_b = (middle_own - mean_own) * rstd_own
     grad_own = cot_own.astype(F32) + rstd_own * (
         sums[:, :384] * gain_b - sum_one / D - nhat_b * (sum_two / D)
@@ -231,32 +233,27 @@
     crossed = lax.ppermute(
         grad_own.astype(BF), NAMES, [(target, source) for source, target in crossing()]
     )
-    got = send_all(jnp.concatenate([crossed, active_b], axis=1), ROW)
-    grad_all = both_cores(got[:, :384])
-    active_all = both_cores(got[:, 384:])
+    grad_all = both_cores(send_all(crossed, ROW))
     part = contract_cols(grad_all[0], down_first[:, :384])
     part = part + contract_cols(grad_all[1], down_first[:, 384:])
-    part_b = dot(active_all[0], down_second[:768]) + dot(active_all[1], down_second[768:])
-    message = jnp.concatenate([part.astype(BF), part_b.astype(BF)], axis=1)
-    sums = jnp.sum(exchange(message.reshape(16, 16, 1152), DP).astype(F32), axis=0)
-    residual_out = (middle_own + sums[:, 768:]).astype(BF)
-    d_hid_a = (sums[:, :768] * gelu_slope(hidden_a)).astype(BF)
+    sums = jnp.sum(exchange(part.astype(BF).reshape(16, 16, 768), DP).astype(F32), axis=0)
+    d_hid_a = (sums * gelu_slope(hidden_a)).astype(BF)
     floats = d_hid_a.astype(F32)
     cols = pack(
         [
             jnp.sum(floats * gain_up_a, axis=1, keepdims=True),
             jnp.sum(floats * hidden_a, axis=1, keepdims=True),
-        ]
+        ],
+        64 * core,
     )
     got = send_all(jnp.concatenate([d_hid_a, cols], axis=1), DP)
     part = contract_cols(got[:, :768], up_first).astype(BF)
     message = jnp.concatenate([part, got[:, 768:]], axis=1).reshape(2, 2, 64, 896)
     got = exchange(jnp.transpose(message, (1, 0, 2, 3)).reshape(2, 128, 896), "core")
-    part = jnp.sum(got[:, :, :768].astype(F32), axis=0).astype(BF)
-    message = jnp.concatenate([part, got[0, :, 768:], got[1, :, 768:]], axis=1)
-    sums = jnp.sum(exchange(message.reshape(16, 8, 1024), ROW).astype(F32), axis=0)
-    sum_one = unpack(sums[:, 768:896], 0) + unpack(sums[:, 896:], 0)
-    sum_two = unpack(sums[:, 768:896], 1) + unpack(sums[:, 896:], 1)
+    part = jnp.sum(got.astype(F32), axis=0).astype(BF)
+    sums = jnp.sum(exchange(part.reshape(16, 8, 896), ROW).astype(F32), axis=0)
+    sum_one = unpack_pair(sums[:, 768:], 0)
+    sum_two = unpack_pair(sums[:, 768:], 1)
     stats = lax.dynamic_slice_in_dim(stats_a, own_row, 8, 0).astype(F32)
     rstd = unpack(stats, 1)
     nhat_a = (x_own.astype(F32) - unpack(stats, 0)) * rstd

time: 342 us -> 331 us (0.968)
  waiting for transfers between devices: 146 us -> 139 us
  blocking collectives: 93.1 us -> 100 us
  starting transfers between devices: 63 us -> 57.1 us
  matrix products: 13.5 us -> 9.98 us
    all_to_all x9, waiting for transfers between devices: 139 us -> 131 us  [exchange(): return lax.all_to_all(blocks, axis, 0, 0)]
    all_to_all x6, blocking collectives: 83.6 us -> 90.8 us  [exchange(): return lax.all_to_all(blocks, axis, 0, 0)]
    all_to_all x9, starting transfers between devices: 59.2 us -> 53.1 us  [exchange(): return lax.all_to_all(blocks, axis, 0, 0)]
where the time goes in v3:
time: 331 us; the launch traced here: 329 us
  waiting for transfers between devices  139 us (42%)
  blocking collectives  100 us (30%)
  starting transfers between devices  57.1 us (17%)
  other arithmetic  16.8 us (5%)
  matrix products  9.98 us (3%)
  local copies, waits for them, and re-layouts  4.93 us (1%)
    all_to_all x9, waiting for transfers between devices, exchange(): return lax.all_to_all(blocks, axis, 0, 0)  131 us
    all_to_all x6, blocking collectives, exchange(): return lax.all_to_all(blocks, axis, 0, 0)  90.8 us
    all_to_all x9, starting transfers between devices, exchange(): return lax.all_to_all(blocks, axis, 0, 0)  53.1 us
    all_gather x4, blocking collectives, both_cores(): return lax.all_gather(values, 'core', axis=0, tiled=False)  9.16 us
  transfers between devices with their start and end apart: 11, of which 11 were waited for; matrix products, arithmetic and copies ran while one was open for 2% of the time, Pallas kernels for 0%

profile of v3, /device:TPU:64, one launch (start us, length us, event | category | flops | bytes accessed | tf_op | source)
XLA Modules:
  0.0 329.4 jit_solution(7939900213504825559)
XLA Ops:
  0.7 1.0 convert_reduce_fusion.6
  1.7 0.9 fusion.82
  2.7 0.7 pad_maximum_fusion.14
  3.4 0.7 broadcast_in_dim.280
  4.1 12.4 %all-to-all-start = ((bf16[16,8,896]{2,1,0:T(8,128)(2,1)}), bf16[16,8,896]{2,1,0:T(8,128)(2,1)S(1)}, u32[]{:S(2)}, u32[]{:S(2)}) async-start(bf16[16,8,896]{2,1,0:T(8,128)(2,1)} %broadcast_in_dim.280), calls=%async_computation | async-start | bytes 458752 | tf_op jit(solution)/shard_map/all_to_all | solution.py:76
  16.5 0.7 convert_element_type.200
  17.2 1.0 fusion.119
  18.2 0.4 fusion.117
  18.7 8.7 %all-to-all-done = bf16[16,8,896]{2,1,0:T(8,128)(2,1)S(1)} async-done(((bf16[16,8,896]{2,1,0:T(8,128)(2,1)}), bf16[16,8,896]{2,1,0:T(8,128)(2,1)S(1)}, u32[]{:S(2)}, u32[]{:S(2)}) %all-to-all-start) | async-done | bytes 229408 | tf_op jit(solution)/shard_map/all_to_all | solution.py:76
  27.4 2.1 all_gather.18
  29.8 0.5 convolution_convert_fusion.3
  30.4 25.0 %all_to_all.75 = bf16[16,16,1024]{2,1,0:T(8,128)(2,1)S(1)} all-to-all(bf16[16,16,1024]{2,1,0:T(8,128)(2,1)S(1)} %pad_maximum_fusion.3), channel_id=1, replica_groups=mesh['xh'=2,'core'=2,'z'=8,'y'=8,'xl'=2] {'y','xl'}, dimensions={0} | all-to-all | bytes 1048576 | tf_op jit(solution)/shard_map/all_to_all | solution.py:76
  55.4 0.4 copy.165
  56.7 0.8 broadcast_in_dim.290
  57.6 3.6 %all-to-all-start.2 = ((bf16[16,16,896]{2,1,0:T(8,128)(2,1)}), bf16[16,16,896]{2,1,0:T(8,128)(2,1)S(1)}, u32[]{:S(2)}, u32[]{:S(2)}) async-start(bf16[16,16,896]{2,1,0:T(8,128)(2,1)} %broadcast_in_dim.290), calls=%async_computation.2 | async-start | bytes 917504 | tf_op jit(solution)/shard_map/all_to_all | solution.py:76
  61.1 0.5 fusion.142
  61.7 0.6 fusion.140
  62.3 13.9 %all-to-all-done.2 = bf16[16,16,896]{2,1,0:T(8,128)(2,1)S(1)} async-done(((bf16[16,16,896]{2,1,0:T(8,128)(2,1)}), bf16[16,16,896]{2,1,0:T(8,128)(2,1)S(1)}, u32[]{:S(2)}, u32[]{:S(2)}) %all-to-all-start.2) | async-done | bytes 458784 | tf_op jit(solution)/shard_map/all_to_all | solution.py:76
  76.2 0.6 fusion.153
  76.9 0.5 convolution_convert_fusion.2
  77.7 0.5 fusion.40
  78.3 4.3 %all_to_all.76 = bf16[2,256,512]{2,1,0:T(8,128)(2,1)S(1)} all-to-all(bf16[2,256,512]{2,1,0:T(8,128)(2,1)S(1)} %pad_maximum_fusion.4), channel_id=1, replica_groups=mesh['xh'=2,'core'=2,'z'=8,'y'=8,'xl'=2] {'core'}, dimensions={0} | all-to-all | bytes 1048576 | tf_op jit(solution)/shard_map/all_to_all | solution.py:76
  82.6 0.8 reduce_sum.196
  83.4 5.2 %all-to-all-start.4 = ((bf16[16,16,512]{2,1,0:T(8,128)(2,1)}), bf16[16,16,512]{2,1,0:T(8,128)(2,1)S(1)}, u32[]{:S(2)}, u32[]{:S(2)}) async-start(bf16[16,16,512]{2,1,0:T(8,128)(2,1)} %bitcast.12), calls=%async_computation.4 | async-start | bytes 524288 | tf_op jit(solution)/shard_map/all_to_all | solution.py:76
  88.6 11.8 %all-to-all-done.4 = bf16[16,16,512]{2,1,0:T(8,128)(2,1)S(1)} async-done(((bf16[16,16,512]{2,1,0:T(8,128)(2,1)}), bf16[16,16,512]{2,1,0:T(8,128)(2,1)S(1)}, u32[]{:S(2)}, u32[]{:S(2)}) %all-to-all-start.4) | async-done | bytes 262176 | tf_op jit(solution)/shard_map/all_to_all | solution.py:76
  100.9 1.9 collective-permute-start
  102.8 3.2 collective-permute-done
  106.0 0.7 pad_maximum_fusion.11
  106.7 0.8 broadcast_in_dim.299
  107.5 11.1 %all-to-all-start.5 = ((bf16[16,16,896]{2,1,0:T(8,128)(2,1)}), bf16[16,16,896]{2,1,0:T(8,128)(2,1)S(1)}, u32[]{:S(2)}, u32[]{:S(2)}) async-start(bf16[16,16,896]{2,1,0:T(8,128)(2,1)} %broadcast_in_dim.299), calls=%async_computation.5 | async-start | bytes 917504 | tf_op jit(solution)/shard_map/all_to_all | solution.py:76
  118.7 0.7 convert_element_type.221
  119.4 0.9 convolution_convert_fusion
  120.4 14.1 %all-to-all-done.5 = bf16[16,16,896]{2,1,0:T(8,128)(2,1)S(1)} async-done(((bf16[16,16,896]{2,1,0:T(8,128)(2,1)}), bf16[16,16,896]{2,1,0:T(8,128)(2,1)S(1)}, u32[]{:S(2)}, u32[]{:S(2)}) %all-to-all-start.5) | async-done | bytes 458784 | tf_op jit(solution)/shard_map/all_to_all | solution.py:76
  134.8 0.5 fusion.23
  136.2 0.4 copy-done.32
  137.4 0.5 fusion.46
  138.3 5.2 %all_to_all.77 = bf16[2,256,1792]{2,1,0:T(8,128)(2,1)S(1)} all-to-all(bf16[2,256,1792]{2,1,0:T(8,128)(2,1)S(1)} %pad_maximum_fusion), channel_id=1, replica_groups=mesh['xh'=2,'core'=2,'z'=8,'y'=8,'xl'=2] {'core'}, dimensions={0} | all-to-all | bytes 3670016 | tf_op jit(solution)/shard_map/all_to_all | solution.py:76
  143.6 1.5 reduce_sum.198
  145.1 6.0 %all-to-all-start.7 = ((bf16[16,16,1792]{2,1,0:T(8,128)(2,1)}), bf16[16,16,1792]{2,1,0:T(8,128)(2,1)S(1)}, u32[]{:S(2)}, u32[]{:S(2)}) async-start(bf16[16,16,1792]{2,1,0:T(8,128)(2,1)} %bitcast.85), calls=%async_computation.7 | async-start | bytes 1835008 | tf_op jit(solution)/shard_map/all_to_all | solution.py:76
  151.1 25.2 %all-to-all-done.7 = bf16[16,16,1792]{2,1,0:T(8,128)(2,1)S(1)} async-done(((bf16[16,16,1792]{2,1,0:T(8,128)(2,1)}), bf16[16,16,1792]{2,1,0:T(8,128)(2,1)S(1)}, u32[]{:S(2)}, u32[]{:S(2)}) %all-to-all-start.7) | async-done | bytes 917536 | tf_op jit(solution)/shard_map/all_to_all | solution.py:76
  177.4 29.5 %all_to_all.78 = bf16[16,16,1664]{2,1,0:T(8,128)(2,1)S(1)} all-to-all(bf16[16,16,1664]{2,1,0:T(8,128)(2,1)S(1)} %broadcast_in_dim.319), channel_id=1, replica_groups=mesh['xh'=2,'core'=2,'z'=8,'y'=8,'xl'=2] {'xh','z'}, dimensions={0} | all-to-all | bytes 1703936 | tf_op jit(solution)/shard_map/all_to_all | solution.py:76
  207.0 2.6 all-gather
  210.0 2.4 all-gather.1
  213.5 0.8 pad_maximum_fusion.5
  214.3 3.6 %all-to-all-start.9 = ((bf16[16,16,896]{2,1,0:T(8,128)(2,1)}), bf16[16,16,896]{2,1,0:T(8,128)(2,1)S(1)}, u32[]{:S(2)}, u32[]{:S(2)}) async-start(bf16[16,16,896]{2,1,0:T(8,128)(2,1)} %bitcast.26), calls=%async_computation.9 | async-start | bytes 917504 | tf_op jit(solution)/shard_map/all_to_all | solution.py:76
  217.9 17.1 %all-to-all-done.9 = bf16[16,16,896]{2,1,0:T(8,128)(2,1)S(1)} async-done(((bf16[16,16,896]{2,1,0:T(8,128)(2,1)}), bf16[16,16,896]{2,1,0:T(8,128)(2,1)S(1)}, u32[]{:S(2)}, u32[]{:S(2)}) %all-to-all-start.9) | async-done | bytes 458784 | tf_op jit(solution)/shard_map/all_to_all | solution.py:76
  235.5 0.6 fusion.80
  236.1 2.1 collective-permute-start.1
  238.2 4.4 %collective-permute-done.1 = bf16[16,384]{1,0:T(8,128)(2,1)S(1)} collective-permute-done((bf16[16,384]{1,0:T(8,128)(2,1)S(1)}, bf16[16,384]{1,0:T(8,128)(2,1)S(1)}, u32[]{:S(2)}, u32[]{:S(2)}) %collective-permute-start.1) | collective-permute-done | bytes 12320 | tf_op jit(solution)/shard_map/ppermute | solution.py:233
  242.6 22.8 %all_to_all.79 = bf16[16,16,384]{2,1,0:T(8,128)(2,1)S(1)} all-to-all(bf16[16,16,384]{2,1,0:T(8,128)(2,1)S(1)} %broadcast_in_dim.321), channel_id=1, replica_groups=mesh['xh'=2,'core'=2,'z'=8,'y'=8,'xl'=2] {'xh','z'}, dimensions={0} | all-to-all | bytes 393216 | tf_op jit(solution)/shard_map/all_to_all | solution.py:76
  265.4 2.1 all_gather.23
  267.9 1.1 fusion
  269.0 3.6 %all-to-all-start.11 = ((bf16[16,16,768]{2,1,0:T(8,128)(2,1)}), bf16[16,16,768]{2,1,0:T(8,128)(2,1)S(1)}, u32[]{:S(2)}, u32[]{:S(2)}) async-start(bf16[16,16,768]{2,1,0:T(8,128)(2,1)} %bitcast.94), calls=%async_computation.11 | async-start | bytes 786432 | tf_op jit(solution)/shard_map/all_to_all | solution.py:76
  272.6 15.7 %all-to-all-done.11 = bf16[16,16,768]{2,1,0:T(8,128)(2,1)S(1)} async-done(((bf16[16,16,768]{2,1,0:T(8,128)(2,1)}), bf16[16,16,768]{2,1,0:T(8,128)(2,1)S(1)}, u32[]{:S(2)}, u32[]{:S(2)}) %all-to-all-start.11) | async-done | bytes 393248 | tf_op jit(solution)/shard_map/all_to_all | solution.py:76
  288.7 0.8 broadcast_in_dim.328
  289.6 3.6 %all-to-all-start.12 = ((bf16[16,16,896]{2,1,0:T(8,128)(2,1)}), bf16[16,16,896]{2,1,0:T(8,128)(2,1)S(1)}, u32[]{:S(2)}, u32[]{:S(2)}) async-start(bf16[16,16,896]{2,1,0:T(8,128)(2,1)} %broadcast_in_dim.328), calls=%async_computation.12 | async-start | bytes 917504 | tf_op jit(solution)/shard_map/all_to_all | solution.py:76
  293.1 0.7 dynamic-slice_convert_fusion.1
  293.8 13.9 %all-to-all-done.12 = bf16[16,16,896]{2,1,0:T(8,128)(2,1)S(1)} async-done(((bf16[16,16,896]{2,1,0:T(8,128)(2,1)}), bf16[16,16,896]{2,1,0:T(8,128)(2,1)S(1)}, u32[]{:S(2)}, u32[]{:S(2)}) %all-to-all-start.12) | async-done | bytes 458784 | tf_op jit(solution)/shard_map/all_to_all | solution.py:76
  307.7 0.5 convolution_convert_fusion.1
  308.3 4.1 %all_to_all.80 = bf16[2,128,896]{2,1,0:T(8,128)(2,1)S(1)} all-to-all(bf16[2,128,896]{2,1,0:T(8,128)(2,1)S(1)} %bitcast.92), channel_id=1, replica_groups=mesh['xh'=2,'core'=2,'z'=8,'y'=8,'xl'=2] {'core'}, dimensions={0} | all-to-all | bytes 917504 | tf_op jit(solution)/shard_map/all_to_all | solution.py:76
  312.5 0.8 reduce_sum.207
  313.2 4.0 %all-to-all-start.14 = ((bf16[16,8,896]{2,1,0:T(8,128)(2,1)}), bf16[16,8,896]{2,1,0:T(8,128)(2,1)S(1)}, u32[]{:S(2)}, u32[]{:S(2)}) async-start(bf16[16,8,896]{2,1,0:T(8,128)(2,1)} %bitcast.41), calls=%async_computation.14 | async-start | bytes 458752 | tf_op jit(solution)/shard_map/all_to_all | solution.py:76
  317.5 11.0 %all-to-all-done.14 = bf16[16,8,896]{2,1,0:T(8,128)(2,1)S(1)} async-done(((bf16[16,8,896]{2,1,0:T(8,128)(2,1)}), bf16[16,8,896]{2,1,0:T(8,128)(2,1)S(1)}, u32[]{:S(2)}, u32[]{:S(2)}) %all-to-all-start.14) | async-done | bytes 229408 | tf_op jit(solution)/shard_map/all_to_all | solution.py:76
  328.7 0.7 fusion.94
  (164 shorter events, 8.9 us)
Async XLA Ops:
  0.6 16.6 %copy-start = (bf16[768,768]{1,0:T(8,128)(2,1)S(1)}, bf16[768,768]{1,0:T(8,128)(2,1)}, u32[]{:S(2)}) copy-start(bf16[768,768]{1,0:T(8,128)(2,1)} %param.9) | copy-start | bytes 3538948
  0.6 17.5 %copy-start.1 = (bf16[768,768]{1,0:T(8,128)(2,1)S(1)}, bf16[768,768]{1,0:T(8,128)(2,1)}, u32[]{:S(2)}) copy-start(bf16[768,768]{1,0:T(8,128)(2,1)} %param.10) | copy-start | bytes 3538948
  4.1 23.3 %all-to-all-start = ((bf16[16,8,896]{2,1,0:T(8,128)(2,1)}), bf16[16,8,896]{2,1,0:T(8,128)(2,1)S(1)}, u32[]{:S(2)}, u32[]{:S(2)}) async-start(bf16[16,8,896]{2,1,0:T(8,128)(2,1)} %broadcast_in_dim.280), calls=%async_computation | async-start | bytes 458752 | tf_op jit(solution)/shard_map/all_to_all | solution.py:76
  17.2 12.6 %copy-start.11 = (f32[768]{0:T(1024)}, f32[768]{0:T(1024)S(1)}, u32[]{:S(2)}) copy-start(f32[768]{0:T(1024)S(1)} %convert_element_type.200) | copy-start | bytes 9220
  29.6 0.8 copy-start.3
  56.1 0.6 copy-start.15
  56.2 20.0 %copy-start.7 = (f32[16,768]{1,0:T(8,128)}, f32[16,768]{1,0:T(8,128)S(1)}, u32[]{:S(2)}) copy-start(f32[16,768]{1,0:T(8,128)S(1)} %add_reduce_fusion) | copy-start | bytes 147460
  57.6 18.7 %all-to-all-start.2 = ((bf16[16,16,896]{2,1,0:T(8,128)(2,1)}), bf16[16,16,896]{2,1,0:T(8,128)(2,1)S(1)}, u32[]{:S(2)}, u32[]{:S(2)}) async-start(bf16[16,16,896]{2,1,0:T(8,128)(2,1)} %broadcast_in_dim.290), calls=%async_computation.2 | async-start | bytes 917504 | tf_op jit(solution)/shard_map/all_to_all | solution.py:76
  76.9 0.8 copy-start.17
  76.9 0.8 copy-start.20
  76.9 0.8 copy-start.23
  78.3 10.3 %copy-start.4 = (bf16[2,2,64,896]{3,2,1,0:T(8,128)(2,1)S(1)}, bf16[2,2,64,896]{3,2,1,0:T(8,128)(2,1)}, u32[]{:S(2)}) copy-start(bf16[2,2,64,896]{3,2,1,0:T(8,128)(2,1)} %copy-done.3) | copy-start | bytes 1376260
  83.4 17.1 %all-to-all-start.4 = ((bf16[16,16,512]{2,1,0:T(8,128)(2,1)}), bf16[16,16,512]{2,1,0:T(8,128)(2,1)S(1)}, u32[]{:S(2)}, u32[]{:S(2)}) async-start(bf16[16,16,512]{2,1,0:T(8,128)(2,1)} %bitcast.12), calls=%async_computation.4 | async-start | bytes 524288 | tf_op jit(solution)/shard_map/all_to_all | solution.py:76
  88.6 30.7 %copy-start.5 = (bf16[384,1536]{1,0:T(8,128)(2,1)S(1)}, bf16[384,1536]{1,0:T(8,128)(2,1)}, u32[]{:S(2)}) copy-start(bf16[384,1536]{1,0:T(8,128)(2,1)} %param.12) | copy-start | bytes 3538948
  100.9 5.1 %collective-permute-start = (bf16[16,512]{1,0:T(8,128)(2,1)S(1)}, bf16[16,512]{1,0:T(8,128)(2,1)S(1)}, u32[]{:S(2)}, u32[]{:S(2)}) collective-permute-start(bf16[16,512]{1,0:T(8,128)(2,1)S(1)} %pad_maximum_fusion.13), channel_id=1, source_target_pairs={{0,0},{1,32},{2,64},{3,96},{4,128},{5,160},{6,192},{7,224},{8,256}... | collective-permute-start | bytes 49160 | tf_op jit(solution)/shard_map/ppermute | solution.py:171
  107.5 27.0 %all-to-all-start.5 = ((bf16[16,16,896]{2,1,0:T(8,128)(2,1)}), bf16[16,16,896]{2,1,0:T(8,128)(2,1)S(1)}, u32[]{:S(2)}, u32[]{:S(2)}) async-start(bf16[16,16,896]{2,1,0:T(8,128)(2,1)} %broadcast_in_dim.299), calls=%async_computation.5 | async-start | bytes 917504 | tf_op jit(solution)/shard_map/all_to_all | solution.py:76
  119.4 16.4 %copy-start.13 = (f32[384]{0:T(512)}, f32[384]{0:T(512)S(1)}, u32[]{:S(2)}) copy-start(f32[384]{0:T(512)S(1)} %convert_element_type.221) | copy-start | bytes 4612
  120.4 17.0 %copy-start.26 = (pred[128]{0:T(512)(128)(4,1)}, pred[128]{0:T(512)(128)(4,1)S(1)}, u32[]{:S(2)}) copy-start(pred[128]{0:T(512)(128)(4,1)S(1)} %fusion.139) | copy-start | bytes 388
  120.4 17.0 %copy-start.28 = (pred[128]{0:T(512)(128)(4,1)}, pred[128]{0:T(512)(128)(4,1)S(1)}, u32[]{:S(2)}) copy-start(pred[128]{0:T(512)(128)(4,1)S(1)} %get-tuple-element.98) | copy-start | bytes 388
  120.4 17.0 %copy-start.30 = (pred[128]{0:T(512)(128)(4,1)}, pred[128]{0:T(512)(128)(4,1)S(1)}, u32[]{:S(2)}) copy-start(pred[128]{0:T(512)(128)(4,1)S(1)} %get-tuple-element.99) | copy-start | bytes 388
  135.3 1.3 copy-start.32
  136.6 0.8 copy-start.18
  136.6 0.8 copy-start.21
  136.6 0.8 copy-start.24
  145.0 32.1 %copy-start.19 = (pred[128]{0:T(512)(128)(4,1)S(1)}, pred[128]{0:T(512)(128)(4,1)}, u32[]{:S(2)}) copy-start(pred[128]{0:T(512)(128)(4,1)} %fusion.142) | copy-start | bytes 388
  145.0 32.1 %copy-start.22 = (pred[128]{0:T(512)(128)(4,1)S(1)}, pred[128]{0:T(512)(128)(4,1)}, u32[]{:S(2)}) copy-start(pred[128]{0:T(512)(128)(4,1)} %get-tuple-element.100) | copy-start | bytes 388
  145.0 32.1 %copy-start.25 = (pred[128]{0:T(512)(128)(4,1)S(1)}, pred[128]{0:T(512)(128)(4,1)}, u32[]{:S(2)}) copy-start(pred[128]{0:T(512)(128)(4,1)} %get-tuple-element.101) | copy-start | bytes 388
  145.0 32.1 %copy-start.27 = (pred[128]{0:T(512)(128)(4,1)S(1)}, pred[128]{0:T(512)(128)(4,1)}, u32[]{:S(2)}) copy-start(pred[128]{0:T(512)(128)(4,1)} %copy-done.26) | copy-start | bytes 388
  145.0 32.2 %copy-start.29 = (pred[128]{0:T(512)(128)(4,1)S(1)}, pred[128]{0:T(512)(128)(4,1)}, u32[]{:S(2)}) copy-start(pred[128]{0:T(512)(128)(4,1)} %copy-done.28) | copy-start | bytes 388
  145.0 32.2 %copy-start.31 = (pred[128]{0:T(512)(128)(4,1)S(1)}, pred[128]{0:T(512)(128)(4,1)}, u32[]{:S(2)}) copy-start(pred[128]{0:T(512)(128)(4,1)} %copy-done.30) | copy-start | bytes 388
  145.1 31.2 %all-to-all-start.7 = ((bf16[16,16,1792]{2,1,0:T(8,128)(2,1)}), bf16[16,16,1792]{2,1,0:T(8,128)(2,1)S(1)}, u32[]{:S(2)}, u32[]{:S(2)}) async-start(bf16[16,16,1792]{2,1,0:T(8,128)(2,1)} %bitcast.85), calls=%async_computation.7 | async-start | bytes 1835008 | tf_op jit(solution)/shard_map/all_to_all | solution.py:76
  206.9 2.7 copy-start.6
  209.6 2.8 copy-start.33
  213.5 22.0 %copy-start.10 = (bf16[1,16,384]{2,1,0:T(8,128)(2,1)S(1)}, bf16[1,16,384]{2,1,0:T(8,128)(2,1)}, u32[]{:S(2)}) copy-start(bf16[1,16,384]{2,1,0:T(8,128)(2,1)} %param.15) | copy-start | bytes 36868
  213.5 22.0 %copy-start.14 = (f32[384]{0:T(512)S(1)}, f32[384]{0:T(512)}, u32[]{:S(2)}) copy-start(f32[384]{0:T(512)} %copy-done.13) | copy-start | bytes 4612
  214.3 20.7 %all-to-all-start.9 = ((bf16[16,16,896]{2,1,0:T(8,128)(2,1)}), bf16[16,16,896]{2,1,0:T(8,128)(2,1)S(1)}, u32[]{:S(2)}, u32[]{:S(2)}) async-start(bf16[16,16,896]{2,1,0:T(8,128)(2,1)} %bitcast.26), calls=%async_computation.9 | async-start | bytes 917504 | tf_op jit(solution)/shard_map/all_to_all | solution.py:76
  217.9 49.6 %copy-start.2 = (bf16[768,768]{1,0:T(8,128)(2,1)S(1)}, bf16[768,768]{1,0:T(8,128)(2,1)}, u32[]{:S(2)}) copy-start(bf16[768,768]{1,0:T(8,128)(2,1)} %param.10) | copy-start | bytes 3538948
  236.1 6.5 %collective-permute-start.1 = (bf16[16,384]{1,0:T(8,128)(2,1)S(1)}, bf16[16,384]{1,0:T(8,128)(2,1)S(1)}, u32[]{:S(2)}, u32[]{:S(2)}) collective-permute-start(bf16[16,384]{1,0:T(8,128)(2,1)S(1)} %get-tuple-element.50), channel_id=1, source_target_pairs={{0,0},{32,1},{64,2},{96,3},{128,4},{160,5},{192,6},{224,7},{256,8}... | collective-permute-start | bytes 36872 | tf_op jit(solution)/shard_map/ppermute | solution.py:233
  267.9 20.5 %copy-start.8 = (f32[16,768]{1,0:T(8,128)S(1)}, f32[16,768]{1,0:T(8,128)}, u32[]{:S(2)}) copy-start(f32[16,768]{1,0:T(8,128)} %copy-done.7) | copy-start | bytes 147460
  267.9 20.5 %copy-start.16 = (f32[16]{0:T(128)S(1)}, f32[16]{0:T(128)}, u32[]{:S(2)}) copy-start(f32[16]{0:T(128)} %copy-done.15) | copy-start | bytes 196
  269.0 19.3 %all-to-all-start.11 = ((bf16[16,16,768]{2,1,0:T(8,128)(2,1)}), bf16[16,16,768]{2,1,0:T(8,128)(2,1)S(1)}, u32[]{:S(2)}, u32[]{:S(2)}) async-start(bf16[16,16,768]{2,1,0:T(8,128)(2,1)} %bitcast.94), calls=%async_computation.11 | async-start | bytes 786432 | tf_op jit(solution)/shard_map/all_to_all | solution.py:76
  289.6 18.2 %all-to-all-start.12 = ((bf16[16,16,896]{2,1,0:T(8,128)(2,1)}), bf16[16,16,896]{2,1,0:T(8,128)(2,1)S(1)}, u32[]{:S(2)}, u32[]{:S(2)}) async-start(bf16[16,16,896]{2,1,0:T(8,128)(2,1)} %broadcast_in_dim.328), calls=%async_computation.12 | async-start | bytes 917504 | tf_op jit(solution)/shard_map/all_to_all | solution.py:76
  308.3 20.4 %copy-start.9 = (bf16[1,8,768]{2,1,0:T(8,128)(2,1)S(1)}, bf16[1,8,768]{2,1,0:T(8,128)(2,1)}, u32[]{:S(2)}) copy-start(bf16[1,8,768]{2,1,0:T(8,128)(2,1)} %param.8) | copy-start | bytes 36868
  308.3 20.4 %copy-start.12 = (f32[768]{0:T(1024)S(1)}, f32[768]{0:T(1024)}, u32[]{:S(2)}) copy-start(f32[768]{0:T(1024)} %copy-done.11) | copy-start | bytes 9220
  313.2 15.3 %all-to-all-start.14 = ((bf16[16,8,896]{2,1,0:T(8,128)(2,1)}), bf16[16,8,896]{2,1,0:T(8,128)(2,1)S(1)}, u32[]{:S(2)}, u32[]{:S(2)}) async-start(bf16[16,8,896]{2,1,0:T(8,128)(2,1)} %bitcast.41), calls=%async_computation.14 | async-start | bytes 458752 | tf_op jit(solution)/shard_map/all_to_all | solution.py:76

commit v4 on v3

--- a/solution.py
+++ b/solution.py
@@ -85,6 +85,12 @@
     return lax.all_gather(values, "core", axis=0, tiled=False)
 
 
+def pair_sum(core, first, second):
+    both = both_cores(jnp.where(core == 0, second, first))
+    kept = jnp.where(core == 0, first, second)
+    return (kept.astype(F32) + jnp.where(core == 0, both[1], both[0]).astype(F32)).astype(BF)
+
+
 def tile_rows(vector, rows):
     block = vector.reshape(-1, LANES)
     return jnp.concatenate([block, jnp.zeros((rows - block.shape[0], LANES), vector.dtype)], axis=0)
@@ -115,37 +121,29 @@
     u_a = dot(jnp.broadcast_to(gain_first[None], (8, 768)), up_first)[0].astype(BF)
     u_b = dot(jnp.broadcast_to(gain_second[None], (8, 384)), up_second)[0].astype(BF)
     down_sum = contract_cols(jnp.ones((8, 768), BF), down_first)[0].astype(BF)
-    sums_a = jnp.concatenate([tile_rows(u_a, 8), tile_rows(down_sum, 8)], axis=0)
-
-    floats = x_own.astype(F32)
+    sums_a = jnp.concatenate([u_a.reshape(8, 96), down_sum.reshape(8, 96)], axis=0)
+    sums_a = jnp.pad(sums_a, ((0, 0), (0, 32)))
+
+    got = both_cores(send_all(x_own, ROW))
+    x_all = jnp.transpose(got.reshape(2, 2, 64, 768), (1, 0, 2, 3)).reshape(256, 768)
+
+    floats = x_all.astype(F32)
     centre = jnp.sum(floats, axis=1, keepdims=True) / 768
-    spread = jnp.sum((floats - centre) * (floats - centre), axis=1, keepdims=True)
-    message = jnp.concatenate([x_own, pack([centre, spread])], axis=1)
-    got = both_cores(send_all(message, ROW))
-    x_all = jnp.transpose(got.reshape(2, 2, 64, 896), (1, 0, 2, 3)).reshape(256, 896)
-    x_cols = x_all[:, 768:]
-    x_all = x_all[:, :768]
-
-    centred = (x_all.astype(F32) - unpack(x_cols.astype(F32), 0)) * gain_a
-    part = dot(centred.astype(BF), up_first).astype(BF)
-    message = jnp.concatenate(
-        [
-            part.reshape(16, 16, 768),
-            x_cols.reshape(16, 16, LANES),
-            jnp.broadcast_to(sums_a[None], (16, 16, LANES)),
-        ],
-        axis=2,
-    )
-    got = exchange(message, DP)
-    cols = got[:, :, 768:896].astype(F32)
+    centred = floats - centre
+    x_cols = pack([centre, jnp.sum(centred * centred, axis=1, keepdims=True)], 96)
+    lane = lax.broadcasted_iota(jnp.int32, (16, 16, LANES), 2)
+    x_cols = jnp.where(lane < 96, sums_a, x_cols.reshape(16, 16, LANES))
+    part = dot((centred * gain_a).astype(BF), up_first).astype(BF)
+    got = exchange(jnp.concatenate([part.reshape(16, 16, 768), x_cols], axis=2), DP)
+    cols = got[:, :, 864:].astype(F32)
     centres = unpack(cols, 0)
     mean_a = jnp.mean(centres, axis=0)
     off = centres - mean_a
     var_a = (jnp.sum(unpack(cols, 1), axis=0) + 768 * jnp.sum(off * off, axis=0)) / D
     rstd_a = lax.rsqrt(var_a + EPS)
-    u_all = got[:, :6, 896:].reshape(16, 1, 768).astype(F32)
+    u_all = got[:, :8, 768:864].reshape(16, 1, 768).astype(F32)
     gain_up_a = jnp.sum(u_all, axis=0)
-    down_sum = jnp.sum(got[:, 8:14, 896:].astype(F32), axis=0).reshape(1, 768)
+    down_sum = jnp.sum(got[:, 8:, 768:864].astype(F32), axis=0).reshape(1, 768)
     hidden_a = rstd_a * jnp.sum(got[:, :, :768].astype(F32) + off * u_all, axis=0)
     active = gelu_value(hidden_a).astype(BF)
     got = send_all(jnp.concatenate([active, pack([mean_a, rstd_a])], axis=1), DP)
@@ -154,14 +152,11 @@
     part = dot(active, down_first).astype(BF)
     shift = row_dot(active.astype(F32), down_sum) + unpack(stats_a.astype(F32), 0) * (D / 32)
     cols = pack([shift], 64 * core)
-    message = jnp.stack(
-        [
-            jnp.concatenate([part[:, :384], cols], axis=1),
-            jnp.concatenate([part[:, 384:], cols], axis=1),
-        ]
-    )
-    got = exchange(message, "core")
-    part = jnp.sum(got.astype(F32), axis=0).astype(BF)
+    part = pair_sum(
+        core,
+        jnp.concatenate([part[:, :384], cols], axis=1),
+        jnp.concatenate([part[:, 384:], cols], axis=1),
+    )
     sums = jnp.sum(exchange(part.reshape(16, 16, 512), ROW).astype(F32), axis=0)
     centre = unpack_pair(sums[:, 384:], 0) / D
     rows = lax.dynamic_slice_in_dim(x_all, chunk * 16, 16, 0)
@@ -234,8 +229,8 @@
         grad_own.astype(BF), NAMES, [(target, source) for source, target in crossing()]
     )
     grad_all = both_cores(send_all(crossed, ROW))
-    part = contract_cols(grad_all[0], down_first[:, :384])
-    part = part + contract_cols(grad_all[1], down_first[:, 384:])
+    grad_cols = jnp.concatenate([grad_all[0], grad_all[1]], axis=1)
+    part = contract_cols(grad_cols, down_first)
     sums = jnp.sum(exchange(part.astype(BF).reshape(16, 16, 768), DP).astype(F32), axis=0)
     d_hid_a = (sums * gelu_slope(hidden_a)).astype(BF)
     floats = d_hid_a.astype(F32)
@@ -249,16 +244,14 @@
     got = send_all(jnp.concatenate([d_hid_a, cols], axis=1), DP)
     part = contract_cols(got[:, :768], up_first).astype(BF)
     message = jnp.concatenate([part, got[:, 768:]], axis=1).reshape(2, 2, 64, 896)
-    got = exchange(jnp.transpose(message, (1, 0, 2, 3)).reshape(2, 128, 896), "core")
-    part = jnp.sum(got.astype(F32), axis=0).astype(BF)
+    part = pair_sum(core, message[:, 0].reshape(128, 896), message[:, 1].reshape(128, 896))
     sums = jnp.sum(exchange(part.reshape(16, 8, 896), ROW).astype(F32), axis=0)
     sum_one = unpack_pair(sums[:, 768:], 0)
     sum_two = unpack_pair(sums[:, 768:], 1)
     stats = lax.dynamic_slice_in_dim(stats_a, own_row, 8, 0).astype(F32)
     rstd = unpack(stats, 1)
     nhat_a = (x_own.astype(F32) - unpack(stats, 0)) * rstd
-    upstream = lax.dynamic_slice_in_dim(grad_all, own_row, 8, 1).astype(F32)
-    upstream = jnp.concatenate([upstream[0], upstream[1]], axis=1)
+    upstream = lax.dynamic_slice_in_dim(grad_cols, own_row, 8, 0).astype(F32)
     result = upstream + rstd * (sums[:, :768] * gain_a - sum_one / D - nhat_a * (sum_two / D))
     return residual_out[None], result.astype(BF)[None]
 

time: 331 us -> 321 us (0.970)
  blocking collectives: 100 us -> 89.1 us
  other arithmetic: 16.8 us -> 10.8 us
  waiting for transfers between devices: 139 us -> 144 us
    all_to_all x6 -> x4, blocking collectives: 90.8 us -> 75.6 us  [exchange(): return lax.all_to_all(blocks, axis, 0, 0)]
    all_to_all x9, waiting for transfers between devices: 131 us -> 136 us  [exchange(): return lax.all_to_all(blocks, axis, 0, 0)]
    all_gather x4 -> x6, blocking collectives: 9.16 us -> 13.4 us  [both_cores(): return lax.all_gather(values, 'core', axis=0, tiled=False)]
  transfers between devices with their start and end apart: 11 -> 11, of which waited for: 11 -> 11; matrix products, arithmetic and copies ran while one was open for 2% -> 1% of each run, Pallas kernels for 0% -> 0%
where the time goes in v4:
time: 321 us; the launch traced here: 320 us
  waiting for transfers between devices  144 us (45%)
  blocking collectives  89.1 us (28%)
  starting transfers between devices  60.2 us (19%)
  other arithmetic  10.8 us (3%)
  matrix products  9.65 us (3%)
  local copies, waits for them, and re-layouts  4.97 us (2%)
    all_to_all x9, waiting for transfers between devices, exchange(): return lax.all_to_all(blocks, axis, 0, 0)  136 us
    all_to_all x4, blocking collectives, exchange(): return lax.all_to_all(blocks, axis, 0, 0)  75.6 us
    all_to_all x9, starting transfers between devices, exchange(): return lax.all_to_all(blocks, axis, 0, 0)  56.4 us
    all_gather x6, blocking collectives, both_cores(): return lax.all_gather(values, 'core', axis=0, tiled=False)  13.4 us
  transfers between devices with their start and end apart: 11, of which 11 were waited for; matrix products, arithmetic and copies ran while one was open for 1% of the time, Pallas kernels for 0%

profile of v4, /device:TPU:64, one launch (start us, length us, event | category | flops | bytes accessed | tf_op | source)
XLA Modules:
  0.0 319.8 jit_solution(18359782925829267564)
XLA Ops:
  0.6 1.5 broadcast_in_dim.270
  2.1 12.4 %all-to-all-start = ((bf16[16,8,768]{2,1,0:T(8,128)(2,1)}), bf16[16,8,768]{2,1,0:T(8,128)(2,1)S(1)}, u32[]{:S(2)}, u32[]{:S(2)}) async-start(bf16[16,8,768]{2,1,0:T(8,128)(2,1)} %broadcast_in_dim.270), calls=%async_computation | async-start | bytes 393216 | tf_op jit(solution)/shard_map/all_to_all | solution.py:76
  14.6 1.6 fusion.119
  16.2 0.4 fusion.117
  16.9 8.4 %all-to-all-done = bf16[16,8,768]{2,1,0:T(8,128)(2,1)S(1)} async-done(((bf16[16,8,768]{2,1,0:T(8,128)(2,1)}), bf16[16,8,768]{2,1,0:T(8,128)(2,1)S(1)}, u32[]{:S(2)}, u32[]{:S(2)}) %all-to-all-start) | async-done | bytes 196640 | tf_op jit(solution)/shard_map/all_to_all | solution.py:76
  25.3 2.1 all_gather.26
  27.5 0.2 fusion.7
  28.1 0.5 convolution_convert_fusion.4
  28.6 0.3 fusion.54
  28.9 0.8 pad_maximum_fusion.3
  29.7 7.2 %all-to-all-start.1 = ((bf16[16,16,896]{2,1,0:T(8,128)(2,1)}), bf16[16,16,896]{2,1,0:T(8,128)(2,1)S(1)}, u32[]{:S(2)}, u32[]{:S(2)}) async-start(bf16[16,16,896]{2,1,0:T(8,128)(2,1)} %pad_maximum_fusion.3), calls=%async_computation.1 | async-start | bytes 917504 | tf_op jit(solution)/shard_map/all_to_all | solution.py:76
  37.0 16.5 %all-to-all-done.1 = bf16[16,16,896]{2,1,0:T(8,128)(2,1)S(1)} async-done(((bf16[16,16,896]{2,1,0:T(8,128)(2,1)}), bf16[16,16,896]{2,1,0:T(8,128)(2,1)S(1)}, u32[]{:S(2)}, u32[]{:S(2)}) %all-to-all-start.1) | async-done | bytes 458784 | tf_op jit(solution)/shard_map/all_to_all | solution.py:76
  54.3 0.8 broadcast_in_dim.286
  55.1 3.6 %all-to-all-start.2 = ((bf16[16,16,896]{2,1,0:T(8,128)(2,1)}), bf16[16,16,896]{2,1,0:T(8,128)(2,1)S(1)}, u32[]{:S(2)}, u32[]{:S(2)}) async-start(bf16[16,16,896]{2,1,0:T(8,128)(2,1)} %broadcast_in_dim.286), calls=%async_computation.2 | async-start | bytes 917504 | tf_op jit(solution)/shard_map/all_to_all | solution.py:76
  58.8 14.9 %all-to-all-done.2 = bf16[16,16,896]{2,1,0:T(8,128)(2,1)S(1)} async-done(((bf16[16,16,896]{2,1,0:T(8,128)(2,1)}), bf16[16,16,896]{2,1,0:T(8,128)(2,1)S(1)}, u32[]{:S(2)}, u32[]{:S(2)}) %all-to-all-start.2) | async-done | bytes 458784 | tf_op jit(solution)/shard_map/all_to_all | solution.py:76
  73.7 0.5 convolution_convert_fusion.3
  74.5 0.5 fusion.41
  75.1 2.2 all_gather.27
  77.3 0.8 fusion.8
  78.1 4.8 %all-to-all-start.3 = ((bf16[16,16,512]{2,1,0:T(8,128)(2,1)}), bf16[16,16,512]{2,1,0:T(8,128)(2,1)S(1)}, u32[]{:S(2)}, u32[]{:S(2)}) async-start(bf16[16,16,512]{2,1,0:T(8,128)(2,1)} %fusion.8), calls=%async_computation.3 | async-start | bytes 524288 | tf_op jit(solution)/shard_map/all_to_all | solution.py:76
  82.9 11.9 %all-to-all-done.3 = bf16[16,16,512]{2,1,0:T(8,128)(2,1)S(1)} async-done(((bf16[16,16,512]{2,1,0:T(8,128)(2,1)}), bf16[16,16,512]{2,1,0:T(8,128)(2,1)S(1)}, u32[]{:S(2)}, u32[]{:S(2)}) %all-to-all-start.3) | async-done | bytes 262176 | tf_op jit(solution)/shard_map/all_to_all | solution.py:76
  95.1 1.9 collective-permute-start
  97.1 3.2 %collective-permute-done = bf16[16,512]{1,0:T(8,128)(2,1)S(1)} collective-permute-done((bf16[16,512]{1,0:T(8,128)(2,1)S(1)}, bf16[16,512]{1,0:T(8,128)(2,1)S(1)}, u32[]{:S(2)}, u32[]{:S(2)}) %collective-permute-start) | collective-permute-done | bytes 16416 | tf_op jit(solution)/shard_map/ppermute | solution.py:166
  100.3 0.8 broadcast_in_dim.295
  101.1 11.2 %all-to-all-start.4 = ((bf16[16,16,896]{2,1,0:T(8,128)(2,1)}), bf16[16,16,896]{2,1,0:T(8,128)(2,1)S(1)}, u32[]{:S(2)}, u32[]{:S(2)}) async-start(bf16[16,16,896]{2,1,0:T(8,128)(2,1)} %broadcast_in_dim.295), calls=%async_computation.4 | async-start | bytes 917504 | tf_op jit(solution)/shard_map/all_to_all | solution.py:76
  112.4 0.3 convolution_convert_fusion
  112.7 15.5 %all-to-all-done.4 = bf16[16,16,896]{2,1,0:T(8,128)(2,1)S(1)} async-done(((bf16[16,16,896]{2,1,0:T(8,128)(2,1)}), bf16[16,16,896]{2,1,0:T(8,128)(2,1)S(1)}, u32[]{:S(2)}, u32[]{:S(2)}) %all-to-all-start.4) | async-done | bytes 458784 | tf_op jit(solution)/shard_map/all_to_all | solution.py:76
  128.4 0.5 fusion.23
  129.0 0.4 convolution_convert_fusion.6
  129.4 0.4 convolution_convert_fusion.8
  129.8 0.4 copy-done.9
  130.2 0.4 convolution_convert_fusion.5
  130.6 0.4 convolution_convert_fusion.7
  131.0 0.5 fusion.47
  131.9 5.2 %all_to_all.65 = bf16[2,256,1792]{2,1,0:T(8,128)(2,1)S(1)} all-to-all(bf16[2,256,1792]{2,1,0:T(8,128)(2,1)S(1)} %pad_maximum_fusion), channel_id=1, replica_groups=mesh['xh'=2,'core'=2,'z'=8,'y'=8,'xl'=2] {'core'}, dimensions={0} | all-to-all | bytes 3670016 | tf_op jit(solution)/shard_map/all_to_all | solution.py:76
  137.1 1.5 reduce_sum.176
  138.6 6.0 %all-to-all-start.6 = ((bf16[16,16,1792]{2,1,0:T(8,128)(2,1)}), bf16[16,16,1792]{2,1,0:T(8,128)(2,1)S(1)}, u32[]{:S(2)}, u32[]{:S(2)}) async-start(bf16[16,16,1792]{2,1,0:T(8,128)(2,1)} %bitcast.81), calls=%async_computation.6 | async-start | bytes 1835008 | tf_op jit(solution)/shard_map/all_to_all | solution.py:76
  144.7 25.2 %all-to-all-done.6 = bf16[16,16,1792]{2,1,0:T(8,128)(2,1)S(1)} async-done(((bf16[16,16,1792]{2,1,0:T(8,128)(2,1)}), bf16[16,16,1792]{2,1,0:T(8,128)(2,1)S(1)}, u32[]{:S(2)}, u32[]{:S(2)}) %all-to-all-start.6) | async-done | bytes 917536 | tf_op jit(solution)/shard_map/all_to_all | solution.py:76
  170.2 0.2 fusion.95
  170.9 29.5 %all_to_all.66 = bf16[16,16,1664]{2,1,0:T(8,128)(2,1)S(1)} all-to-all(bf16[16,16,1664]{2,1,0:T(8,128)(2,1)S(1)} %broadcast_in_dim.315), channel_id=1, replica_groups=mesh['xh'=2,'core'=2,'z'=8,'y'=8,'xl'=2] {'xh','z'}, dimensions={0} | all-to-all | bytes 1703936 | tf_op jit(solution)/shard_map/all_to_all | solution.py:76
  200.5 2.6 all-gather
  203.1 0.4 fusion.16
  203.5 2.4 all-gather.1
  205.8 0.4 fusion.13
  206.2 0.4 fusion.1
  206.6 0.4 fusion
  207.0 0.8 pad_maximum_fusion.4
  207.8 3.6 %all-to-all-start.8 = ((bf16[16,16,896]{2,1,0:T(8,128)(2,1)}), bf16[16,16,896]{2,1,0:T(8,128)(2,1)S(1)}, u32[]{:S(2)}, u32[]{:S(2)}) async-start(bf16[16,16,896]{2,1,0:T(8,128)(2,1)} %bitcast.29), calls=%async_computation.8 | async-start | bytes 917504 | tf_op jit(solution)/shard_map/all_to_all | solution.py:76
  211.4 17.1 %all-to-all-done.8 = bf16[16,16,896]{2,1,0:T(8,128)(2,1)S(1)} async-done(((bf16[16,16,896]{2,1,0:T(8,128)(2,1)}), bf16[16,16,896]{2,1,0:T(8,128)(2,1)S(1)}, u32[]{:S(2)}, u32[]{:S(2)}) %all-to-all-start.8) | async-done | bytes 458784 | tf_op jit(solution)/shard_map/all_to_all | solution.py:76
  228.9 0.6 fusion.81
  229.5 1.9 collective-permute-start.1
  231.5 4.6 %collective-permute-done.1 = bf16[16,384]{1,0:T(8,128)(2,1)S(1)} collective-permute-done((bf16[16,384]{1,0:T(8,128)(2,1)S(1)}, bf16[16,384]{1,0:T(8,128)(2,1)S(1)}, u32[]{:S(2)}, u32[]{:S(2)}) %collective-permute-start.1) | collective-permute-done | bytes 12320 | tf_op jit(solution)/shard_map/ppermute | solution.py:228
  236.0 22.8 %all_to_all.67 = bf16[16,16,384]{2,1,0:T(8,128)(2,1)S(1)} all-to-all(bf16[16,16,384]{2,1,0:T(8,128)(2,1)S(1)} %broadcast_in_dim.317), channel_id=1, replica_groups=mesh['xh'=2,'core'=2,'z'=8,'y'=8,'xl'=2] {'xh','z'}, dimensions={0} | all-to-all | bytes 393216 | tf_op jit(solution)/shard_map/all_to_all | solution.py:76
  258.9 2.1 all_gather.32
  261.0 1.2 convolution_convert_fusion.2
  262.2 3.6 %all-to-all-start.10 = ((bf16[16,16,768]{2,1,0:T(8,128)(2,1)}), bf16[16,16,768]{2,1,0:T(8,128)(2,1)S(1)}, u32[]{:S(2)}, u32[]{:S(2)}) async-start(bf16[16,16,768]{2,1,0:T(8,128)(2,1)} %bitcast.36), calls=%async_computation.10 | async-start | bytes 786432 | tf_op jit(solution)/shard_map/all_to_all | solution.py:76
  265.9 15.7 %all-to-all-done.10 = bf16[16,16,768]{2,1,0:T(8,128)(2,1)S(1)} async-done(((bf16[16,16,768]{2,1,0:T(8,128)(2,1)}), bf16[16,16,768]{2,1,0:T(8,128)(2,1)S(1)}, u32[]{:S(2)}, u32[]{:S(2)}) %all-to-all-start.10) | async-done | bytes 393248 | tf_op jit(solution)/shard_map/all_to_all | solution.py:76
  282.0 18.1 %all_to_all.68 = bf16[16,16,896]{2,1,0:T(8,128)(2,1)S(1)} all-to-all(bf16[16,16,896]{2,1,0:T(8,128)(2,1)S(1)} %broadcast_in_dim.324), channel_id=1, replica_groups=mesh['xh'=2,'core'=2,'z'=8,'y'=8,'xl'=2] {'y','xl'}, dimensions={0} | all-to-all | bytes 917504 | tf_op jit(solution)/shard_map/all_to_all | solution.py:76
  300.1 0.5 convolution_convert_fusion.1
  300.7 2.1 all_gather.33
  302.9 0.8 fusion.19
  303.6 4.0 %all-to-all-start.12 = ((bf16[16,8,896]{2,1,0:T(8,128)(2,1)}), bf16[16,8,896]{2,1,0:T(8,128)(2,1)S(1)}, u32[]{:S(2)}, u32[]{:S(2)}) async-start(bf16[16,8,896]{2,1,0:T(8,128)(2,1)} %fusion.19), calls=%async_computation.12 | async-start | bytes 458752 | tf_op jit(solution)/shard_map/all_to_all | solution.py:76
  307.8 11.1 %all-to-all-done.12 = bf16[16,8,896]{2,1,0:T(8,128)(2,1)S(1)} async-done(((bf16[16,8,896]{2,1,0:T(8,128)(2,1)}), bf16[16,8,896]{2,1,0:T(8,128)(2,1)S(1)}, u32[]{:S(2)}, u32[]{:S(2)}) %all-to-all-start.12) | async-done | bytes 229408 | tf_op jit(solution)/shard_map/all_to_all | solution.py:76
  319.1 0.7 fusion.92
  (122 shorter events, 5.5 us)
Async XLA Ops:
  0.6 15.6 %copy-start = (bf16[768,768]{1,0:T(8,128)(2,1)S(1)}, bf16[768,768]{1,0:T(8,128)(2,1)}, u32[]{:S(2)}) copy-start(bf16[768,768]{1,0:T(8,128)(2,1)} %param.10) | copy-start | bytes 3538948
  2.1 23.1 %all-to-all-start = ((bf16[16,8,768]{2,1,0:T(8,128)(2,1)}), bf16[16,8,768]{2,1,0:T(8,128)(2,1)S(1)}, u32[]{:S(2)}, u32[]{:S(2)}) async-start(bf16[16,8,768]{2,1,0:T(8,128)(2,1)} %broadcast_in_dim.270), calls=%async_computation | async-start | bytes 393216 | tf_op jit(solution)/shard_map/all_to_all | solution.py:76
  14.6 2.1 copy-start.7
  16.6 11.4 %copy-start.1 = (bf16[768,768]{1,0:T(8,128)(2,1)S(1)}, bf16[768,768]{1,0:T(8,128)(2,1)}, u32[]{:S(2)}) copy-start(bf16[768,768]{1,0:T(8,128)(2,1)} %param.9) | copy-start | bytes 3538948
  29.7 23.8 %all-to-all-start.1 = ((bf16[16,16,896]{2,1,0:T(8,128)(2,1)}), bf16[16,16,896]{2,1,0:T(8,128)(2,1)S(1)}, u32[]{:S(2)}, u32[]{:S(2)}) async-start(bf16[16,16,896]{2,1,0:T(8,128)(2,1)} %pad_maximum_fusion.3), calls=%async_computation.1 | async-start | bytes 917504 | tf_op jit(solution)/shard_map/all_to_all | solution.py:76
  55.1 18.6 %all-to-all-start.2 = ((bf16[16,16,896]{2,1,0:T(8,128)(2,1)}), bf16[16,16,896]{2,1,0:T(8,128)(2,1)S(1)}, u32[]{:S(2)}, u32[]{:S(2)}) async-start(bf16[16,16,896]{2,1,0:T(8,128)(2,1)} %broadcast_in_dim.286), calls=%async_computation.2 | async-start | bytes 917504 | tf_op jit(solution)/shard_map/all_to_all | solution.py:76
  77.3 23.0 %copy-start.5 = (bf16[1,16,384]{2,1,0:T(8,128)(2,1)S(1)}, bf16[1,16,384]{2,1,0:T(8,128)(2,1)}, u32[]{:S(2)}) copy-start(bf16[1,16,384]{2,1,0:T(8,128)(2,1)} %param.15) | copy-start | bytes 36868
  78.1 34.2 %copy-start.8 = (bf16[384]{0:T(512)(128)(2,1)S(1)}, bf16[384]{0:T(512)(128)(2,1)}, u32[]{:S(2)}) copy-start(bf16[384]{0:T(512)(128)(2,1)} %param.14) | copy-start | bytes 2308
  78.1 34.2 %copy-start.3 = (bf16[384,1536]{1,0:T(8,128)(2,1)S(1)}, bf16[384,1536]{1,0:T(8,128)(2,1)}, u32[]{:S(2)}) copy-start(bf16[384,1536]{1,0:T(8,128)(2,1)} %param.12) | copy-start | bytes 3538948
  78.1 16.6 %all-to-all-start.3 = ((bf16[16,16,512]{2,1,0:T(8,128)(2,1)}), bf16[16,16,512]{2,1,0:T(8,128)(2,1)S(1)}, u32[]{:S(2)}, u32[]{:S(2)}) async-start(bf16[16,16,512]{2,1,0:T(8,128)(2,1)} %fusion.8), calls=%async_computation.3 | async-start | bytes 524288 | tf_op jit(solution)/shard_map/all_to_all | solution.py:76
  95.1 5.1 %collective-permute-start = (bf16[16,512]{1,0:T(8,128)(2,1)S(1)}, bf16[16,512]{1,0:T(8,128)(2,1)S(1)}, u32[]{:S(2)}, u32[]{:S(2)}) collective-permute-start(bf16[16,512]{1,0:T(8,128)(2,1)S(1)} %pad_maximum_fusion.16), channel_id=1, source_target_pairs={{0,0},{1,32},{2,64},{3,96},{4,128},{5,160},{6,192},{7,224},{8,256}... | collective-permute-start | bytes 49160 | tf_op jit(solution)/shard_map/ppermute | solution.py:166
  101.1 27.1 %all-to-all-start.4 = ((bf16[16,16,896]{2,1,0:T(8,128)(2,1)}), bf16[16,16,896]{2,1,0:T(8,128)(2,1)S(1)}, u32[]{:S(2)}, u32[]{:S(2)}) async-start(bf16[16,16,896]{2,1,0:T(8,128)(2,1)} %broadcast_in_dim.295), calls=%async_computation.4 | async-start | bytes 917504 | tf_op jit(solution)/shard_map/all_to_all | solution.py:76
  129.0 1.3 copy-start.9
  138.6 31.2 %all-to-all-start.6 = ((bf16[16,16,1792]{2,1,0:T(8,128)(2,1)}), bf16[16,16,1792]{2,1,0:T(8,128)(2,1)S(1)}, u32[]{:S(2)}, u32[]{:S(2)}) async-start(bf16[16,16,1792]{2,1,0:T(8,128)(2,1)} %bitcast.81), calls=%async_computation.6 | async-start | bytes 1835008 | tf_op jit(solution)/shard_map/all_to_all | solution.py:76
  200.4 2.7 copy-start.4
  203.1 2.8 copy-start.10
  207.8 20.7 %all-to-all-start.8 = ((bf16[16,16,896]{2,1,0:T(8,128)(2,1)}), bf16[16,16,896]{2,1,0:T(8,128)(2,1)S(1)}, u32[]{:S(2)}, u32[]{:S(2)}) async-start(bf16[16,16,896]{2,1,0:T(8,128)(2,1)} %bitcast.29), calls=%async_computation.8 | async-start | bytes 917504 | tf_op jit(solution)/shard_map/all_to_all | solution.py:76
  229.5 6.5 %collective-permute-start.1 = (bf16[16,384]{1,0:T(8,128)(2,1)S(1)}, bf16[16,384]{1,0:T(8,128)(2,1)S(1)}, u32[]{:S(2)}, u32[]{:S(2)}) collective-permute-start(bf16[16,384]{1,0:T(8,128)(2,1)S(1)} %get-tuple-element.54), channel_id=1, source_target_pairs={{0,0},{32,1},{64,2},{96,3},{128,4},{160,5},{192,6},{224,7},{256,8}... | collective-permute-start | bytes 36872 | tf_op jit(solution)/shard_map/ppermute | solution.py:228
  262.2 19.3 %all-to-all-start.10 = ((bf16[16,16,768]{2,1,0:T(8,128)(2,1)}), bf16[16,16,768]{2,1,0:T(8,128)(2,1)S(1)}, u32[]{:S(2)}, u32[]{:S(2)}) async-start(bf16[16,16,768]{2,1,0:T(8,128)(2,1)} %bitcast.36), calls=%async_computation.10 | async-start | bytes 786432 | tf_op jit(solution)/shard_map/all_to_all | solution.py:76
  265.8 34.3 %copy-start.2 = (bf16[768,768]{1,0:T(8,128)(2,1)S(1)}, bf16[768,768]{1,0:T(8,128)(2,1)}, u32[]{:S(2)}) copy-start(bf16[768,768]{1,0:T(8,128)(2,1)} %param.9) | copy-start | bytes 3538948
  300.7 18.4 %copy-start.6 = (bf16[1,8,768]{2,1,0:T(8,128)(2,1)S(1)}, bf16[1,8,768]{2,1,0:T(8,128)(2,1)}, u32[]{:S(2)}) copy-start(bf16[1,8,768]{2,1,0:T(8,128)(2,1)} %param.8) | copy-start | bytes 36868
  303.6 15.3 %all-to-all-start.12 = ((bf16[16,8,896]{2,1,0:T(8,128)(2,1)}), bf16[16,8,896]{2,1,0:T(8,128)(2,1)S(1)}, u32[]{:S(2)}, u32[]{:S(2)}) async-start(bf16[16,8,896]{2,1,0:T(8,128)(2,1)} %fusion.19), calls=%async_computation.12 | async-start | bytes 458752 | tf_op jit(solution)/shard_map/all_to_all | solution.py:76

commit v5 on v4

--- a/solution.py
+++ b/solution.py
@@ -164,7 +164,6 @@
     middle = (rows + sums[:, :384]).astype(BF)
 
     crossed = lax.ppermute(jnp.concatenate([middle, pack([centre])], axis=1), NAMES, crossing())
-    middle_own = crossed[:, :384].astype(F32)
     got = send_all(jnp.concatenate([crossed, cot_own], axis=1), DP)
     cot_all = got[:, 512:]
     centred = got[:, :384].astype(F32) - unpack(got[:, 384:512].astype(F32), 0)
@@ -213,6 +212,8 @@
     part_b = dot(active[0], down_second[:768]) + dot(active[1], down_second[768:])
     message = jnp.concatenate([part.astype(BF), cols, part_b.astype(BF)], axis=1)
     got = exchange(message.reshape(16, 16, 896), DP)
+    got, crossed, cot_own = lax.optimization_barrier((got, crossed, cot_own))
+    middle_own = crossed[:, :384].astype(F32)
     sums = jnp.sum(got.astype(F32), axis=0)
     residual_out = (middle_own + sums[:, 512:]).astype(BF)
     sum_one = unpack_pair(sums[:, 384:512], 0)

time: 321 us -> 319 us (level)
  blocking collectives: 89.1 us -> 109 us
  waiting for transfers between devices: 144 us -> 127 us
  starting transfers between devices: 60.2 us -> 56.6 us
    all_to_all x4 -> x5, blocking collectives: 75.6 us -> 95.4 us  [exchange(): return lax.all_to_all(blocks, axis, 0, 0)]
    all_to_all x9 -> x8, waiting for transfers between devices: 136 us -> 119 us  [exchange(): return lax.all_to_all(blocks, axis, 0, 0)]
    all_to_all x9 -> x8, starting transfers between devices: 56.4 us -> 52.8 us  [exchange(): return lax.all_to_all(blocks, axis, 0, 0)]
  transfers between devices with their start and end apart: 11 -> 10, of which waited for: 11 -> 10; matrix products, arithmetic and copies ran while one was open for 1% -> 1% of each run, Pallas kernels for 0% -> 0%
where the time goes in v5:
time: 319 us; the launch traced here: 318 us
  waiting for transfers between devices  127 us (40%)
  blocking collectives  109 us (34%)
  starting transfers between devices  56.6 us (18%)
  other arithmetic  9.99 us (3%)
  matrix products  9.65 us (3%)
  local copies, waits for them, and re-layouts  4.97 us (2%)
    all_to_all x8, waiting for transfers between devices, exchange(): return lax.all_to_all(blocks, axis, 0, 0)  119 us
    all_to_all x5, blocking collectives, exchange(): return lax.all_to_all(blocks, axis, 0, 0)  95.4 us
    all_to_all x8, starting transfers between devices, exchange(): return lax.all_to_all(blocks, axis, 0, 0)  52.8 us
    all_gather x6, blocking collectives, both_cores(): return lax.all_gather(values, 'core', axis=0, tiled=False)  13.4 us
  transfers between devices with their start and end apart: 10, of which 10 were waited for; matrix products, arithmetic and copies ran while one was open for 1% of the time, Pallas kernels for 0%

profile of v5, /device:TPU:64, one launch (start us, length us, event | category | flops | bytes accessed | tf_op | source)
XLA Modules:
  0.0 318.1 jit_solution(2477350558539967488)
XLA Ops:
  0.6 1.5 broadcast_in_dim.270
  2.1 12.4 %all-to-all-start = ((bf16[16,8,768]{2,1,0:T(8,128)(2,1)}), bf16[16,8,768]{2,1,0:T(8,128)(2,1)S(1)}, u32[]{:S(2)}, u32[]{:S(2)}) async-start(bf16[16,8,768]{2,1,0:T(8,128)(2,1)} %broadcast_in_dim.270), calls=%async_computation | async-start | bytes 393216 | tf_op jit(solution)/shard_map/all_to_all | solution.py:76
  14.6 1.6 fusion.119
  16.2 0.4 fusion.117
  16.9 8.4 %all-to-all-done = bf16[16,8,768]{2,1,0:T(8,128)(2,1)S(1)} async-done(((bf16[16,8,768]{2,1,0:T(8,128)(2,1)}), bf16[16,8,768]{2,1,0:T(8,128)(2,1)S(1)}, u32[]{:S(2)}, u32[]{:S(2)}) %all-to-all-start) | async-done | bytes 196640 | tf_op jit(solution)/shard_map/all_to_all | solution.py:76
  25.3 2.1 all_gather.26
  27.5 0.2 fusion.7
  28.1 0.5 convolution_convert_fusion.4
  28.6 0.3 fusion.54
  28.9 0.8 pad_maximum_fusion.3
  29.7 7.2 %all-to-all-start.1 = ((bf16[16,16,896]{2,1,0:T(8,128)(2,1)}), bf16[16,16,896]{2,1,0:T(8,128)(2,1)S(1)}, u32[]{:S(2)}, u32[]{:S(2)}) async-start(bf16[16,16,896]{2,1,0:T(8,128)(2,1)} %pad_maximum_fusion.3), calls=%async_computation.1 | async-start | bytes 917504 | tf_op jit(solution)/shard_map/all_to_all | solution.py:76
  37.0 16.5 %all-to-all-done.1 = bf16[16,16,896]{2,1,0:T(8,128)(2,1)S(1)} async-done(((bf16[16,16,896]{2,1,0:T(8,128)(2,1)}), bf16[16,16,896]{2,1,0:T(8,128)(2,1)S(1)}, u32[]{:S(2)}, u32[]{:S(2)}) %all-to-all-start.1) | async-done | bytes 458784 | tf_op jit(solution)/shard_map/all_to_all | solution.py:76
  54.3 0.8 broadcast_in_dim.286
  55.1 3.6 %all-to-all-start.2 = ((bf16[16,16,896]{2,1,0:T(8,128)(2,1)}), bf16[16,16,896]{2,1,0:T(8,128)(2,1)S(1)}, u32[]{:S(2)}, u32[]{:S(2)}) async-start(bf16[16,16,896]{2,1,0:T(8,128)(2,1)} %broadcast_in_dim.286), calls=%async_computation.2 | async-start | bytes 917504 | tf_op jit(solution)/shard_map/all_to_all | solution.py:76
  58.8 14.9 %all-to-all-done.2 = bf16[16,16,896]{2,1,0:T(8,128)(2,1)S(1)} async-done(((bf16[16,16,896]{2,1,0:T(8,128)(2,1)}), bf16[16,16,896]{2,1,0:T(8,128)(2,1)S(1)}, u32[]{:S(2)}, u32[]{:S(2)}) %all-to-all-start.2) | async-done | bytes 458784 | tf_op jit(solution)/shard_map/all_to_all | solution.py:76
  73.7 0.5 convolution_convert_fusion.3
  74.5 0.5 fusion.41
  75.1 2.2 all_gather.27
  77.3 0.8 fusion.8
  78.1 4.8 %all-to-all-start.3 = ((bf16[16,16,512]{2,1,0:T(8,128)(2,1)}), bf16[16,16,512]{2,1,0:T(8,128)(2,1)S(1)}, u32[]{:S(2)}, u32[]{:S(2)}) async-start(bf16[16,16,512]{2,1,0:T(8,128)(2,1)} %fusion.8), calls=%async_computation.3 | async-start | bytes 524288 | tf_op jit(solution)/shard_map/all_to_all | solution.py:76
  82.9 11.9 %all-to-all-done.3 = bf16[16,16,512]{2,1,0:T(8,128)(2,1)S(1)} async-done(((bf16[16,16,512]{2,1,0:T(8,128)(2,1)}), bf16[16,16,512]{2,1,0:T(8,128)(2,1)S(1)}, u32[]{:S(2)}, u32[]{:S(2)}) %all-to-all-start.3) | async-done | bytes 262176 | tf_op jit(solution)/shard_map/all_to_all | solution.py:76
  95.1 1.9 collective-permute-start
  97.1 3.2 %collective-permute-done = bf16[16,512]{1,0:T(8,128)(2,1)S(1)} collective-permute-done((bf16[16,512]{1,0:T(8,128)(2,1)S(1)}, bf16[16,512]{1,0:T(8,128)(2,1)S(1)}, u32[]{:S(2)}, u32[]{:S(2)}) %collective-permute-start) | collective-permute-done | bytes 16416 | tf_op jit(solution)/shard_map/ppermute | solution.py:166
  100.3 0.8 broadcast_in_dim.295
  101.1 11.2 %all-to-all-start.4 = ((bf16[16,16,896]{2,1,0:T(8,128)(2,1)}), bf16[16,16,896]{2,1,0:T(8,128)(2,1)S(1)}, u32[]{:S(2)}, u32[]{:S(2)}) async-start(bf16[16,16,896]{2,1,0:T(8,128)(2,1)} %broadcast_in_dim.295), calls=%async_computation.4 | async-start | bytes 917504 | tf_op jit(solution)/shard_map/all_to_all | solution.py:76
  112.4 0.3 convolution_convert_fusion
  112.7 15.5 %all-to-all-done.4 = bf16[16,16,896]{2,1,0:T(8,128)(2,1)S(1)} async-done(((bf16[16,16,896]{2,1,0:T(8,128)(2,1)}), bf16[16,16,896]{2,1,0:T(8,128)(2,1)S(1)}, u32[]{:S(2)}, u32[]{:S(2)}) %all-to-all-start.4) | async-done | bytes 458784 | tf_op jit(solution)/shard_map/all_to_all | solution.py:76
  128.4 0.5 fusion.23
  129.0 0.4 convolution_convert_fusion.6
  129.4 0.4 convolution_convert_fusion.8
  129.8 0.4 copy-done.9
  130.2 0.4 convolution_convert_fusion.5
  130.6 0.4 convolution_convert_fusion.7
  131.0 0.5 fusion.47
  131.9 5.2 %all_to_all.65 = bf16[2,256,1792]{2,1,0:T(8,128)(2,1)S(1)} all-to-all(bf16[2,256,1792]{2,1,0:T(8,128)(2,1)S(1)} %pad_maximum_fusion), channel_id=1, replica_groups=mesh['xh'=2,'core'=2,'z'=8,'y'=8,'xl'=2] {'core'}, dimensions={0} | all-to-all | bytes 3670016 | tf_op jit(solution)/shard_map/all_to_all | solution.py:76
  137.1 1.5 reduce_sum.176
  138.6 6.0 %all-to-all-start.6 = ((bf16[16,16,1792]{2,1,0:T(8,128)(2,1)}), bf16[16,16,1792]{2,1,0:T(8,128)(2,1)S(1)}, u32[]{:S(2)}, u32[]{:S(2)}) async-start(bf16[16,16,1792]{2,1,0:T(8,128)(2,1)} %bitcast.78), calls=%async_computation.6 | async-start | bytes 1835008 | tf_op jit(solution)/shard_map/all_to_all | solution.py:76
  144.7 25.2 %all-to-all-done.6 = bf16[16,16,1792]{2,1,0:T(8,128)(2,1)S(1)} async-done(((bf16[16,16,1792]{2,1,0:T(8,128)(2,1)}), bf16[16,16,1792]{2,1,0:T(8,128)(2,1)S(1)}, u32[]{:S(2)}, u32[]{:S(2)}) %all-to-all-start.6) | async-done | bytes 917536 | tf_op jit(solution)/shard_map/all_to_all | solution.py:76
  170.0 0.2 fusion.94
  170.2 0.2 fusion.95
  170.4 0.2 fusion.56
  170.9 29.5 %all_to_all.66 = bf16[16,16,1664]{2,1,0:T(8,128)(2,1)S(1)} all-to-all(bf16[16,16,1664]{2,1,0:T(8,128)(2,1)S(1)} %broadcast_in_dim.315), channel_id=1, replica_groups=mesh['xh'=2,'core'=2,'z'=8,'y'=8,'xl'=2] {'xh','z'}, dimensions={0} | all-to-all | bytes 1703936 | tf_op jit(solution)/shard_map/all_to_all | solution.py:76
  200.5 2.6 all-gather
  203.1 0.4 fusion.16
  203.5 2.4 all-gather.1
  205.8 0.4 fusion.13
  206.2 0.4 fusion.1
  206.6 0.4 fusion
  207.0 19.7 %all_to_all.67 = bf16[16,16,896]{2,1,0:T(8,128)(2,1)S(1)} all-to-all(bf16[16,16,896]{2,1,0:T(8,128)(2,1)S(1)} %bitcast.82), channel_id=1, replica_groups=mesh['xh'=2,'core'=2,'z'=8,'y'=8,'xl'=2] {'y','xl'}, dimensions={0} | all-to-all | bytes 917504 | tf_op jit(solution)/shard_map/all_to_all | solution.py:76
  227.3 0.6 fusion.81
  227.9 1.9 collective-permute-start.1
  229.8 4.6 %collective-permute-done.1 = bf16[16,384]{1,0:T(8,128)(2,1)S(1)} collective-permute-done((bf16[16,384]{1,0:T(8,128)(2,1)S(1)}, bf16[16,384]{1,0:T(8,128)(2,1)S(1)}, u32[]{:S(2)}, u32[]{:S(2)}) %collective-permute-start.1) | collective-permute-done | bytes 12320 | tf_op jit(solution)/shard_map/ppermute | solution.py:229
  234.4 22.8 %all_to_all.68 = bf16[16,16,384]{2,1,0:T(8,128)(2,1)S(1)} all-to-all(bf16[16,16,384]{2,1,0:T(8,128)(2,1)S(1)} %broadcast_in_dim.317), channel_id=1, replica_groups=mesh['xh'=2,'core'=2,'z'=8,'y'=8,'xl'=2] {'xh','z'}, dimensions={0} | all-to-all | bytes 393216 | tf_op jit(solution)/shard_map/all_to_all | solution.py:76
  257.2 2.1 all_gather.32
  259.3 1.2 convolution_convert_fusion.2
  260.5 3.6 %all-to-all-start.10 = ((bf16[16,16,768]{2,1,0:T(8,128)(2,1)}), bf16[16,16,768]{2,1,0:T(8,128)(2,1)S(1)}, u32[]{:S(2)}, u32[]{:S(2)}) async-start(bf16[16,16,768]{2,1,0:T(8,128)(2,1)} %bitcast.36), calls=%async_computation.10 | async-start | bytes 786432 | tf_op jit(solution)/shard_map/all_to_all | solution.py:76
  264.2 15.7 %all-to-all-done.10 = bf16[16,16,768]{2,1,0:T(8,128)(2,1)S(1)} async-done(((bf16[16,16,768]{2,1,0:T(8,128)(2,1)}), bf16[16,16,768]{2,1,0:T(8,128)(2,1)S(1)}, u32[]{:S(2)}, u32[]{:S(2)}) %all-to-all-start.10) | async-done | bytes 393248 | tf_op jit(solution)/shard_map/all_to_all | solution.py:76
  280.3 18.1 %all_to_all.69 = bf16[16,16,896]{2,1,0:T(8,128)(2,1)S(1)} all-to-all(bf16[16,16,896]{2,1,0:T(8,128)(2,1)S(1)} %broadcast_in_dim.324), channel_id=1, replica_groups=mesh['xh'=2,'core'=2,'z'=8,'y'=8,'xl'=2] {'y','xl'}, dimensions={0} | all-to-all | bytes 917504 | tf_op jit(solution)/shard_map/all_to_all | solution.py:76
  298.4 0.5 convolution_convert_fusion.1
  299.1 2.1 all_gather.33
  301.2 0.8 fusion.19
  302.0 4.0 %all-to-all-start.12 = ((bf16[16,8,896]{2,1,0:T(8,128)(2,1)}), bf16[16,8,896]{2,1,0:T(8,128)(2,1)S(1)}, u32[]{:S(2)}, u32[]{:S(2)}) async-start(bf16[16,8,896]{2,1,0:T(8,128)(2,1)} %fusion.19), calls=%async_computation.12 | async-start | bytes 458752 | tf_op jit(solution)/shard_map/all_to_all | solution.py:76
  306.2 11.1 %all-to-all-done.12 = bf16[16,8,896]{2,1,0:T(8,128)(2,1)S(1)} async-done(((bf16[16,8,896]{2,1,0:T(8,128)(2,1)}), bf16[16,8,896]{2,1,0:T(8,128)(2,1)S(1)}, u32[]{:S(2)}, u32[]{:S(2)}) %all-to-all-start.12) | async-done | bytes 229408 | tf_op jit(solution)/shard_map/all_to_all | solution.py:76
  317.5 0.7 fusion.92
  (121 shorter events, 5.1 us)
Async XLA Ops:
  0.6 15.6 %copy-start = (bf16[768,768]{1,0:T(8,128)(2,1)S(1)}, bf16[768,768]{1,0:T(8,128)(2,1)}, u32[]{:S(2)}) copy-start(bf16[768,768]{1,0:T(8,128)(2,1)} %param.10) | copy-start | bytes 3538948
  2.1 23.1 %all-to-all-start = ((bf16[16,8,768]{2,1,0:T(8,128)(2,1)}), bf16[16,8,768]{2,1,0:T(8,128)(2,1)S(1)}, u32[]{:S(2)}, u32[]{:S(2)}) async-start(bf16[16,8,768]{2,1,0:T(8,128)(2,1)} %broadcast_in_dim.270), calls=%async_computation | async-start | bytes 393216 | tf_op jit(solution)/shard_map/all_to_all | solution.py:76
  14.6 2.1 copy-start.7
  16.6 11.4 %copy-start.1 = (bf16[768,768]{1,0:T(8,128)(2,1)S(1)}, bf16[768,768]{1,0:T(8,128)(2,1)}, u32[]{:S(2)}) copy-start(bf16[768,768]{1,0:T(8,128)(2,1)} %param.9) | copy-start | bytes 3538948
  29.7 23.8 %all-to-all-start.1 = ((bf16[16,16,896]{2,1,0:T(8,128)(2,1)}), bf16[16,16,896]{2,1,0:T(8,128)(2,1)S(1)}, u32[]{:S(2)}, u32[]{:S(2)}) async-start(bf16[16,16,896]{2,1,0:T(8,128)(2,1)} %pad_maximum_fusion.3), calls=%async_computation.1 | async-start | bytes 917504 | tf_op jit(solution)/shard_map/all_to_all | solution.py:76
  55.1 18.6 %all-to-all-start.2 = ((bf16[16,16,896]{2,1,0:T(8,128)(2,1)}), bf16[16,16,896]{2,1,0:T(8,128)(2,1)S(1)}, u32[]{:S(2)}, u32[]{:S(2)}) async-start(bf16[16,16,896]{2,1,0:T(8,128)(2,1)} %broadcast_in_dim.286), calls=%async_computation.2 | async-start | bytes 917504 | tf_op jit(solution)/shard_map/all_to_all | solution.py:76
  77.3 23.0 %copy-start.5 = (bf16[1,16,384]{2,1,0:T(8,128)(2,1)S(1)}, bf16[1,16,384]{2,1,0:T(8,128)(2,1)}, u32[]{:S(2)}) copy-start(bf16[1,16,384]{2,1,0:T(8,128)(2,1)} %param.15) | copy-start | bytes 36868
  78.1 34.2 %copy-start.8 = (bf16[384]{0:T(512)(128)(2,1)S(1)}, bf16[384]{0:T(512)(128)(2,1)}, u32[]{:S(2)}) copy-start(bf16[384]{0:T(512)(128)(2,1)} %param.14) | copy-start | bytes 2308
  78.1 34.2 %copy-start.3 = (bf16[384,1536]{1,0:T(8,128)(2,1)S(1)}, bf16[384,1536]{1,0:T(8,128)(2,1)}, u32[]{:S(2)}) copy-start(bf16[384,1536]{1,0:T(8,128)(2,1)} %param.12) | copy-start | bytes 3538948
  78.1 16.6 %all-to-all-start.3 = ((bf16[16,16,512]{2,1,0:T(8,128)(2,1)}), bf16[16,16,512]{2,1,0:T(8,128)(2,1)S(1)}, u32[]{:S(2)}, u32[]{:S(2)}) async-start(bf16[16,16,512]{2,1,0:T(8,128)(2,1)} %fusion.8), calls=%async_computation.3 | async-start | bytes 524288 | tf_op jit(solution)/shard_map/all_to_all | solution.py:76
  95.1 5.1 %collective-permute-start = (bf16[16,512]{1,0:T(8,128)(2,1)S(1)}, bf16[16,512]{1,0:T(8,128)(2,1)S(1)}, u32[]{:S(2)}, u32[]{:S(2)}) collective-permute-start(bf16[16,512]{1,0:T(8,128)(2,1)S(1)} %pad_maximum_fusion.16), channel_id=1, source_target_pairs={{0,0},{1,32},{2,64},{3,96},{4,128},{5,160},{6,192},{7,224},{8,256}... | collective-permute-start | bytes 49160 | tf_op jit(solution)/shard_map/ppermute | solution.py:166
  101.1 27.1 %all-to-all-start.4 = ((bf16[16,16,896]{2,1,0:T(8,128)(2,1)}), bf16[16,16,896]{2,1,0:T(8,128)(2,1)S(1)}, u32[]{:S(2)}, u32[]{:S(2)}) async-start(bf16[16,16,896]{2,1,0:T(8,128)(2,1)} %broadcast_in_dim.295), calls=%async_computation.4 | async-start | bytes 917504 | tf_op jit(solution)/shard_map/all_to_all | solution.py:76
  129.0 1.3 copy-start.9
  138.6 31.2 %all-to-all-start.6 = ((bf16[16,16,1792]{2,1,0:T(8,128)(2,1)}), bf16[16,16,1792]{2,1,0:T(8,128)(2,1)S(1)}, u32[]{:S(2)}, u32[]{:S(2)}) async-start(bf16[16,16,1792]{2,1,0:T(8,128)(2,1)} %bitcast.78), calls=%async_computation.6 | async-start | bytes 1835008 | tf_op jit(solution)/shard_map/all_to_all | solution.py:76
  200.4 2.7 copy-start.4
  203.1 2.8 copy-start.10
  227.9 6.5 %collective-permute-start.1 = (bf16[16,384]{1,0:T(8,128)(2,1)S(1)}, bf16[16,384]{1,0:T(8,128)(2,1)S(1)}, u32[]{:S(2)}, u32[]{:S(2)}) collective-permute-start(bf16[16,384]{1,0:T(8,128)(2,1)S(1)} %get-tuple-element.60), channel_id=1, source_target_pairs={{0,0},{32,1},{64,2},{96,3},{128,4},{160,5},{192,6},{224,7},{256,8}... | collective-permute-start | bytes 36872 | tf_op jit(solution)/shard_map/ppermute | solution.py:229
  260.5 19.3 %all-to-all-start.10 = ((bf16[16,16,768]{2,1,0:T(8,128)(2,1)}), bf16[16,16,768]{2,1,0:T(8,128)(2,1)S(1)}, u32[]{:S(2)}, u32[]{:S(2)}) async-start(bf16[16,16,768]{2,1,0:T(8,128)(2,1)} %bitcast.36), calls=%async_computation.10 | async-start | bytes 786432 | tf_op jit(solution)/shard_map/all_to_all | solution.py:76
  264.1 34.3 %copy-start.2 = (bf16[768,768]{1,0:T(8,128)(2,1)S(1)}, bf16[768,768]{1,0:T(8,128)(2,1)}, u32[]{:S(2)}) copy-start(bf16[768,768]{1,0:T(8,128)(2,1)} %param.9) | copy-start | bytes 3538948
  299.1 18.4 %copy-start.6 = (bf16[1,8,768]{2,1,0:T(8,128)(2,1)S(1)}, bf16[1,8,768]{2,1,0:T(8,128)(2,1)}, u32[]{:S(2)}) copy-start(bf16[1,8,768]{2,1,0:T(8,128)(2,1)} %param.8) | copy-start | bytes 36868
  302.0 15.2 %all-to-all-start.12 = ((bf16[16,8,896]{2,1,0:T(8,128)(2,1)}), bf16[16,8,896]{2,1,0:T(8,128)(2,1)S(1)}, u32[]{:S(2)}, u32[]{:S(2)}) async-start(bf16[16,8,896]{2,1,0:T(8,128)(2,1)} %fusion.19), calls=%async_computation.12 | async-start | bytes 458752 | tf_op jit(solution)/shard_map/all_to_all | solution.py:76

commit v6 on v5

--- a/solution.py
+++ b/solution.py
@@ -170,22 +170,23 @@
     ones = jnp.ones((1, 384), F32)
     cols = pack([row_dot(centred * centred, ones), row_dot(centred, ones)], 64 * core)
     centred = (centred * gain_b).astype(BF)
-    message = jnp.stack(
-        [
+    halves = [
+        (
+            jnp.concatenate([dot(centred, up_second[:, at : at + 768]).astype(BF), cols], axis=1),
             jnp.concatenate(
                 [
-                    dot(centred, up_second[:, at : at + 768]).astype(BF),
                     contract_cols(cot_all, down_second[at : at + 768]).astype(BF),
-                    cols,
                     jnp.tile(tile_rows(u_b[at : at + 768], 16), (16, 1)),
                 ],
                 axis=1,
-            )
-            for at in (0, 768)
-        ]
-    )
-    got = exchange(message, "core")
-    part = jnp.sum(got.astype(F32), axis=0).astype(BF)
+            ),
+        )
+        for at in (0, 768)
+    ]
+    part, part_d = (pair_sum(core, first, second) for first, second in zip(*halves))
+    part = jnp.concatenate(
+        [part[:, :768], part_d[:, :768], part[:, 768:], part_d[:, 768:]], axis=1
+    )
     sums = jnp.sum(exchange(part.reshape(16, 16, 1792), ROW).astype(F32), axis=0)
     gain_up_b = sums[:6, 1664:].reshape(1, 768)
     off = unpack_pair(sums[:, 1536:1664], 1) / D

time: 319 us -> 325 us (1.019)
  matrix products: 9.65 us -> 13 us
    all_to_all x5 -> x4, blocking collectives: 95.4 us -> 90.2 us  [exchange(): return lax.all_to_all(blocks, axis, 0, 0)]
    all_gather x6 -> x8, blocking collectives: 13.4 us -> 18.4 us  [both_cores(): return lax.all_gather(values, 'core', axis=0, tiled=False)]
    dot_general x8, matrix products: 4.36 us -> 7.77 us  [dot(): return jnp.dot(left, right, preferred_element_type=F32)]
where the time goes in v6:
time: 325 us; the launch traced here: 323 us
  waiting for transfers between devices  126 us (39%)
  blocking collectives  109 us (34%)
  starting transfers between devices  56.6 us (17%)
  matrix products  13 us (4%)
  other arithmetic  10.6 us (3%)
  local copies, waits for them, and re-layouts  7.49 us (2%)
    all_to_all x8, waiting for transfers between devices, exchange(): return lax.all_to_all(blocks, axis, 0, 0)  118 us
    all_to_all x4, blocking collectives, exchange(): return lax.all_to_all(blocks, axis, 0, 0)  90.2 us
    all_to_all x8, starting transfers between devices, exchange(): return lax.all_to_all(blocks, axis, 0, 0)  52.8 us
    all_gather x8, blocking collectives, both_cores(): return lax.all_gather(values, 'core', axis=0, tiled=False)  18.4 us
    dot_general x8, matrix products, dot(): return jnp.dot(left, right, preferred_element_type=F32)  7.77 us
  transfers between devices with their start and end apart: 10, of which 10 were waited for; matrix products, arithmetic and copies ran while one was open for 1% of the time, Pallas kernels for 0%

profile of v6, /device:TPU:64, one launch (start us, length us, event | category | flops | bytes accessed | tf_op | source)
XLA Modules:
  0.0 323.2 jit_solution(15301201525167498361)
XLA Ops:
  0.6 1.5 broadcast_in_dim.270
  2.1 12.4 %all-to-all-start = ((bf16[16,8,768]{2,1,0:T(8,128)(2,1)}), bf16[16,8,768]{2,1,0:T(8,128)(2,1)S(1)}, u32[]{:S(2)}, u32[]{:S(2)}) async-start(bf16[16,8,768]{2,1,0:T(8,128)(2,1)} %broadcast_in_dim.270), calls=%async_computation | async-start | bytes 393216 | tf_op jit(solution)/shard_map/all_to_all | solution.py:76
  14.6 1.6 fusion.121
  16.2 0.4 fusion.119
  16.9 8.4 %all-to-all-done = bf16[16,8,768]{2,1,0:T(8,128)(2,1)S(1)} async-done(((bf16[16,8,768]{2,1,0:T(8,128)(2,1)}), bf16[16,8,768]{2,1,0:T(8,128)(2,1)S(1)}, u32[]{:S(2)}, u32[]{:S(2)}) %all-to-all-start) | async-done | bytes 196640 | tf_op jit(solution)/shard_map/all_to_all | solution.py:76
  25.3 2.1 all_gather.34
  28.1 0.5 convolution_convert_fusion.4
  28.9 0.8 pad_maximum_fusion.5
  29.7 7.2 %all-to-all-start.1 = ((bf16[16,16,896]{2,1,0:T(8,128)(2,1)}), bf16[16,16,896]{2,1,0:T(8,128)(2,1)S(1)}, u32[]{:S(2)}, u32[]{:S(2)}) async-start(bf16[16,16,896]{2,1,0:T(8,128)(2,1)} %pad_maximum_fusion.5), calls=%async_computation.1 | async-start | bytes 917504 | tf_op jit(solution)/shard_map/all_to_all | solution.py:76
  37.0 16.5 %all-to-all-done.1 = bf16[16,16,896]{2,1,0:T(8,128)(2,1)S(1)} async-done(((bf16[16,16,896]{2,1,0:T(8,128)(2,1)}), bf16[16,16,896]{2,1,0:T(8,128)(2,1)S(1)}, u32[]{:S(2)}, u32[]{:S(2)}) %all-to-all-start.1) | async-done | bytes 458784 | tf_op jit(solution)/shard_map/all_to_all | solution.py:76
  54.4 0.8 broadcast_in_dim.286
  55.2 3.6 %all-to-all-start.2 = ((bf16[16,16,896]{2,1,0:T(8,128)(2,1)}), bf16[16,16,896]{2,1,0:T(8,128)(2,1)S(1)}, u32[]{:S(2)}, u32[]{:S(2)}) async-start(bf16[16,16,896]{2,1,0:T(8,128)(2,1)} %broadcast_in_dim.286), calls=%async_computation.2 | async-start | bytes 917504 | tf_op jit(solution)/shard_map/all_to_all | solution.py:76
  58.9 14.9 %all-to-all-done.2 = bf16[16,16,896]{2,1,0:T(8,128)(2,1)S(1)} async-done(((bf16[16,16,896]{2,1,0:T(8,128)(2,1)}), bf16[16,16,896]{2,1,0:T(8,128)(2,1)S(1)}, u32[]{:S(2)}, u32[]{:S(2)}) %all-to-all-start.2) | async-done | bytes 458784 | tf_op jit(solution)/shard_map/all_to_all | solution.py:76
  73.7 0.5 convolution_convert_fusion.3
  74.2 0.3 copy-done.4
  74.8 0.7 copy-done.5
  75.5 0.5 fusion.43
  76.1 2.2 all_gather.35
  78.4 0.8 fusion.6
  79.1 4.8 %all-to-all-start.3 = ((bf16[16,16,512]{2,1,0:T(8,128)(2,1)}), bf16[16,16,512]{2,1,0:T(8,128)(2,1)S(1)}, u32[]{:S(2)}, u32[]{:S(2)}) async-start(bf16[16,16,512]{2,1,0:T(8,128)(2,1)} %fusion.6), calls=%async_computation.3 | async-start | bytes 524288 | tf_op jit(solution)/shard_map/all_to_all | solution.py:76
  83.9 11.9 %all-to-all-done.3 = bf16[16,16,512]{2,1,0:T(8,128)(2,1)S(1)} async-done(((bf16[16,16,512]{2,1,0:T(8,128)(2,1)}), bf16[16,16,512]{2,1,0:T(8,128)(2,1)S(1)}, u32[]{:S(2)}, u32[]{:S(2)}) %all-to-all-start.3) | async-done | bytes 262176 | tf_op jit(solution)/shard_map/all_to_all | solution.py:76
  96.1 0.7 fusion.90
  96.9 1.9 collective-permute-start
  98.8 3.2 collective-permute-done
  102.0 0.8 broadcast_in_dim.295
  102.8 11.2 %all-to-all-start.4 = ((bf16[16,16,896]{2,1,0:T(8,128)(2,1)}), bf16[16,16,896]{2,1,0:T(8,128)(2,1)S(1)}, u32[]{:S(2)}, u32[]{:S(2)}) async-start(bf16[16,16,896]{2,1,0:T(8,128)(2,1)} %broadcast_in_dim.295), calls=%async_computation.4 | async-start | bytes 917504 | tf_op jit(solution)/shard_map/all_to_all | solution.py:76
  114.1 1.5 convolution_convert_fusion
  115.7 14.2 %all-to-all-done.4 = bf16[16,16,896]{2,1,0:T(8,128)(2,1)S(1)} async-done(((bf16[16,16,896]{2,1,0:T(8,128)(2,1)}), bf16[16,16,896]{2,1,0:T(8,128)(2,1)S(1)}, u32[]{:S(2)}, u32[]{:S(2)}) %all-to-all-start.4) | async-done | bytes 458784 | tf_op jit(solution)/shard_map/all_to_all | solution.py:76
  130.2 1.5 convolution_convert_fusion.8
  131.7 1.5 convolution_convert_fusion.7
  133.1 0.5 fusion.25
  133.7 0.5 fusion.49
  134.3 2.5 all_gather.36
  137.0 1.2 copy-done.11
  138.2 0.4 convolution_convert_fusion.5
  138.6 0.4 convolution_convert_fusion.6
  139.2 2.5 all_gather.37
  141.9 0.7 slice-done
  142.6 1.0 pad_maximum_fusion
  143.6 6.0 %all-to-all-start.5 = ((bf16[16,16,1792]{2,1,0:T(8,128)(2,1)}), bf16[16,16,1792]{2,1,0:T(8,128)(2,1)S(1)}, u32[]{:S(2)}, u32[]{:S(2)}) async-start(bf16[16,16,1792]{2,1,0:T(8,128)(2,1)} %bitcast.29), calls=%async_computation.5 | async-start | bytes 1835008 | tf_op jit(solution)/shard_map/all_to_all | solution.py:76
  149.7 25.2 %all-to-all-done.5 = bf16[16,16,1792]{2,1,0:T(8,128)(2,1)S(1)} async-done(((bf16[16,16,1792]{2,1,0:T(8,128)(2,1)}), bf16[16,16,1792]{2,1,0:T(8,128)(2,1)S(1)}, u32[]{:S(2)}, u32[]{:S(2)}) %all-to-all-start.5) | async-done | bytes 917536 | tf_op jit(solution)/shard_map/all_to_all | solution.py:76
  175.9 29.5 %all_to_all.60 = bf16[16,16,1664]{2,1,0:T(8,128)(2,1)S(1)} all-to-all(bf16[16,16,1664]{2,1,0:T(8,128)(2,1)S(1)} %broadcast_in_dim.315), channel_id=1, replica_groups=mesh['xh'=2,'core'=2,'z'=8,'y'=8,'xl'=2] {'xh','z'}, dimensions={0} | all-to-all | bytes 1703936 | tf_op jit(solution)/shard_map/all_to_all | solution.py:76
  205.5 2.6 all-gather
  208.1 0.4 fusion.14
  208.5 0.4 fusion
  208.9 2.4 all-gather.1
  211.3 0.4 fusion.9
  211.6 0.4 fusion.1
  212.1 19.7 %all_to_all.61 = bf16[16,16,896]{2,1,0:T(8,128)(2,1)S(1)} all-to-all(bf16[16,16,896]{2,1,0:T(8,128)(2,1)S(1)} %bitcast.94), channel_id=1, replica_groups=mesh['xh'=2,'core'=2,'z'=8,'y'=8,'xl'=2] {'y','xl'}, dimensions={0} | all-to-all | bytes 917504 | tf_op jit(solution)/shard_map/all_to_all | solution.py:76
  232.3 0.6 fusion.83
  232.9 1.9 collective-permute-start.1
  234.8 4.6 %collective-permute-done.1 = bf16[16,384]{1,0:T(8,128)(2,1)S(1)} collective-permute-done((bf16[16,384]{1,0:T(8,128)(2,1)S(1)}, bf16[16,384]{1,0:T(8,128)(2,1)S(1)}, u32[]{:S(2)}, u32[]{:S(2)}) %collective-permute-start.1) | collective-permute-done | bytes 12320 | tf_op jit(solution)/shard_map/ppermute | solution.py:230
  239.4 22.8 %all_to_all.62 = bf16[16,16,384]{2,1,0:T(8,128)(2,1)S(1)} all-to-all(bf16[16,16,384]{2,1,0:T(8,128)(2,1)S(1)} %broadcast_in_dim.317), channel_id=1, replica_groups=mesh['xh'=2,'core'=2,'z'=8,'y'=8,'xl'=2] {'xh','z'}, dimensions={0} | all-to-all | bytes 393216 | tf_op jit(solution)/shard_map/all_to_all | solution.py:76
  262.2 2.1 all_gather.42
  264.3 1.2 convolution_convert_fusion.2
  265.6 3.6 %all-to-all-start.9 = ((bf16[16,16,768]{2,1,0:T(8,128)(2,1)}), bf16[16,16,768]{2,1,0:T(8,128)(2,1)S(1)}, u32[]{:S(2)}, u32[]{:S(2)}) async-start(bf16[16,16,768]{2,1,0:T(8,128)(2,1)} %bitcast.128), calls=%async_computation.9 | async-start | bytes 786432 | tf_op jit(solution)/shard_map/all_to_all | solution.py:76
  269.2 15.7 %all-to-all-done.9 = bf16[16,16,768]{2,1,0:T(8,128)(2,1)S(1)} async-done(((bf16[16,16,768]{2,1,0:T(8,128)(2,1)}), bf16[16,16,768]{2,1,0:T(8,128)(2,1)S(1)}, u32[]{:S(2)}, u32[]{:S(2)}) %all-to-all-start.9) | async-done | bytes 393248 | tf_op jit(solution)/shard_map/all_to_all | solution.py:76
  285.3 18.1 %all_to_all.63 = bf16[16,16,896]{2,1,0:T(8,128)(2,1)S(1)} all-to-all(bf16[16,16,896]{2,1,0:T(8,128)(2,1)S(1)} %broadcast_in_dim.324), channel_id=1, replica_groups=mesh['xh'=2,'core'=2,'z'=8,'y'=8,'xl'=2] {'y','xl'}, dimensions={0} | all-to-all | bytes 917504 | tf_op jit(solution)/shard_map/all_to_all | solution.py:76
  303.5 0.5 convolution_convert_fusion.1
  304.1 2.1 all_gather.43
  306.2 0.8 fusion.21
  307.0 4.0 %all-to-all-start.11 = ((bf16[16,8,896]{2,1,0:T(8,128)(2,1)}), bf16[16,8,896]{2,1,0:T(8,128)(2,1)S(1)}, u32[]{:S(2)}, u32[]{:S(2)}) async-start(bf16[16,8,896]{2,1,0:T(8,128)(2,1)} %fusion.21), calls=%async_computation.11 | async-start | bytes 458752 | tf_op jit(solution)/shard_map/all_to_all | solution.py:76
  311.2 11.1 %all-to-all-done.11 = bf16[16,8,896]{2,1,0:T(8,128)(2,1)S(1)} async-done(((bf16[16,8,896]{2,1,0:T(8,128)(2,1)}), bf16[16,8,896]{2,1,0:T(8,128)(2,1)S(1)}, u32[]{:S(2)}, u32[]{:S(2)}) %all-to-all-start.11) | async-done | bytes 229408 | tf_op jit(solution)/shard_map/all_to_all | solution.py:76
  322.5 0.7 fusion.94
  (134 shorter events, 6.7 us)
Async XLA Ops:
  0.6 15.6 %copy-start = (bf16[768,768]{1,0:T(8,128)(2,1)S(1)}, bf16[768,768]{1,0:T(8,128)(2,1)}, u32[]{:S(2)}) copy-start(bf16[768,768]{1,0:T(8,128)(2,1)} %param.10) | copy-start | bytes 3538948
  2.1 23.1 %all-to-all-start = ((bf16[16,8,768]{2,1,0:T(8,128)(2,1)}), bf16[16,8,768]{2,1,0:T(8,128)(2,1)S(1)}, u32[]{:S(2)}, u32[]{:S(2)}) async-start(bf16[16,8,768]{2,1,0:T(8,128)(2,1)} %broadcast_in_dim.270), calls=%async_computation | async-start | bytes 393216 | tf_op jit(solution)/shard_map/all_to_all | solution.py:76
  14.6 2.1 copy-start.9
  16.6 11.4 %copy-start.2 = (bf16[768,768]{1,0:T(8,128)(2,1)S(1)}, bf16[768,768]{1,0:T(8,128)(2,1)}, u32[]{:S(2)}) copy-start(bf16[768,768]{1,0:T(8,128)(2,1)} %param.9) | copy-start | bytes 3538948
  27.9 0.9 copy-start.6
  29.7 23.8 %all-to-all-start.1 = ((bf16[16,16,896]{2,1,0:T(8,128)(2,1)}), bf16[16,16,896]{2,1,0:T(8,128)(2,1)S(1)}, u32[]{:S(2)}, u32[]{:S(2)}) async-start(bf16[16,16,896]{2,1,0:T(8,128)(2,1)} %pad_maximum_fusion.5), calls=%async_computation.1 | async-start | bytes 917504 | tf_op jit(solution)/shard_map/all_to_all | solution.py:76
  55.2 18.6 %all-to-all-start.2 = ((bf16[16,16,896]{2,1,0:T(8,128)(2,1)}), bf16[16,16,896]{2,1,0:T(8,128)(2,1)S(1)}, u32[]{:S(2)}, u32[]{:S(2)}) async-start(bf16[16,16,896]{2,1,0:T(8,128)(2,1)} %broadcast_in_dim.286), calls=%async_computation.2 | async-start | bytes 917504 | tf_op jit(solution)/shard_map/all_to_all | solution.py:76
  73.7 0.8 copy-start.4
  74.5 1.0 copy-start.5
  78.3 23.7 %copy-start.7 = (bf16[1,16,384]{2,1,0:T(8,128)(2,1)S(1)}, bf16[1,16,384]{2,1,0:T(8,128)(2,1)}, u32[]{:S(2)}) copy-start(bf16[1,16,384]{2,1,0:T(8,128)(2,1)} %param.15) | copy-start | bytes 36868
  79.1 34.9 %copy-start.10 = (bf16[384]{0:T(512)(128)(2,1)S(1)}, bf16[384]{0:T(512)(128)(2,1)}, u32[]{:S(2)}) copy-start(bf16[384]{0:T(512)(128)(2,1)} %param.14) | copy-start | bytes 2308
  79.1 16.6 %all-to-all-start.3 = ((bf16[16,16,512]{2,1,0:T(8,128)(2,1)}), bf16[16,16,512]{2,1,0:T(8,128)(2,1)S(1)}, u32[]{:S(2)}, u32[]{:S(2)}) async-start(bf16[16,16,512]{2,1,0:T(8,128)(2,1)} %fusion.6), calls=%async_computation.3 | async-start | bytes 524288 | tf_op jit(solution)/shard_map/all_to_all | solution.py:76
  96.9 5.1 %collective-permute-start = (bf16[16,512]{1,0:T(8,128)(2,1)S(1)}, bf16[16,512]{1,0:T(8,128)(2,1)S(1)}, u32[]{:S(2)}, u32[]{:S(2)}) collective-permute-start(bf16[16,512]{1,0:T(8,128)(2,1)S(1)} %pad_maximum_fusion.18), channel_id=1, source_target_pairs={{0,0},{1,32},{2,64},{3,96},{4,128},{5,160},{6,192},{7,224},{8,256}... | collective-permute-start | bytes 49160 | tf_op jit(solution)/shard_map/ppermute | solution.py:166
  102.8 27.1 %all-to-all-start.4 = ((bf16[16,16,896]{2,1,0:T(8,128)(2,1)}), bf16[16,16,896]{2,1,0:T(8,128)(2,1)S(1)}, u32[]{:S(2)}, u32[]{:S(2)}) async-start(bf16[16,16,896]{2,1,0:T(8,128)(2,1)} %broadcast_in_dim.295), calls=%async_computation.4 | async-start | bytes 917504 | tf_op jit(solution)/shard_map/all_to_all | solution.py:76
  136.8 1.4 copy-start.11
  137.0 2.0 copy-start.1
  141.6 1.0 slice-start
  141.6 1.0 slice-start.1
  143.6 31.2 %all-to-all-start.5 = ((bf16[16,16,1792]{2,1,0:T(8,128)(2,1)}), bf16[16,16,1792]{2,1,0:T(8,128)(2,1)S(1)}, u32[]{:S(2)}, u32[]{:S(2)}) async-start(bf16[16,16,1792]{2,1,0:T(8,128)(2,1)} %bitcast.29), calls=%async_computation.5 | async-start | bytes 1835008 | tf_op jit(solution)/shard_map/all_to_all | solution.py:76
  205.4 2.6 copy-start.3
  208.5 2.8 copy-start.12
  232.9 6.5 %collective-permute-start.1 = (bf16[16,384]{1,0:T(8,128)(2,1)S(1)}, bf16[16,384]{1,0:T(8,128)(2,1)S(1)}, u32[]{:S(2)}, u32[]{:S(2)}) collective-permute-start(bf16[16,384]{1,0:T(8,128)(2,1)S(1)} %get-tuple-element.58), channel_id=1, source_target_pairs={{0,0},{32,1},{64,2},{96,3},{128,4},{160,5},{192,6},{224,7},{256,8}... | collective-permute-start | bytes 36872 | tf_op jit(solution)/shard_map/ppermute | solution.py:230
  265.6 19.3 %all-to-all-start.9 = ((bf16[16,16,768]{2,1,0:T(8,128)(2,1)}), bf16[16,16,768]{2,1,0:T(8,128)(2,1)S(1)}, u32[]{:S(2)}, u32[]{:S(2)}) async-start(bf16[16,16,768]{2,1,0:T(8,128)(2,1)} %bitcast.128), calls=%async_computation.9 | async-start | bytes 786432 | tf_op jit(solution)/shard_map/all_to_all | solution.py:76
  304.1 18.4 %copy-start.8 = (bf16[1,8,768]{2,1,0:T(8,128)(2,1)S(1)}, bf16[1,8,768]{2,1,0:T(8,128)(2,1)}, u32[]{:S(2)}) copy-start(bf16[1,8,768]{2,1,0:T(8,128)(2,1)} %param.8) | copy-start | bytes 36868
  307.0 15.3 %all-to-all-start.11 = ((bf16[16,8,896]{2,1,0:T(8,128)(2,1)}), bf16[16,8,896]{2,1,0:T(8,128)(2,1)S(1)}, u32[]{:S(2)}, u32[]{:S(2)}) async-start(bf16[16,8,896]{2,1,0:T(8,128)(2,1)} %fusion.21), calls=%async_computation.11 | async-start | bytes 458752 | tf_op jit(solution)/shard_map/all_to_all | solution.py:76
